TPU v7x, 32 devices: a whole 2x2x4 slice. The times are simulated.
32 devices in a mesh: band: 4 (over y, x), sector: 8 (over z, core).
Axes of the slice: x: 2, y: 2, z: 4, core: 2. Of those that a mesh axis runs over, the one named last changes fastest.
Arguments:
- grid_cells: bfloat16 [2048, 128, 128], P(('band', 'sector')), may hold values from -6 to 6
- remap_weight: bfloat16 [2048, 2, 128, 128], P(('band', 'sector')), may hold values from -0.15625 to 0.15625
- remap_dest: int32 [2048, 2], P(('band', 'sector')), may hold values from 0 to 31, all different within a row; in each aligned block of 64 rows (0 to 63, 64 to 127, ...) at most 8 rows name the same one
- remap_tile: int32 [2048, 2], P(('band', 'sector')), may hold values from 0 to 11
- w_embed: bfloat16 [128, 1024], replicated, may hold values from -0.5 to 0.5
- norm_gain: float32 [1024], replicated, may hold values from 0.25 to 1.75
- w_query: bfloat16 [1024, 1024], replicated
- w_key: bfloat16 [1024, 1024], replicated
- w_value: bfloat16 [1024, 1024], replicated, may hold values from -0.1875 to 0.1875
- w_out: bfloat16 [1024, 1024], replicated, may hold values from -0.1875 to 0.1875
- neighbours: int32 [8, 48, 9], P('band', 'sector'), may hold values from 0 to 383, as said below
Outputs:
- layer_out: bfloat16 [8, 48, 128, 1024], P('band', 'sector')
Inputs may be any that keep to these rules, and one draw needn't show every extreme that they name: `remap_dest`: within the row-blocks of one device, no device number is named more than 8 times; some number is named exactly 8 times. `neighbours`: entry 0 of a tile is the tile itself; every entry lies at most one tile row and one tile column away, columns counted around the sphere, rows never past the first or last; entries may repeat.
All inputs are finite; a program needn't handle non-finite values.
Results may differ from a plain program's by a relative error of at most 0.0064.
Values may be sent and summed in bfloat16 or wider, within the bound.
No kernel may reach another device: no remote copies, remote signals or barrier semaphores. Data moves between devices by JAX's collectives and lax.ppermute only.
A program may use at most 256 MiB of HBM per device.

v0:
```python
import math

import jax
import jax.numpy as jnp
from jax import lax
from jax.sharding import PartitionSpec as P

HEADS = 16
HD = 64


def padded(block, sides, width, periodic):
    for axis, dim in sides:
        count = lax.axis_size(axis)
        forward = [(i, i + 1) for i in range(count - 1)]
        if periodic:
            forward.append((count - 1, 0))
        backward = [(target, source) for source, target in forward]
        low = lax.ppermute(
            lax.slice_in_dim(block, block.shape[dim] - width, None, axis=dim), axis, forward
        )
        high = lax.ppermute(lax.slice_in_dim(block, 0, width, axis=dim), axis, backward)
        block = jnp.concatenate([low, block, high], axis=dim)
    return block


def tile_angles(rows, cols, nrows, ncols, tile):
    place = jnp.arange(tile)
    across = (place // 16).astype(jnp.float32)
    along = (place % 16).astype(jnp.float32)
    theta = math.pi * (rows[..., None].astype(jnp.float32) + (across + 0.5) * 16.0 / tile) / nrows
    phi = 2.0 * math.pi * (cols[..., None].astype(jnp.float32) + (along + 0.5) / 16.0) / ncols
    return (theta, phi)


def project_heads(weight, tiles):
    full = jnp.einsum("wf,rctw->frct", weight, tiles, preferred_element_type=jnp.float32)
    return full.reshape((HEADS, HD) + full.shape[1:])


def rotate_heads(values, theta, phi):
    quarter = values.shape[1] // 4
    freq = jnp.arange(1, quarter + 1).astype(jnp.float32).reshape((quarter, 1, 1, 1))
    lat_angle = theta[None] * freq
    lon_angle = phi[None] * freq

    def turn(lower, upper, angle):
        cosine = jnp.cos(angle)
        sine = jnp.sin(angle)
        return [lower * cosine - upper * sine, lower * sine + upper * cosine]

    pieces = turn(values[:, :quarter], values[:, quarter : 2 * quarter], lat_angle)
    pieces = pieces + turn(
        values[:, 2 * quarter : 3 * quarter], values[:, 3 * quarter :], lon_angle
    )
    return jnp.concatenate(pieces, axis=1)


def keys_and_values(tiles, theta, phi, w_key, w_value):
    keys = rotate_heads(project_heads(w_key, tiles), theta, phi).astype(jnp.bfloat16)
    values = project_heads(w_value, tiles).astype(jnp.bfloat16)
    return jnp.stack([keys, values], axis=0)


def body(
    grid_cells,
    remap_weight,
    remap_dest,
    remap_tile,
    w_embed,
    norm_gain,
    w_query,
    w_key,
    w_value,
    w_out,
    neighbours,
):
    nband = lax.axis_size("band")
    nsect = lax.axis_size("sector")
    ndev = nband * nsect
    blocks, top, rowcells, tile = remap_weight.shape
    chan = grid_cells.shape[2]
    width = w_embed.shape[1]
    trows, tcols = (neighbours.shape[0], neighbours.shape[1])
    cap = max(2, 2 * blocks * top // ndev)
    items = blocks * top
    parts = jnp.einsum(
        "rkct,rcf->rktf", remap_weight, grid_cells, preferred_element_type=jnp.float32
    )
    parts = parts.astype(jnp.bfloat16).reshape(items, tile, chan)
    dest = remap_dest.reshape(-1)
    local = remap_tile.reshape(-1)
    order = jnp.arange(items)
    earlier = (dest[:, None] == dest[None, :]) & (order[None, :] < order[:, None])
    rank = jnp.sum(earlier.astype(jnp.int32), axis=1)
    slot = dest * cap + rank
    send_parts = jnp.zeros((ndev * cap, tile, chan), jnp.bfloat16).at[slot].set(parts)
    send_ids = jnp.full((ndev * cap,), -1, jnp.int32).at[slot].set(local)
    got_parts, got_ids = (
        lax.all_to_all(send_parts, ("band", "sector"), split_axis=0, concat_axis=0, tiled=True),
        lax.all_to_all(send_ids, ("band", "sector"), split_axis=0, concat_axis=0, tiled=True),
    )
    owned = trows * tcols
    select = (got_ids[None, :] == jnp.arange(owned)[:, None]).astype(jnp.bfloat16)
    remapped = jnp.einsum(
        "ls,stc->ltc", select, got_parts, preferred_element_type=jnp.float32
    ).astype(jnp.bfloat16)
    embedded = jnp.dot(remapped.reshape(-1, chan), w_embed, preferred_element_type=jnp.float32)
    meansq = jnp.mean(embedded * embedded, axis=-1, keepdims=True)
    normed = (embedded * lax.rsqrt(meansq + 1e-05) * norm_gain).astype(jnp.bfloat16)
    band_at = lax.axis_index("band")
    sect_at = lax.axis_index("sector")
    nrows = trows * nband
    ncols = tcols * nsect
    own_rows = band_at * trows + jnp.arange(trows)
    own_cols = sect_at * tcols + jnp.arange(tcols)
    own_theta, own_phi = tile_angles(
        own_rows[:, None] + 0 * own_cols[None, :],
        0 * own_rows[:, None] + own_cols[None, :],
        nrows,
        ncols,
        tile,
    )
    normed_tiles = normed.reshape(trows, tcols, tile, width)
    queries = rotate_heads(project_heads(w_query, normed_tiles), own_theta, own_phi).astype(
        jnp.bfloat16
    )
    queries = queries.reshape(HEADS, HD, owned, tile)
    wider = padded(normed_tiles, (("band", 0),), 1, False)
    wider = padded(wider, (("sector", 1),), 1, True)
    ext_rows = band_at * trows - 1 + jnp.arange(trows + 2)
    ext_cols = jnp.mod(sect_at * tcols - 1 + jnp.arange(tcols + 2), ncols)
    ext_theta, ext_phi = tile_angles(
        ext_rows[:, None] + 0 * ext_cols[None, :],
        0 * ext_rows[:, None] + ext_cols[None, :],
        nrows,
        ncols,
        tile,
    )
    gathered = keys_and_values(wider, ext_theta, ext_phi, w_key, w_value)
    ext_flat = gathered.reshape(2, HEADS, HD, (trows + 2) * (tcols + 2), tile)
    grow = neighbours // ncols
    gcol = neighbours % ncols
    local_row = grow - band_at * trows + 1
    local_col = jnp.mod(gcol - sect_at * tcols + 1, ncols)
    index = (local_row * (tcols + 2) + local_col).reshape(owned, 9)
    group = 4
    ngroups = owned // group
    index_groups = index.reshape(ngroups, group * 9)

    def attend(inputs):
        which, listed = inputs
        query_heads = lax.dynamic_slice_in_dim(queries, which * group, group, 2)
        chosen = jnp.take(ext_flat, listed, axis=3).reshape(2, HEADS, HD, group, 9, tile)
        scores = jnp.einsum(
            "hdbq,hdbjk->hbqjk", query_heads, chosen[0], preferred_element_type=jnp.float32
        ) / math.sqrt(HD)
        probs = jax.nn.softmax(scores, axis=(-2, -1)).astype(jnp.bfloat16)
        mixed = jnp.einsum(
            "hbqjk,hdbjk->hdbq", probs, chosen[1], preferred_element_type=jnp.float32
        )
        return mixed.astype(jnp.bfloat16)

    attended = lax.map(attend, (jnp.arange(ngroups), index_groups))
    result = jnp.einsum(
        "nhdgq,hde->ngqe",
        attended,
        w_out.reshape(HEADS, HD, width),
        preferred_element_type=jnp.float32,
    )
    result = result.reshape(-1, width) + embedded
    return result.astype(jnp.bfloat16).reshape(trows, tcols, tile, width)


def solution(mesh):
    return jax.shard_map(
        body,
        mesh=mesh,
        in_specs=(
            P(("band", "sector"), None, None),
            P(("band", "sector"), None, None, None),
            P(("band", "sector"), None),
            P(("band", "sector"), None),
            P(),
            P(),
            P(),
            P(),
            P(),
            P(),
            P("band", "sector", None),
        ),
        out_specs=P("band", "sector", None, None),
        check_vma=False,
    )
```

profile of v0, /device:TPU:4, one launch (start us, length us, event | category | flops | bytes accessed | tf_op | source)
XLA Modules:
  0.0 766.3 jit_solution(12540007953388923070)
XLA Ops:
  4.8 6.1 all-to-all-start
  10.9 6.1 convolution_convert_fusion
  17.0 5.4 broadcast_in_dim.18
  22.4 19.3 %scatter_fusion = bf16[256,128,128]{2,1,0:T(8,128)(2,1)} fusion(bf16[256,128,128]{2,1,0:T(8,128)(2,1)} %broadcast_in_dim.18, s32[128]{0:T(128)S(1)} %fusion.35, bf16[128,128,128]{2,1,0:T(8,128)(2,1)} %bitcast.142), kind=kCustom, calls=%fused_computation.2 | custom fusion | bytes 12583424 | tf_op jit(solution)/shard_map/scatter | solution.py:97
  41.6 5.9 all-to-all-start.1
  49.0 182.3 %all-to-all-done.1 = bf16[256,128,128]{2,1,0:T(8,128)(2,1)} async-done(((bf16[256,128,128]{2,1,0:T(8,128)(2,1)}), bf16[256,128,128]{2,1,0:T(8,128)(2,1)}, u32[]{:S(2)}, u32[]{:S(2)}) %all-to-all-start.1) | async-done | bytes 8388640 | tf_op jit(solution)/shard_map/all_to_all | solution.py:100
  231.3 7.9 %fusion.19 = bf16[12,128,128]{2,0,1:T(8,128)(2,1)S(1)} fusion(bf16[256,128,128]{2,1,0:T(8,128)(2,1)} %all-to-all-done.1, s32[256]{0:T(256)S(1)} %eq.42), kind=kOutput, calls=%fused_computation.52 | convolution fusion | flops 100862976 | bytes 8782848 | tf_op jit(solution)/shard_map/ls,stc->ltc/dot_general | solution.py:105
  245.8 15.8 %collective-permute-start = (bf16[1,6,128,1024]{3,2,1,0:T(8,128)(2,1)S(1)}, bf16[1,6,128,1024]{3,2,1,0:T(8,128)(2,1)S(1)}, u32[]{:S(2)}, u32[]{:S(2)}) collective-permute-start(bf16[1,6,128,1024]{3,2,1,0:T(8,128)(2,1)S(1)} %bitcast.149), channel_id=1, source_target_pairs={{0,8},{8,16},{16,24},{1,9},{9,17},{17,25},{2,10},{10,18},{18,26},{... | collective-permute-start | bytes 4718600 | tf_op jit(solution)/shard_map/ppermute | solution.py:19
  264.5 17.4 %collective-permute-done.1 = bf16[1,6,128,1024]{3,2,1,0:T(8,128)(2,1)S(1)} collective-permute-done((bf16[1,6,128,1024]{3,2,1,0:T(8,128)(2,1)S(1)}, bf16[1,6,128,1024]{3,2,1,0:T(8,128)(2,1)S(1)}, u32[]{:S(2)}, u32[]{:S(2)}) %collective-permute-start.1) | collective-permute-done | bytes 1572896 | tf_op jit(solution)/shard_map/ppermute | solution.py:22
  281.9 34.0 %collective-permute-done = bf16[1,6,128,1024]{3,2,1,0:T(8,128)(2,1)S(1)} collective-permute-done((bf16[1,6,128,1024]{3,2,1,0:T(8,128)(2,1)S(1)}, bf16[1,6,128,1024]{3,2,1,0:T(8,128)(2,1)S(1)}, u32[]{:S(2)}, u32[]{:S(2)}) %collective-permute-start) | collective-permute-done | bytes 1572896 | tf_op jit(solution)/shard_map/ppermute | solution.py:19
  317.7 3.5 collective-permute-start.3
  321.2 5.3 convolution_bitcast_fusion.1
  326.5 6.6 copy.84
  333.1 3.9 subtract_convert_fusion.3
  342.2 12.3 %convert_bitcast_fusion = bf16[1024,4,8,128]{0,3,2,1:T(8,128)(2,1)} fusion(bf16[1024,1024]{1,0:T(8,128)(2,1)S(1)} %copy-done, bf16[4,1,128,1024]{3,2,1,0:T(8,128)(2,1)} %collective-permute-done.3, bf16[1,6,128,1024]{3,2,1,0:T(8,128)(2,1)S(1)} %copy-done.6, bf16[2,6,128,1024]{3,2,1,0:T(8,128)(2,1)S(1)} %bitcast.140, ...), kind=kOutput, calls=%fused_computation.27 | convolution fusion | flops 8610906112 | bytes 18874368 | tf_op jit(solution)/shard_map/wf,rctw->frct/dot_general | solution.py:37
  354.6 12.6 %copy.83 = bf16[1024,4,8,128]{3,2,1,0:T(8,128)(2,1)} copy(bf16[1024,4,8,128]{0,3,2,1:T(8,128)(2,1)} %convert_bitcast_fusion) | data formatting | bytes 16777216 | tf_op jit(solution)/shard_map/convert_element_type | solution.py:61
  367.1 15.0 %convolution_bitcast_fusion = f32[1024,4,8,128]{0,3,2,1:T(8,128)} fusion(bf16[1024,1024]{1,0:T(8,128)(2,1)} %param.20, bf16[4,1,128,1024]{3,2,1,0:T(8,128)(2,1)} %collective-permute-done.3, bf16[1,6,128,1024]{3,2,1,0:T(8,128)(2,1)S(1)} %copy-done.7, bf16[2,6,128,1024]{3,2,1,0:T(8,128)(2,1)} %bitcast.139, bf16[1,6,128,1024]{3,2,1,0:T(8,128)(2,1)} %copy-done.8, ...), kind=kOutput, calls=%fused_computation.23 | convolution fusion | flops 8606711808 | bytes 27262976 | tf_op jit(solution)/shard_map/wf,rctw->frct/dot_general | solution.py:37
  382.1 17.5 %copy.82 = f32[1024,4,8,128]{3,2,1,0:T(8,128)} copy(f32[1024,4,8,128]{0,3,2,1:T(8,128)} %convolution_bitcast_fusion) | data formatting | bytes 33554432 | tf_op jit(solution)/shard_map/wf,rctw->frct/dot_general | solution.py:37
  399.6 7.3 fusion.10
  409.9 9.0 %copy.89 = bf16[2,16,64,32,128]{4,2,3,1,0:T(8,128)(2,1)} copy(bf16[2,16,64,32,128]{4,3,2,1,0:T(8,128)(2,1)S(1)} %pad_maximum_fusion) | data formatting | bytes 33554432 | tf_op jit(solution)/shard_map/while | solution.py:164
  419.0 325.3 %while.10 = (s32[]{:T(128)}, bf16[3,16,64,4,128]{4,2,3,1,0:T(8,128)(2,1)}, s32[3,36]{1,0:T(4,128)S(1)}, bf16[2,16,64,32,128]{4,2,3,1,0:T(8,128)(2,1)}, s32[3]{0:...) while((s32[]{:T(128)}, ...), condition=%wide.region_7.8_spmd, body=%wide.region_4.7_spmd.sunk | while | flops 2510800384 | bytes 285381568 | solution.py:164
  420.7 13.8 %gather_fusion = bf16[36,2,16,64,128]{4,3,2,1,0:T(8,128)(2,1)} fusion(bf16[2,16,64,32,128]{4,2,3,1,0:T(8,128)(2,1)} %get-tuple-element.174, s32[1024]{0:T(1024)S(1)} %pad_clamp_fusion.2), kind=kCustom, calls=%fused_computation.clone.1 | custom fusion | bytes 37748880 | tf_op jit(solution)/shard_map/while/body/eval_jaxpr/jit(_take)/gather | solution.py:154
  434.5 9.7 %select_bitcast_fusion.2 = bf16[2,16,64,36,128]{4,2,1,0,3:T(8,128)(2,1)S(1)} fusion(bf16[36,2,16,64,128]{4,3,2,1,0:T(8,128)(2,1)} %gather_fusion, pred[36]{0:T(512)(128)(4,1)S(1)} %compare_and_fusion.2), kind=kLoop, calls=%fused_computation.7.clone.1 | loop fusion | flops 9437184 | bytes 37748772 | tf_op jit(solution)/shard_map/while/body/eval_jaxpr/jit(_take)/select_n | solution.py:154
  444.3 8.3 %fusion.56 = (bf16[1,16,64,36,128]{4,2,1,0,3:T(8,128)(2,1)}, bf16[1,16,64,36,128]{4,2,1,0,3:T(8,128)(2,1)}) fusion(bf16[2,16,64,36,128]{4,2,1,0,3:T(8,128)(2,1)S(1)} %select_bitcast_fusion.2), kind=kLoop, calls=%fused_computation.103.clone.1 | loop fusion | bytes 37748736 | tf_op jit(solution)/shard_map/while/body/eval_jaxpr/slice | solution.py:156
  452.6 10.7 %copy.116 = bf16[1,16,64,36,128]{4,2,3,1,0:T(8,128)(2,1)} copy(bf16[1,16,64,36,128]{4,2,1,0,3:T(8,128)(2,1)} %get-tuple-element.147) | data formatting | bytes 18874368 | tf_op jit(solution)/shard_map/while/body/eval_jaxpr/slice | solution.py:160
  463.3 10.7 %copy.117 = bf16[1,16,64,36,128]{4,2,3,1,0:T(8,128)(2,1)} copy(bf16[1,16,64,36,128]{4,2,1,0,3:T(8,128)(2,1)} %get-tuple-element.148) | data formatting | bytes 18874368 | tf_op jit(solution)/shard_map/while/body/eval_jaxpr/slice | solution.py:156
  474.0 17.3 %multiply_reduce_fusion.3 = (f32[16,4,128]{2,1,0:T(4,128)S(1)}, f32[16,4,128,9,128]{2,4,3,1,0:T(8,128)}) fusion(bf16[16,64,4,9,128]{4,1,3,2,0:T(8,128)(2,1)} %bitcast.131, bf16[16,64,12,128]{3,1,0,2:T(8,128)(2,1)} %get-tuple-element.176, s32[]{:T(128)S(6)} %select_n.141), kind=kOutput, calls=%fused_computation.5.clone.1 | convolution fusion | flops 1226825728 | bytes 48267268 | tf_op jit(solution)/shard_map/while/body/eval_jaxpr/hdbq,hdbjk->hbqjk/dot_general | solution.py:155
  491.2 16.3 %fusion.57 = f32[16,4,128]{2,1,0:T(4,128)S(1)} fusion(f32[16,4,128,9,128]{2,4,3,1,0:T(8,128)} %get-tuple-element.149, f32[16,4,128]{2,1,0:T(4,128)S(1)} %get-tuple-element.150), kind=kLoop, calls=%fused_computation.6.clone.1 | loop fusion | flops 28303360 | bytes 37814272 | tf_op jit(solution)/shard_map/while/body/eval_jaxpr/reduce_sum | solution.py:158
  507.5 20.1 %fusion.58 = bf16[3,16,64,4,128]{4,2,3,1,0:T(8,128)(2,1)} fusion(bf16[3,16,64,4,128]{4,2,3,1,0:T(8,128)(2,1)} %get-tuple-element.162, s32[]{:T(128)S(6)} %copy.122, bf16[16,64,4,9,128]{4,1,3,2,0:T(8,128)(2,1)} %bitcast.132, f32[16,4,128,9,128]{2,4,3,1,0:T(8,128)} %get-tuple-element.149, f32[16,4,128]{2,1,0:T(4,128)S(1)} %fusion.57, ...), kind=kOutput, calls=%fused_computation.11.clone.1 | convolution fusion | flops 1246232576 | bytes 48300036 | tf_op jit(solution)/shard_map/while/body/eval_jaxpr/hbqjk,hdbjk->hdbq/dot_general | solution.py:159
  529.0 13.8 %gather_fusion = bf16[36,2,16,64,128]{4,3,2,1,0:T(8,128)(2,1)} fusion(bf16[2,16,64,32,128]{4,2,3,1,0:T(8,128)(2,1)} %get-tuple-element.174, s32[1024]{0:T(1024)S(1)} %pad_clamp_fusion.2), kind=kCustom, calls=%fused_computation.clone.1 | custom fusion | bytes 37748880 | tf_op jit(solution)/shard_map/while/body/eval_jaxpr/jit(_take)/gather | solution.py:154
  542.8 9.7 %select_bitcast_fusion.2 = bf16[2,16,64,36,128]{4,2,1,0,3:T(8,128)(2,1)S(1)} fusion(bf16[36,2,16,64,128]{4,3,2,1,0:T(8,128)(2,1)} %gather_fusion, pred[36]{0:T(512)(128)(4,1)S(1)} %compare_and_fusion.2), kind=kLoop, calls=%fused_computation.7.clone.1 | loop fusion | flops 9437184 | bytes 37748772 | tf_op jit(solution)/shard_map/while/body/eval_jaxpr/jit(_take)/select_n | solution.py:154
  552.5 8.3 %fusion.56 = (bf16[1,16,64,36,128]{4,2,1,0,3:T(8,128)(2,1)}, bf16[1,16,64,36,128]{4,2,1,0,3:T(8,128)(2,1)}) fusion(bf16[2,16,64,36,128]{4,2,1,0,3:T(8,128)(2,1)S(1)} %select_bitcast_fusion.2), kind=kLoop, calls=%fused_computation.103.clone.1 | loop fusion | bytes 37748736 | tf_op jit(solution)/shard_map/while/body/eval_jaxpr/slice | solution.py:156
  560.9 10.7 %copy.116 = bf16[1,16,64,36,128]{4,2,3,1,0:T(8,128)(2,1)} copy(bf16[1,16,64,36,128]{4,2,1,0,3:T(8,128)(2,1)} %get-tuple-element.147) | data formatting | bytes 18874368 | tf_op jit(solution)/shard_map/while/body/eval_jaxpr/slice | solution.py:160
  571.5 10.7 %copy.117 = bf16[1,16,64,36,128]{4,2,3,1,0:T(8,128)(2,1)} copy(bf16[1,16,64,36,128]{4,2,1,0,3:T(8,128)(2,1)} %get-tuple-element.148) | data formatting | bytes 18874368 | tf_op jit(solution)/shard_map/while/body/eval_jaxpr/slice | solution.py:156
  582.2 17.3 %multiply_reduce_fusion.3 = (f32[16,4,128]{2,1,0:T(4,128)S(1)}, f32[16,4,128,9,128]{2,4,3,1,0:T(8,128)}) fusion(bf16[16,64,4,9,128]{4,1,3,2,0:T(8,128)(2,1)} %bitcast.131, bf16[16,64,12,128]{3,1,0,2:T(8,128)(2,1)} %get-tuple-element.176, s32[]{:T(128)S(6)} %select_n.141), kind=kOutput, calls=%fused_computation.5.clone.1 | convolution fusion | flops 1226825728 | bytes 48267268 | tf_op jit(solution)/shard_map/while/body/eval_jaxpr/hdbq,hdbjk->hbqjk/dot_general | solution.py:155
  599.5 16.3 %fusion.57 = f32[16,4,128]{2,1,0:T(4,128)S(1)} fusion(f32[16,4,128,9,128]{2,4,3,1,0:T(8,128)} %get-tuple-element.149, f32[16,4,128]{2,1,0:T(4,128)S(1)} %get-tuple-element.150), kind=kLoop, calls=%fused_computation.6.clone.1 | loop fusion | flops 28303360 | bytes 37814272 | tf_op jit(solution)/shard_map/while/body/eval_jaxpr/reduce_sum | solution.py:158
  615.8 20.1 %fusion.58 = bf16[3,16,64,4,128]{4,2,3,1,0:T(8,128)(2,1)} fusion(bf16[3,16,64,4,128]{4,2,3,1,0:T(8,128)(2,1)} %get-tuple-element.162, s32[]{:T(128)S(6)} %copy.122, bf16[16,64,4,9,128]{4,1,3,2,0:T(8,128)(2,1)} %bitcast.132, f32[16,4,128,9,128]{2,4,3,1,0:T(8,128)} %get-tuple-element.149, f32[16,4,128]{2,1,0:T(4,128)S(1)} %fusion.57, ...), kind=kOutput, calls=%fused_computation.11.clone.1 | convolution fusion | flops 1246232576 | bytes 48300036 | tf_op jit(solution)/shard_map/while/body/eval_jaxpr/hbqjk,hdbjk->hdbq/dot_general | solution.py:159
  637.2 13.7 %gather_fusion = bf16[36,2,16,64,128]{4,3,2,1,0:T(8,128)(2,1)} fusion(bf16[2,16,64,32,128]{4,2,3,1,0:T(8,128)(2,1)} %get-tuple-element.174, s32[1024]{0:T(1024)S(1)} %pad_clamp_fusion.2), kind=kCustom, calls=%fused_computation.clone.1 | custom fusion | bytes 37748880 | tf_op jit(solution)/shard_map/while/body/eval_jaxpr/jit(_take)/gather | solution.py:154
  651.0 9.7 %select_bitcast_fusion.2 = bf16[2,16,64,36,128]{4,2,1,0,3:T(8,128)(2,1)S(1)} fusion(bf16[36,2,16,64,128]{4,3,2,1,0:T(8,128)(2,1)} %gather_fusion, pred[36]{0:T(512)(128)(4,1)S(1)} %compare_and_fusion.2), kind=kLoop, calls=%fused_computation.7.clone.1 | loop fusion | flops 9437184 | bytes 37748772 | tf_op jit(solution)/shard_map/while/body/eval_jaxpr/jit(_take)/select_n | solution.py:154
  660.7 8.3 %fusion.56 = (bf16[1,16,64,36,128]{4,2,1,0,3:T(8,128)(2,1)}, bf16[1,16,64,36,128]{4,2,1,0,3:T(8,128)(2,1)}) fusion(bf16[2,16,64,36,128]{4,2,1,0,3:T(8,128)(2,1)S(1)} %select_bitcast_fusion.2), kind=kLoop, calls=%fused_computation.103.clone.1 | loop fusion | bytes 37748736 | tf_op jit(solution)/shard_map/while/body/eval_jaxpr/slice | solution.py:156
  669.0 10.7 %copy.116 = bf16[1,16,64,36,128]{4,2,3,1,0:T(8,128)(2,1)} copy(bf16[1,16,64,36,128]{4,2,1,0,3:T(8,128)(2,1)} %get-tuple-element.147) | data formatting | bytes 18874368 | tf_op jit(solution)/shard_map/while/body/eval_jaxpr/slice | solution.py:160
  679.7 10.7 %copy.117 = bf16[1,16,64,36,128]{4,2,3,1,0:T(8,128)(2,1)} copy(bf16[1,16,64,36,128]{4,2,1,0,3:T(8,128)(2,1)} %get-tuple-element.148) | data formatting | bytes 18874368 | tf_op jit(solution)/shard_map/while/body/eval_jaxpr/slice | solution.py:156
  690.4 17.3 %multiply_reduce_fusion.3 = (f32[16,4,128]{2,1,0:T(4,128)S(1)}, f32[16,4,128,9,128]{2,4,3,1,0:T(8,128)}) fusion(bf16[16,64,4,9,128]{4,1,3,2,0:T(8,128)(2,1)} %bitcast.131, bf16[16,64,12,128]{3,1,0,2:T(8,128)(2,1)} %get-tuple-element.176, s32[]{:T(128)S(6)} %select_n.141), kind=kOutput, calls=%fused_computation.5.clone.1 | convolution fusion | flops 1226825728 | bytes 48267268 | tf_op jit(solution)/shard_map/while/body/eval_jaxpr/hdbq,hdbjk->hbqjk/dot_general | solution.py:155
  707.7 16.3 %fusion.57 = f32[16,4,128]{2,1,0:T(4,128)S(1)} fusion(f32[16,4,128,9,128]{2,4,3,1,0:T(8,128)} %get-tuple-element.149, f32[16,4,128]{2,1,0:T(4,128)S(1)} %get-tuple-element.150), kind=kLoop, calls=%fused_computation.6.clone.1 | loop fusion | flops 28303360 | bytes 37814272 | tf_op jit(solution)/shard_map/while/body/eval_jaxpr/reduce_sum | solution.py:158
  724.0 20.1 %fusion.58 = bf16[3,16,64,4,128]{4,2,3,1,0:T(8,128)(2,1)} fusion(bf16[3,16,64,4,128]{4,2,3,1,0:T(8,128)(2,1)} %get-tuple-element.162, s32[]{:T(128)S(6)} %copy.122, bf16[16,64,4,9,128]{4,1,3,2,0:T(8,128)(2,1)} %bitcast.132, f32[16,4,128,9,128]{2,4,3,1,0:T(8,128)} %get-tuple-element.149, f32[16,4,128]{2,1,0:T(4,128)S(1)} %fusion.57, ...), kind=kOutput, calls=%fused_computation.11.clone.1 | convolution fusion | flops 1246232576 | bytes 48300036 | tf_op jit(solution)/shard_map/while/body/eval_jaxpr/hbqjk,hdbjk->hdbq/dot_general | solution.py:159
  744.3 6.0 copy.90
  750.3 6.1 dot_general.44
  756.3 9.8 %fusion.9 = bf16[1536,1024]{1,0:T(8,128)(2,1)} fusion(f32[1536,1024]{1,0:T(8,128)} %copy-done.2, bf16[1536,64,16]{0,2,1:T(8,128)(2,1)} %dot_general.44, bf16[16,64,1024]{2,1,0:T(8,128)(2,1)} %bitcast.151), kind=kOutput, calls=%fused_computation.29 | convolution fusion | flops 3224371200 | bytes 14680064 | tf_op jit(solution)/shard_map/nhdgq,hde->ngqe/dot_general | solution.py:165
  (88 shorter events, 27.5 us)
Async XLA Ops:
  0.0 342.2 %copy-start = (bf16[1024,1024]{1,0:T(8,128)(2,1)S(1)}, bf16[1024,1024]{1,0:T(8,128)(2,1)}, u32[]{:S(2)}) copy-start(bf16[1024,1024]{1,0:T(8,128)(2,1)} %param.21) | copy-start | bytes 6291460
  4.8 36.9 %all-to-all-start = ((s32[32,8,1]{1,2,0:T(1,128)}), s32[32,8,1]{1,2,0:T(1,128)S(1)}, u32[]{:S(2)}, u32[]{:S(2)}) async-start(s32[32,8,1]{1,2,0:T(1,128)} %bitcast.16), calls=%async_computation | async-start | bytes 32768 | tf_op jit(solution)/shard_map/all_to_all | solution.py:101
  41.6 6.0 copy-start.11
  41.6 189.7 %all-to-all-start.1 = ((bf16[256,128,128]{2,1,0:T(8,128)(2,1)}), bf16[256,128,128]{2,1,0:T(8,128)(2,1)}, u32[]{:S(2)}, u32[]{:S(2)}) async-start(bf16[256,128,128]{2,1,0:T(8,128)(2,1)} %scatter_fusion), calls=%async_computation.1 | async-start | bytes 16777216 | tf_op jit(solution)/shard_map/all_to_all | solution.py:100
  49.0 190.4 %copy-start.10 = (bf16[128,1024]{1,0:T(8,128)(2,1)S(1)}, bf16[128,1024]{1,0:T(8,128)(2,1)}, u32[]{:S(2)}) copy-start(bf16[128,1024]{1,0:T(8,128)(2,1)} %param.17) | copy-start | bytes 786436
  239.3 1.1 copy-start.12
  240.4 2.6 copy-start.2
  243.0 78.2 %copy-start.3 = (bf16[1536,1024]{1,0:T(8,128)(2,1)}, bf16[1536,1024]{1,0:T(8,128)(2,1)S(1)}, u32[]{:S(2)}) copy-start(bf16[1536,1024]{1,0:T(8,128)(2,1)S(1)} %multiply_convert_fusion) | copy-start | bytes 9437188
  243.3 38.5 %collective-permute-start.1 = (bf16[1,6,128,1024]{3,2,1,0:T(8,128)(2,1)S(1)}, bf16[1,6,128,1024]{3,2,1,0:T(8,128)(2,1)S(1)}, u32[]{:S(2)}, u32[]{:S(2)}) collective-permute-start(bf16[1,6,128,1024]{3,2,1,0:T(8,128)(2,1)S(1)} %bitcast.150), channel_id=1, source_target_pairs={{8,0},{16,8},{24,16},{9,1},{17,9},{25,17},{10,2},{18,10},{26,18},{... | collective-permute-start | bytes 4718600 | tf_op jit(solution)/shard_map/ppermute | solution.py:22
  245.8 70.0 %collective-permute-start = (bf16[1,6,128,1024]{3,2,1,0:T(8,128)(2,1)S(1)}, bf16[1,6,128,1024]{3,2,1,0:T(8,128)(2,1)S(1)}, u32[]{:S(2)}, u32[]{:S(2)}) collective-permute-start(bf16[1,6,128,1024]{3,2,1,0:T(8,128)(2,1)S(1)} %bitcast.149), channel_id=1, source_target_pairs={{0,8},{8,16},{16,24},{1,9},{9,17},{17,25},{2,10},{10,18},{18,26},{... | collective-permute-start | bytes 4718600 | tf_op jit(solution)/shard_map/ppermute | solution.py:19
  281.8 35.6 %copy-start.5 = (bf16[1,6,128,1024]{3,2,1,0:T(8,128)(2,1)}, bf16[1,6,128,1024]{3,2,1,0:T(8,128)(2,1)S(1)}, u32[]{:S(2)}) copy-start(bf16[1,6,128,1024]{3,2,1,0:T(8,128)(2,1)S(1)} %collective-permute-done.1) | copy-start | bytes 4718596
  315.8 1.9 copy-start.8
  315.8 5.4 copy-start.13
  317.7 24.5 %collective-permute-start.2 = (bf16[4,1,128,1024]{3,2,1,0:T(8,128)(2,1)}, bf16[4,1,128,1024]{3,2,1,0:T(8,128)(2,1)}, u32[]{:S(2)}, u32[]{:S(2)}) collective-permute-start(bf16[4,1,128,1024]{3,2,1,0:T(8,128)(2,1)} %get-tuple-element.84), channel_id=1, source_target_pairs={{0,1},{1,2},{2,3},{3,4},{4,5},{5,6},{6,7},{7,0},{8,9},{9,10},{10,1... | collective-permute-start | bytes 3145736 | tf_op jit(solution)/shard_map/ppermute | solution.py:19
  317.7 24.5 %collective-permute-start.3 = (bf16[4,1,128,1024]{3,2,1,0:T(8,128)(2,1)}, bf16[4,1,128,1024]{3,2,1,0:T(8,128)(2,1)}, u32[]{:S(2)}, u32[]{:S(2)}) collective-permute-start(bf16[4,1,128,1024]{3,2,1,0:T(8,128)(2,1)} %get-tuple-element.85), channel_id=1, source_target_pairs={{1,0},{2,1},{3,2},{4,3},{5,4},{6,5},{7,6},{0,7},{9,8},{10,9},{11,1... | collective-permute-start | bytes 3145736 | tf_op jit(solution)/shard_map/ppermute | solution.py:22
  337.0 5.2 copy-start.4
  337.0 5.2 copy-start.6
  337.0 5.2 copy-start.9
  354.6 12.6 %copy-start.7 = (bf16[1,6,128,1024]{3,2,1,0:T(8,128)(2,1)S(1)}, bf16[1,6,128,1024]{3,2,1,0:T(8,128)(2,1)}, u32[]{:S(2)}) copy-start(bf16[1,6,128,1024]{3,2,1,0:T(8,128)(2,1)} %copy-done.5) | copy-start | bytes 4718596
  399.6 7.3 slice-start
  399.6 8.3 %slice-start.1 = ((s8[8388608]{0:T(1024)(128)(4,1)}), s8[4194304]{0:T(1024)(128)(4,1)S(1)}, s32[]{:S(2)}) async-start(s8[8388608]{0:T(1024)(128)(4,1)} %bitcast.134), calls=%async_computation.3 | async-start | bytes 8388608
  756.3 9.8 %copy-start.1 = (bf16[1024,1024]{1,0:T(8,128)(2,1)S(1)}, bf16[1024,1024]{1,0:T(8,128)(2,1)}, u32[]{:S(2)}) copy-start(bf16[1024,1024]{1,0:T(8,128)(2,1)} %param.21) | copy-start | bytes 6291460
where the time goes:
time: 778 us; the launch traced here: 766 us
  waiting for transfers between devices  237 us (30%)
  local copies, waits for them, and re-layouts  223 us (29%)
  matrix products  170 us (22%)
  other arithmetic  100 us (13%)
  starting transfers between devices  33.8 us (4%)
    all_to_all x1, waiting for transfers between devices, body(): lax.all_to_all(send_parts, ('band', 'sector'), split_axis=0, concat_axis=...  182 us
    dot_general x3, matrix products, attend(): jnp.einsum('hbqjk,hdbjk->hdbq', probs, chosen[1], preferred_element_type=...  60.4 us
    slice x6, local copies, waits for them, and re-layouts, attend(): chosen[0]  57 us
    dot_general x3, matrix products, attend(): jnp.einsum('hdbq,hdbjk->hbqjk', query_heads, chosen[0], preferred_element...  51.8 us
    reduce_sum x3, other arithmetic, attend(): probs = jax.nn.softmax(scores, axis=(-2, -1)).astype(jnp.bfloat16)  48.9 us
    gather x3, local copies, waits for them, and re-layouts, attend(): jnp.take(ext_flat, listed, axis=3).reshape(2, HEADS, HD, group, 9, tile)  41.4 us
    ppermute x2, waiting for transfers between devices, padded(): lax.ppermute(lax.slice_in_dim(block, block.shape[dim] - width, None, axis...  37.1 us
    dot_general x3, matrix products, project_heads(): jnp.einsum('wf,rctw->frct', weight, tiles, preferred_element_type=jnp.flo...  32.6 us
  transfers between devices with their start and end apart: 6, of which 4 were waited for; matrix products, arithmetic and copies ran while one was open for 7% of the time, Pallas kernels for 0%

commit v1 on v0

v1 whole, which is shorter than its diff:
```python
import functools
import math

import jax
import jax.numpy as jnp
from jax import lax
from jax.experimental import pallas as pl
from jax.experimental.pallas import tpu as pltpu
from jax.sharding import PartitionSpec as P

HEADS = 16
HD = 64
GROUP = 4
NGROUP = HEADS // GROUP
GW = GROUP * HD
QUARTER = HD // 4
LISTED = 9
PAIRS = (LISTED + 1) // 2


def padded(block, sides, width, periodic):
    for axis, dim in sides:
        count = lax.axis_size(axis)
        forward = [(i, i + 1) for i in range(count - 1)]
        if periodic:
            forward.append((count - 1, 0))
        backward = [(target, source) for source, target in forward]
        low = lax.ppermute(
            lax.slice_in_dim(block, block.shape[dim] - width, None, axis=dim), axis, forward
        )
        high = lax.ppermute(lax.slice_in_dim(block, 0, width, axis=dim), axis, backward)
        block = jnp.concatenate([low, block, high], axis=dim)
    return block


def rotary_tables(ext_rows, ext_cols, nrows, ncols, tile):
    place = jnp.arange(tile)
    across = (place // 16).astype(jnp.float32)
    along = (place % 16).astype(jnp.float32)
    theta = math.pi * (ext_rows[:, None].astype(jnp.float32) + (across + 0.5) * 16.0 / tile) / nrows
    phi = 2.0 * math.pi * (ext_cols[:, None].astype(jnp.float32) + (along + 0.5) / 16.0) / ncols
    lane = jnp.arange(GROUP * 2 * QUARTER)
    freq = (lane % QUARTER + 1).astype(jnp.float32)
    lon = (lane // QUARTER) % 2 == 1
    lat_angle = theta[:, :, None] * freq
    lon_angle = phi[:, :, None] * freq
    return (
        jnp.where(lon, 0.0, jnp.cos(lat_angle)),
        jnp.where(lon, 0.0, jnp.sin(lat_angle)),
        jnp.where(lon, jnp.cos(lon_angle), 0.0),
        jnp.where(lon, jnp.sin(lon_angle), 0.0),
    )


def pair_order():
    new = jnp.arange(GW)
    second = new // (GW // 2)
    rest = new % (GW // 2)
    old = rest // (2 * QUARTER) * HD + (rest // QUARTER) % 2 * 2 * QUARTER + second * QUARTER
    old = old + rest % QUARTER
    return (jnp.arange(GW)[:, None] == old[None, :]).astype(jnp.bfloat16)


def window_kernel(
    sel,
    cnt,
    npair,
    ext,
    lat_cos,
    lat_sin,
    lon_cos,
    lon_sin,
    gain,
    w_embed,
    w_query,
    w_key,
    w_value,
    w_out,
    order,
    out,
    keys,
    values,
    queries,
    embedded,
    wq_pairs,
    wk_pairs,
    normed,
    attended,
):
    row = pl.program_id(0)
    erows, ecols, tile, chan = ext.shape
    tcols = ecols - 2
    width = w_embed.shape[1]
    f32 = jnp.float32
    bf16 = jnp.bfloat16

    def project_row(r, own):
        for c in range(0, ecols, 2):
            x = ext[r, c : c + 2].reshape(2 * tile, chan)
            emb = jnp.dot(x, w_embed[...], preferred_element_type=f32)
            meansq = jnp.mean(emb * emb, axis=-1, keepdims=True)
            scaled = emb * lax.rsqrt(meansq + 1e-05) * gain[...]
            normed[c * tile : (c + 2) * tile, :] = scaled.astype(bf16)
            if own:
                for k in range(2):
                    if 1 <= c + k <= tcols:
                        embedded[r - 1, c + k - 1] = emb[k * tile : (k + 1) * tile]

        def turn(full, c):
            cosine = lat_cos[r] + lon_cos[c]
            sine = lat_sin[r] + lon_sin[c]
            lower = full[:, : GW // 2]
            upper = full[:, GW // 2 :]
            return jnp.concatenate(
                [lower * cosine - upper * sine, lower * sine + upper * cosine], axis=1
            )

        def one_group(g, _):
            full = jnp.dot(normed[...], wk_pairs[g], preferred_element_type=f32)
            for c in range(ecols):
                keys[r * ecols + c, g] = turn(full[c * tile : (c + 1) * tile], c).astype(bf16)
            full = jnp.dot(normed[...], w_value[g], preferred_element_type=f32)
            for c in range(ecols):
                values[r * ecols + c, g] = full[c * tile : (c + 1) * tile].astype(bf16)
            if own:
                full = jnp.dot(
                    normed[tile : (tcols + 1) * tile, :], wq_pairs[g], preferred_element_type=f32
                )
                for c in range(tcols):
                    turned = turn(full[c * tile : (c + 1) * tile], c + 1)
                    queries[(r - 1) * tcols + c, g] = (
                        turned * (math.log2(math.e) / math.sqrt(HD))
                    ).astype(bf16)
            return 0

        lax.fori_loop(0, NGROUP, one_group, 0)

    @pl.when(row == 0)
    def _():
        for g in range(NGROUP):
            wq_pairs[g] = jnp.dot(w_query[g], order[...], preferred_element_type=f32).astype(bf16)
            wk_pairs[g] = jnp.dot(w_key[g], order[...], preferred_element_type=f32).astype(bf16)
        project_row(0, False)

        def own_row(r, _):
            project_row(r, True)
            return 0

        lax.fori_loop(1, erows - 1, own_row, 0)
        project_row(erows - 1, False)

    lane = lax.broadcasted_iota(jnp.int32, (tile, GW), 1)
    pair_head = lane % (GW // 2) // (2 * QUARTER)
    value_head = lane // HD

    def one_tile(c, _):
        t = row * tcols + c

        def with_pairs(count):
            def one_group(g, _):
                query = queries[t, g]
                stacked = jnp.concatenate(
                    [jnp.where(pair_head == h, query, jnp.zeros_like(query)) for h in range(GROUP)],
                    axis=0,
                )
                scores = []
                for j in range(count):
                    near = jnp.concatenate(
                        [keys[sel[t, 2 * j], g], keys[sel[t, 2 * j + 1], g]], axis=0
                    )
                    scores.append(
                        lax.dot_general(
                            stacked, near, (((1,), (1,)), ((), ())), preferred_element_type=f32
                        )
                    )
                top = functools.reduce(jnp.maximum, scores)
                top = jnp.max(top, axis=1, keepdims=True)
                total = jnp.zeros((GROUP * tile, tile), f32)
                mixed = jnp.zeros((GROUP * tile, GW), f32)
                for j in range(count):
                    probs = jnp.exp2(scores[j] - top)
                    first = probs[:, :tile] * cnt[t, 2 * j]
                    second = probs[:, tile:] * cnt[t, 2 * j + 1]
                    total = total + (first + second)
                    near = jnp.concatenate(
                        [values[sel[t, 2 * j], g], values[sel[t, 2 * j + 1], g]], axis=0
                    )
                    mixed = mixed + jnp.dot(
                        jnp.concatenate([first, second], axis=1).astype(bf16),
                        near,
                        preferred_element_type=f32,
                    )
                mixed = mixed / jnp.sum(total, axis=1, keepdims=True)
                result = mixed[:tile]
                for h in range(1, GROUP):
                    result = jnp.where(value_head == h, mixed[h * tile : (h + 1) * tile], result)
                attended[g, pl.ds(pl.multiple_of(c * tile, tile), tile), :] = result.astype(bf16)
                return 0

            lax.fori_loop(0, NGROUP, one_group, 0)

        for count in range(1, PAIRS + 1):
            pl.when(npair[t] == count)(functools.partial(with_pairs, count))
        return 0

    lax.fori_loop(0, tcols, one_tile, 0)
    for c in range(0, tcols, 2):
        rows = slice(c * tile, (c + 2) * tile)
        together = jnp.concatenate([attended[g, rows, :] for g in range(NGROUP)], axis=1)
        result = jnp.dot(together, w_out[...], preferred_element_type=f32)
        result = result + embedded[row, c : c + 2].reshape(2 * tile, width)
        out[0, c : c + 2] = result.astype(bf16).reshape(2, tile, width)


def whole(shape):
    return pl.BlockSpec(shape, lambda *_: (0,) * len(shape), pipeline_mode=pl.Buffered(1))


def window(sel, cnt, npair, operands, trows, tcols):
    ext = operands[0]
    erows, ecols, tile, chan = ext.shape
    width = operands[6].shape[1]
    owned = trows * tcols
    bf16 = jnp.bfloat16
    return pl.pallas_call(
        window_kernel,
        out_shape=jax.ShapeDtypeStruct((trows, tcols, tile, width), bf16),
        grid_spec=pltpu.PrefetchScalarGridSpec(
            num_scalar_prefetch=3,
            grid=(trows,),
            in_specs=[whole(x.shape) for x in operands],
            out_specs=pl.BlockSpec((1, tcols, tile, width), lambda r, *_: (r, 0, 0, 0)),
            scratch_shapes=[
                pltpu.VMEM((erows * ecols, NGROUP, tile, GW), bf16),
                pltpu.VMEM((erows * ecols, NGROUP, tile, GW), bf16),
                pltpu.VMEM((owned, NGROUP, tile, GW), bf16),
                pltpu.VMEM((trows, tcols, tile, width), jnp.float32),
                pltpu.VMEM((NGROUP, width, GW), bf16),
                pltpu.VMEM((NGROUP, width, GW), bf16),
                pltpu.VMEM((ecols * tile, width), bf16),
                pltpu.VMEM((NGROUP, tcols * tile, GW), bf16),
            ],
        ),
        compiler_params=pltpu.CompilerParams(vmem_limit_bytes=62 * 1024 * 1024),
    )(sel, cnt, npair, *operands)


def distinct_tiles(index):
    same = index[:, :, None] == index[:, None, :]
    times = jnp.sum(same, axis=2)
    order = jnp.arange(LISTED)
    new = ~jnp.any(same & (order[None, None, :] < order[None, :, None]), axis=2)
    place = jnp.sum(new[:, None, :] & (order[None, None, :] < order[None, :, None]), axis=2)
    slots = jnp.arange(2 * PAIRS)
    put = new[:, :, None] & (place[:, :, None] == slots[None, None, :])
    found = jnp.any(put, axis=1)
    sel = jnp.where(found, jnp.sum(jnp.where(put, index[:, :, None], 0), axis=1), index[:, :1])
    cnt = jnp.sum(jnp.where(put, times[:, :, None], 0), axis=1).astype(jnp.float32)
    npair = (jnp.sum(new, axis=1) + 1) // 2
    return sel.astype(jnp.int32), cnt, npair.astype(jnp.int32)


def by_group(weight):
    return jnp.swapaxes(weight.reshape(weight.shape[0], NGROUP, GW), 0, 1)


def body(
    grid_cells,
    remap_weight,
    remap_dest,
    remap_tile,
    w_embed,
    norm_gain,
    w_query,
    w_key,
    w_value,
    w_out,
    neighbours,
):
    nband = lax.axis_size("band")
    nsect = lax.axis_size("sector")
    ndev = nband * nsect
    blocks, top, rowcells, tile = remap_weight.shape
    chan = grid_cells.shape[2]
    trows, tcols = (neighbours.shape[0], neighbours.shape[1])
    cap = max(2, 2 * blocks * top // ndev)
    items = blocks * top
    parts = jnp.einsum(
        "rkct,rcf->rktf", remap_weight, grid_cells, preferred_element_type=jnp.float32
    )
    parts = parts.astype(jnp.bfloat16).reshape(items, tile, chan)
    dest = remap_dest.reshape(-1)
    local = remap_tile.reshape(-1)
    order = jnp.arange(items)
    earlier = (dest[:, None] == dest[None, :]) & (order[None, :] < order[:, None])
    rank = jnp.sum(earlier.astype(jnp.int32), axis=1)
    slot = dest * cap + rank
    send_parts = jnp.zeros((ndev * cap, tile, chan), jnp.bfloat16).at[slot].set(parts)
    send_ids = jnp.full((ndev * cap,), -1, jnp.int32).at[slot].set(local)
    got_parts, got_ids = (
        lax.all_to_all(send_parts, ("band", "sector"), split_axis=0, concat_axis=0, tiled=True),
        lax.all_to_all(send_ids, ("band", "sector"), split_axis=0, concat_axis=0, tiled=True),
    )
    owned = trows * tcols
    select = (got_ids[None, :] == jnp.arange(owned)[:, None]).astype(jnp.bfloat16)
    remapped = jnp.einsum(
        "ls,stc->ltc", select, got_parts, preferred_element_type=jnp.float32
    ).astype(jnp.bfloat16)
    band_at = lax.axis_index("band")
    sect_at = lax.axis_index("sector")
    nrows = trows * nband
    ncols = tcols * nsect
    ext = padded(remapped.reshape(trows, tcols, tile, chan), (("band", 0),), 1, False)
    ext = padded(ext, (("sector", 1),), 1, True)
    ext_rows = band_at * trows - 1 + jnp.arange(trows + 2)
    ext_cols = jnp.mod(sect_at * tcols - 1 + jnp.arange(tcols + 2), ncols)
    tables = rotary_tables(ext_rows, ext_cols, nrows, ncols, tile)
    local_row = neighbours // ncols - band_at * trows + 1
    local_col = jnp.mod(neighbours % ncols - sect_at * tcols + 1, ncols)
    index = (local_row * (tcols + 2) + local_col).reshape(owned, LISTED)
    sel, cnt, npair = distinct_tiles(index)
    operands = (ext, *tables, norm_gain.reshape(1, -1), w_embed)
    operands += (by_group(w_query), by_group(w_key), by_group(w_value), w_out, pair_order())
    return window(sel, cnt, npair, operands, trows, tcols)


def solution(mesh):
    return jax.shard_map(
        body,
        mesh=mesh,
        in_specs=(
            P(("band", "sector"), None, None),
            P(("band", "sector"), None, None, None),
            P(("band", "sector"), None),
            P(("band", "sector"), None),
            P(),
            P(),
            P(),
            P(),
            P(),
            P(),
            P("band", "sector", None),
        ),
        out_specs=P("band", "sector", None, None),
        check_vma=False,
    )
```

time: 778 us -> 362 us (0.47); the launches traced: 766 us -> 359 us
  local copies, waits for them, and re-layouts: 223 us -> 45.8 us
  matrix products: 170 us -> 14 us
  Pallas kernels: 0 us -> 98.9 us
  other arithmetic: 100 us -> 11.4 us
  waiting for transfers between devices: 237 us -> 170 us
  starting transfers between devices: 33.8 us -> 18.4 us
    dot_general x11 -> x0, matrix products: 156 us -> none  [the longest x3 60.4 us: attend(): jnp.einsum('hbqjk,hdbjk->hdbq', probs, chosen[1], preferred_element_type=...]
    pallas_call x0 -> x1, Pallas kernels: none -> 98.9 us  [window(): pl.pallas_call(window_kernel, out_shape=jax.ShapeDtypeStruct((trows, tcol...]
    slice x9 -> x1, local copies, waits for them, and re-layouts: 89 us -> 0.11 us  [distinct_tiles(): index[:, :1]]
    reduce_sum x3, other arithmetic: 48.9 us -> 0.63 us  [the longest x1 0.46 us: distinct_tiles(): times = jnp.sum(same, axis=2)]
    gather x3 -> x0, local copies, waits for them, and re-layouts: 41.4 us -> none  [attend(): jnp.take(ext_flat, listed, axis=3).reshape(2, HEADS, HD, group, 9, tile)]
    dot_general x4 -> x1, local copies, waits for them, and re-layouts: 36.1 us -> 0.1 us  [body(): jnp.einsum('ls,stc->ltc', select, got_parts, preferred_element_type=jnp.f...]
    ppermute x2, waiting for transfers between devices: 37.1 us -> 7.54 us  [padded(): lax.ppermute(lax.slice_in_dim(block, block.shape[dim] - width, None, axis...]
    all_to_all x1, waiting for transfers between devices: 182 us -> 158 us  [body(): lax.all_to_all(send_parts, ('band', 'sector'), split_axis=0, concat_axis=...]
  transfers between devices with their start and end apart: 6 -> 6, of which waited for: 4 -> 5; matrix products, arithmetic and copies ran while one was open for 7% -> 16% of each run, Pallas kernels for 0% -> 0%
where the time goes in v1:
time: 362 us; the launch traced here: 359 us
  waiting for transfers between devices  170 us (47%)
  Pallas kernels  98.9 us (27%)
  local copies, waits for them, and re-layouts  45.8 us (13%)
  starting transfers between devices  18.4 us (5%)
  matrix products  14 us (4%)
  other arithmetic  11.4 us (3%)
    all_to_all x1, waiting for transfers between devices, body(): lax.all_to_all(send_parts, ('band', 'sector'), split_axis=0, concat_axis=...  158 us
    pallas_call x1, Pallas kernels, window(): pl.pallas_call(window_kernel, out_shape=jax.ShapeDtypeStruct((trows, tcol...  98.9 us
    scatter x1, local copies, waits for them, and re-layouts, body(): jnp.zeros((ndev * cap, tile, chan), jnp.bfloat16).at[slot].set(parts)  19.4 us
    unnamed x7, local copies, waits for them, and re-layouts  10.1 us
    dot_general x1, matrix products, body(): jnp.einsum('ls,stc->ltc', select, got_parts, preferred_element_type=jnp.f...  7.91 us
    reshape x3, local copies, waits for them, and re-layouts, by_group(): return jnp.swapaxes(weight.reshape(weight.shape[0], NGROUP, GW), 0, 1)  7.77 us
    ppermute x2, waiting for transfers between devices, padded(): lax.ppermute(lax.slice_in_dim(block, block.shape[dim] - width, None, axis...  7.54 us
  transfers between devices with their start and end apart: 6, of which 5 were waited for; matrix products, arithmetic and copies ran while one was open for 16% of the time, Pallas kernels for 0%

profile of v1, /device:TPU:4, one launch (start us, length us, event | category | flops | bytes accessed | tf_op | source)
XLA Modules:
  0.0 359.1 jit_solution(9334292299278419158)
XLA Ops:
  0.0 0.7 broadcast_multiply_fusion
  0.7 0.8 copy.52
  1.4 0.1 copy.51
  1.5 0.1 mul.98
  1.7 0.1 eq.100
  1.8 0.2 convert_reduce_fusion.1
  2.0 0.8 copy.53
  2.8 0.1 reshape.281
  2.9 1.0 scatter_custom_fusion
  3.9 0.7 all_to_all.9
  4.6 6.1 %all-to-all-start = ((s32[32,8,1]{1,2,0:T(1,128)}), s32[32,8,1]{1,2,0:T(1,128)S(1)}, u32[]{:S(2)}, u32[]{:S(2)}) async-start(s32[32,8,1]{1,2,0:T(1,128)} %bitcast.2), calls=%async_computation | async-start | bytes 32768 | tf_op jit(solution)/shard_map/all_to_all | solution.py:302
  10.7 6.1 %convolution_convert_fusion = bf16[64,2,128,128]{3,2,1,0:T(8,128)(2,1)} fusion(bf16[64,2,128,128]{3,2,1,0:T(8,128)(2,1)} %param.12, bf16[64,128,128]{2,1,0:T(8,128)(2,1)} %param.11), kind=kOutput, calls=%fused_computation.4 | convolution fusion | flops 538968064 | bytes 10485760 | tf_op jit(solution)/shard_map/rkct,rcf->rktf/dot_general | solution.py:288
  16.8 5.3 %broadcast_in_dim.89 = bf16[256,128,128]{2,1,0:T(8,128)(2,1)} broadcast(bf16[]{:T(256)} %constant.181.clone.1), dimensions={} | broadcast | bytes 8388610 | tf_op jit(solution)/shard_map/broadcast_in_dim | solution.py:298
  22.2 19.4 %scatter_fusion = bf16[256,128,128]{2,1,0:T(8,128)(2,1)} fusion(bf16[256,128,128]{2,1,0:T(8,128)(2,1)} %broadcast_in_dim.89, s32[128]{0:T(128)S(1)} %fusion.29, bf16[128,128,128]{2,1,0:T(8,128)(2,1)} %bitcast.30), kind=kCustom, calls=%fused_computation.1 | custom fusion | bytes 12583424 | tf_op jit(solution)/shard_map/scatter | solution.py:298
  41.5 5.9 %all-to-all-start.1 = ((bf16[256,128,128]{2,1,0:T(8,128)(2,1)}), bf16[256,128,128]{2,1,0:T(8,128)(2,1)}, u32[]{:S(2)}, u32[]{:S(2)}) async-start(bf16[256,128,128]{2,1,0:T(8,128)(2,1)} %scatter_fusion), calls=%async_computation.1 | async-start | bytes 16777216 | tf_op jit(solution)/shard_map/all_to_all | solution.py:301
  47.5 0.1 copy.47
  47.6 0.3 fusion.11
  47.9 0.1 copy.48
  48.1 0.5 fusion.8
  48.5 0.1 select_reduce_fusion
  48.7 0.6 convert_element_type.66.cnt
  49.3 2.9 copy.58
  52.1 2.6 copy.59
  54.7 2.9 copy.60
  57.6 2.6 copy.61
  60.2 2.9 copy.62
  63.0 2.6 copy.63
  65.7 0.1 slice_reduce_fusion
  65.9 0.1 fusion.10
  66.1 0.7 fusion.7.order
  66.8 1.8 fusion.6
  68.6 3.1 fusion.4
  71.6 0.5 broadcast.450
  72.2 0.7 reduce.5
  72.9 158.2 %all-to-all-done.1 = bf16[256,128,128]{2,1,0:T(8,128)(2,1)} async-done(((bf16[256,128,128]{2,1,0:T(8,128)(2,1)}), bf16[256,128,128]{2,1,0:T(8,128)(2,1)}, u32[]{:S(2)}, u32[]{:S(2)}) %all-to-all-start.1) | async-done | bytes 8388640 | tf_op jit(solution)/shard_map/all_to_all | solution.py:301
  231.1 7.9 %fusion = bf16[12,128,128]{2,0,1:T(8,128)(2,1)S(1)} fusion(bf16[256,128,128]{2,1,0:T(8,128)(2,1)} %all-to-all-done.1, s32[256]{0:T(256)S(1)} %eq.104), kind=kOutput, calls=%fused_computation.2 | convolution fusion | flops 100666368 | bytes 8782848 | tf_op jit(solution)/shard_map/ls,stc->ltc/dot_general | solution.py:306
  239.0 0.1 copy.70
  239.2 2.5 collective-permute-start.1
  241.7 3.4 collective-permute-start
  245.1 0.7 broadcast_select_fusion.sel
  245.7 2.5 collective-permute-done.1
  248.2 4.5 %collective-permute-done = bf16[1,6,128,128]{3,2,1,0:T(8,128)(2,1)S(1)} collective-permute-done((bf16[1,6,128,128]{3,2,1,0:T(8,128)(2,1)S(1)}, bf16[1,6,128,128]{3,2,1,0:T(8,128)(2,1)S(1)}, u32[]{:S(2)}, u32[]{:S(2)}) %collective-permute-start) | collective-permute-done | bytes 196640 | tf_op jit(solution)/shard_map/ppermute | solution.py:28
  252.8 0.5 collective-permute-start.2
  253.3 0.5 and_select_fusion.13.npair
  253.8 2.2 collective-permute-done.3
  256.0 3.1 collective-permute-done.2
  259.0 1.2 pad_maximum_fusion.ext
  260.2 98.9 %shard_map.109 = bf16[2,6,128,1024]{3,2,1,0:T(8,128)(2,1)} custom-call(s32[12,10]{1,0:T(8,128)} %broadcast_select_fusion.sel, f32[12,10]{1,0:T(8,128)} %convert_element_type.66.cnt, s32[12]{0:T(128)} %and_select_fusion.13.npair, bf16[4,8,128,128]{3,2,1,0:T(8,128)(2,1)} %pad_maximum_fusion.ext, f32[4,128,128]{2,1,0:T(8,128)} %get-tuple-element.14.lat_cos, ...), custom_call_target="tpu_custom_call" | custom-call | tf_op jit(solution)/shard_map/pallas_call | solution.py:225
  (23 shorter events, 0.5 us)
Async XLA Ops:
  4.6 36.9 %all-to-all-start = ((s32[32,8,1]{1,2,0:T(1,128)}), s32[32,8,1]{1,2,0:T(1,128)S(1)}, u32[]{:S(2)}, u32[]{:S(2)}) async-start(s32[32,8,1]{1,2,0:T(1,128)} %bitcast.2), calls=%async_computation | async-start | bytes 32768 | tf_op jit(solution)/shard_map/all_to_all | solution.py:302
  41.5 5.9 %copy-start = (s32[2,6,9]{2,0,1:T(2,128)S(1)}, s32[2,6,9]{2,0,1:T(2,128)}, u32[]{:S(2)}) copy-start(s32[2,6,9]{2,0,1:T(2,128)} %param.21) | copy-start | bytes 1300
  41.5 189.6 %all-to-all-start.1 = ((bf16[256,128,128]{2,1,0:T(8,128)(2,1)}), bf16[256,128,128]{2,1,0:T(8,128)(2,1)}, u32[]{:S(2)}, u32[]{:S(2)}) async-start(bf16[256,128,128]{2,1,0:T(8,128)(2,1)} %scatter_fusion), calls=%async_computation.1 | async-start | bytes 16777216 | tf_op jit(solution)/shard_map/all_to_all | solution.py:301
  239.2 9.0 %collective-permute-start.1 = (bf16[1,6,128,128]{3,2,1,0:T(8,128)(2,1)S(1)}, bf16[1,6,128,128]{3,2,1,0:T(8,128)(2,1)S(1)}, u32[]{:S(2)}, u32[]{:S(2)}) collective-permute-start(bf16[1,6,128,128]{3,2,1,0:T(8,128)(2,1)S(1)} %get-tuple-element.10), channel_id=1, source_target_pairs={{8,0},{16,8},{24,16},{9,1},{17,9},{25,17},{10,2},{18,10},{26,18},{... | collective-permute-start | bytes 589832 | tf_op jit(solution)/shard_map/ppermute | solution.py:31
  241.7 11.0 %collective-permute-start = (bf16[1,6,128,128]{3,2,1,0:T(8,128)(2,1)S(1)}, bf16[1,6,128,128]{3,2,1,0:T(8,128)(2,1)S(1)}, u32[]{:S(2)}, u32[]{:S(2)}) collective-permute-start(bf16[1,6,128,128]{3,2,1,0:T(8,128)(2,1)S(1)} %get-tuple-element.9), channel_id=1, source_target_pairs={{0,8},{8,16},{16,24},{1,9},{9,17},{17,25},{2,10},{10,18},{18,26},{... | collective-permute-start | bytes 589832 | tf_op jit(solution)/shard_map/ppermute | solution.py:28
  252.7 3.2 collective-permute-start.3
  252.8 6.2 %collective-permute-start.2 = (bf16[4,1,128,128]{3,2,1,0:T(8,128)(2,1)S(1)}, bf16[4,1,128,128]{3,2,1,0:T(8,128)(2,1)S(1)}, u32[]{:S(2)}, u32[]{:S(2)}) collective-permute-start(bf16[4,1,128,128]{3,2,1,0:T(8,128)(2,1)S(1)} %get-tuple-element.7), channel_id=1, source_target_pairs={{0,1},{1,2},{2,3},{3,4},{4,5},{5,6},{6,7},{7,0},{8,9},{9,10},{10,1... | collective-permute-start | bytes 393224 | tf_op jit(solution)/shard_map/ppermute | solution.py:28

commit v2 on v1

--- a/solution.py
+++ b/solution.py
@@ -18,19 +18,178 @@
 PAIRS = (LISTED + 1) // 2
 
 
-def padded(block, sides, width, periodic):
-    for axis, dim in sides:
-        count = lax.axis_size(axis)
-        forward = [(i, i + 1) for i in range(count - 1)]
-        if periodic:
-            forward.append((count - 1, 0))
-        backward = [(target, source) for source, target in forward]
-        low = lax.ppermute(
-            lax.slice_in_dim(block, block.shape[dim] - width, None, axis=dim), axis, forward
-        )
-        high = lax.ppermute(lax.slice_in_dim(block, 0, width, axis=dim), axis, backward)
-        block = jnp.concatenate([low, block, high], axis=dim)
-    return block
+def whole(shape):
+    return pl.BlockSpec(shape, lambda *_: (0,) * len(shape), pipeline_mode=pl.Buffered(1))
+
+
+def exchange(value, axis, partner):
+    count = lax.axis_size(axis)
+    return lax.ppermute(value, axis, [(i, partner(i, count)) for i in range(count)])
+
+
+def added(*terms):
+    return sum(term.astype(jnp.float32) for term in terms).astype(jnp.bfloat16)
+
+
+def place_kernel(start, listing, own, got, out, held, arrived):
+    step, tile, chan = out.shape
+    items = own.shape[0]
+    first = pl.program_id(0) * step
+
+    @pl.when(first == 0)
+    def _():
+        copies = [
+            pltpu.make_async_copy(source, held.at[pl.ds(k * items, items)], arrived.at[k])
+            for k, source in enumerate((own, got))
+        ]
+        for copy in copies:
+            copy.start()
+        for copy in copies:
+            copy.wait()
+
+    def one_slot(k, _):
+        def one_item(i, total):
+            return total + held[listing[i]].astype(jnp.float32)
+
+        total = jnp.zeros((tile, chan), jnp.float32)
+        total = lax.fori_loop(start[first + k], start[first + k + 1], one_item, total)
+        out[k] = total.astype(out.dtype)
+        return 0
+
+    lax.fori_loop(0, step, one_slot, 0)
+
+
+def placed(start, listing, own, got):
+    slots = start.shape[0] - 1
+    items, tile, chan = own.shape
+    step = 16
+    return pl.pallas_call(
+        place_kernel,
+        out_shape=jax.ShapeDtypeStruct((slots, tile, chan), own.dtype),
+        grid_spec=pltpu.PrefetchScalarGridSpec(
+            num_scalar_prefetch=2,
+            grid=(slots // step,),
+            in_specs=[pl.BlockSpec(memory_space=pl.ANY)] * 2,
+            out_specs=pl.BlockSpec((step, tile, chan), lambda i, *_: (i, 0, 0)),
+            scratch_shapes=[
+                pltpu.VMEM((2 * items, tile, chan), own.dtype),
+                pltpu.SemaphoreType.DMA((2,)),
+            ],
+        ),
+        compiler_params=pltpu.CompilerParams(vmem_limit_bytes=24 * 1024 * 1024),
+        cost_estimate=pl.CostEstimate(
+            flops=0, bytes_accessed=20 * 1024 * 1024, transcendentals=0
+        ),
+    )(start, listing, own, got)
+
+
+def in_order(slot, slots):
+    items = jnp.arange(slot.shape[0])
+    before = (slot[None, :] < slot[:, None]) | (
+        (slot[None, :] == slot[:, None]) & (items[None, :] < items[:, None])
+    )
+    rank = jnp.sum(before.astype(jnp.int32), axis=1)
+    listing = jnp.sum(jnp.where(rank[None, :] == items[:, None], items[None, :], 0), axis=1)
+    start = jnp.sum((slot[None, :] < jnp.arange(slots + 1)[:, None]).astype(jnp.int32), axis=1)
+    return listing.astype(jnp.int32), start
+
+
+def along_ring(blocks, nz):
+    def ahead(step):
+        return lambda i, count: (i + 2 * step) % count
+
+    if nz != 4:
+        return added(blocks[0], *[exchange(blocks[k], "sector", ahead(k)) for k in range(1, nz)])
+    half = blocks[2].shape[-3] // 2
+    relay_on = exchange(blocks[2][..., :half, :, :], "sector", ahead(1))
+    relay_back = exchange(blocks[2][..., half:, :, :], "sector", ahead(-1))
+    on = jnp.concatenate(
+        [added(blocks[1][..., :half, :, :], relay_on), blocks[1][..., half:, :, :]], axis=-3
+    )
+    back = jnp.concatenate(
+        [blocks[3][..., :half, :, :], added(blocks[3][..., half:, :, :], relay_back)], axis=-3
+    )
+    return added(
+        blocks[0], exchange(on, "sector", ahead(1)), exchange(back, "sector", ahead(-1))
+    )
+
+
+def other_core(i, count):
+    return i ^ 1
+
+
+def other_x(i, count):
+    return i ^ 1
+
+
+def other_y(i, count):
+    return i ^ 2
+
+
+def reduced_rows(parts, dest, local, trows, tcols, beside):
+    nb = lax.axis_size("band")
+    ns = lax.axis_size("sector")
+    nz = ns // 2
+    tile, chan = parts.shape[1:]
+    band_at = lax.axis_index("band")
+    sect_at = lax.axis_index("sector")
+    code = jnp.stack([dest, local])
+    code = jnp.concatenate([code, exchange(code, "sector", other_core)], axis=1)
+    dest, local = code[0], code[1]
+    far_band = (dest // ns) ^ band_at
+    far_z = jnp.mod(dest % ns // 2 - sect_at // 2, nz)
+    row, col = local // tcols, local % tcols
+    z_first = trows // 2
+    place = jnp.where(row < z_first, far_z * nb + far_band, far_band * nz + far_z)
+    count = nb * nz * tcols
+    slot = (row * nb * nz + place) * tcols + col
+    slot = jnp.where(dest % 2 == sect_at % 2, slot, trows * count).astype(jnp.int32)
+    listing, start = in_order(slot, trows * count)
+    got = exchange(parts, "sector", other_core)
+    rows = []
+    for r in range(trows):
+        dense = placed(start[r * count : (r + 1) * count + 1], listing, parts, got)
+        if r < z_first:
+            dense = dense.reshape(nz, nb, tcols, tile, chan)
+            mine = along_ring([dense[k] for k in range(nz)], nz)
+            mine = added(
+                mine[0],
+                exchange(mine[1], "band", other_x),
+                exchange(mine[2], "band", other_y),
+                exchange(mine[3], "band", lambda i, count: i ^ 3),
+            )
+        else:
+            dense = dense.reshape(nb, nz, tcols, tile, chan)
+            half = tcols // 2
+            mine = []
+            for cols, first, second, order in (
+                (slice(0, half), other_x, other_y, (1, 3, 0, 2)),
+                (slice(half, tcols), other_y, other_x, (2, 3, 0, 1)),
+            ):
+                far = jnp.stack([dense[b, :, cols] for b in order[:2]])
+                come = exchange(far, "band", first)
+                sums = [added(dense[b, :, cols], come[k]) for k, b in enumerate(order[2:])]
+                mine.append((sums[0], exchange(sums[1], "band", second)))
+            mine, beside = lax.optimization_barrier((mine, beside))
+            blocks = [
+                jnp.concatenate([added(a[k], b[k]) for a, b in mine], axis=0) for k in range(nz)
+            ]
+            mine = along_ring(blocks, nz)
+        rows.append(mine)
+    return rows, beside
+
+
+def window_rows(rows):
+    wide = []
+    for row in rows:
+        left = exchange(row[-1:], "sector", lambda i, count: (i + 1) % count)
+        right = exchange(row[:1], "sector", lambda i, count: (i - 1) % count)
+        wide.append(jnp.concatenate([left, row, right], axis=0))
+    count = lax.axis_size("band")
+    forward = [(i, i + 1) for i in range(count - 1)]
+    above = lax.ppermute(wide[-1], "band", forward)
+    below = lax.ppermute(wide[0], "band", [(b, a) for a, b in forward])
+    return jnp.stack([above, *wide, below])
 
 
 def rotary_tables(ext_rows, ext_cols, nrows, ncols, tile):
@@ -119,7 +278,8 @@
             full = jnp.dot(normed[...], wk_pairs[g], preferred_element_type=f32)
             for c in range(ecols):
                 keys[r * ecols + c, g] = turn(full[c * tile : (c + 1) * tile], c).astype(bf16)
-            full = jnp.dot(normed[...], w_value[g], preferred_element_type=f32)
+            cols = pl.ds(pl.multiple_of(g * GW, GW), GW)
+            full = jnp.dot(normed[...], w_value[:, cols], preferred_element_type=f32)
             for c in range(ecols):
                 values[r * ecols + c, g] = full[c * tile : (c + 1) * tile].astype(bf16)
             if own:
@@ -138,8 +298,11 @@
     @pl.when(row == 0)
     def _():
         for g in range(NGROUP):
-            wq_pairs[g] = jnp.dot(w_query[g], order[...], preferred_element_type=f32).astype(bf16)
-            wk_pairs[g] = jnp.dot(w_key[g], order[...], preferred_element_type=f32).astype(bf16)
+            cols = slice(g * GW, (g + 1) * GW)
+            turned = jnp.dot(w_query[:, cols], order[...], preferred_element_type=f32)
+            wq_pairs[g] = turned.astype(bf16)
+            turned = jnp.dot(w_key[:, cols], order[...], preferred_element_type=f32)
+            wk_pairs[g] = turned.astype(bf16)
         project_row(0, False)
 
         def own_row(r, _):
@@ -159,45 +322,38 @@
         def with_pairs(count):
             def one_group(g, _):
                 query = queries[t, g]
-                stacked = jnp.concatenate(
-                    [jnp.where(pair_head == h, query, jnp.zeros_like(query)) for h in range(GROUP)],
-                    axis=0,
-                )
-                scores = []
-                for j in range(count):
-                    near = jnp.concatenate(
-                        [keys[sel[t, 2 * j], g], keys[sel[t, 2 * j + 1], g]], axis=0
+                near = jnp.concatenate([keys[sel[t, j], g] for j in range(2 * count)], axis=0)
+                held = jnp.concatenate([values[sel[t, j], g] for j in range(2 * count)], axis=0)
+                pieces = []
+                for first in range(0, GROUP, 2):
+                    stacked = jnp.concatenate(
+                        [
+                            jnp.where(pair_head == h, query, jnp.zeros_like(query))
+                            for h in range(first, first + 2)
+                        ],
+                        axis=0,
                     )
-                    scores.append(
-                        lax.dot_general(
-                            stacked, near, (((1,), (1,)), ((), ())), preferred_element_type=f32
-                        )
+                    scores = lax.dot_general(
+                        stacked, near, (((1,), (1,)), ((), ())), preferred_element_type=f32
                     )
-                top = functools.reduce(jnp.maximum, scores)
-                top = jnp.max(top, axis=1, keepdims=True)
-                total = jnp.zeros((GROUP * tile, tile), f32)
-                mixed = jnp.zeros((GROUP * tile, GW), f32)
-                for j in range(count):
-                    probs = jnp.exp2(scores[j] - top)
-                    first = probs[:, :tile] * cnt[t, 2 * j]
-                    second = probs[:, tile:] * cnt[t, 2 * j + 1]
-                    total = total + (first + second)
-                    near = jnp.concatenate(
-                        [values[sel[t, 2 * j], g], values[sel[t, 2 * j + 1], g]], axis=0
+                    top = jnp.max(scores, axis=1, keepdims=True)
+                    probs = jnp.exp2(scores - top)
+                    probs = [
+                        probs[:, j * tile : (j + 1) * tile] * cnt[t, j] for j in range(2 * count)
+                    ]
+                    total = jnp.sum(sum(probs), axis=1, keepdims=True)
+                    mixed = jnp.dot(
+                        jnp.concatenate(probs, axis=1).astype(bf16), held, preferred_element_type=f32
                     )
-                    mixed = mixed + jnp.dot(
-                        jnp.concatenate([first, second], axis=1).astype(bf16),
-                        near,
-                        preferred_element_type=f32,
-                    )
-                mixed = mixed / jnp.sum(total, axis=1, keepdims=True)
+                    pieces.append(mixed * (1.0 / total))
+                mixed = jnp.concatenate(pieces, axis=0)
                 result = mixed[:tile]
                 for h in range(1, GROUP):
                     result = jnp.where(value_head == h, mixed[h * tile : (h + 1) * tile], result)
                 attended[g, pl.ds(pl.multiple_of(c * tile, tile), tile), :] = result.astype(bf16)
                 return 0
 
-            lax.fori_loop(0, NGROUP, one_group, 0)
+            lax.fori_loop(0, NGROUP, one_group, 0, unroll=4)
 
         for count in range(1, PAIRS + 1):
             pl.when(npair[t] == count)(functools.partial(with_pairs, count))
@@ -210,10 +366,6 @@
         result = jnp.dot(together, w_out[...], preferred_element_type=f32)
         result = result + embedded[row, c : c + 2].reshape(2 * tile, width)
         out[0, c : c + 2] = result.astype(bf16).reshape(2, tile, width)
-
-
-def whole(shape):
-    return pl.BlockSpec(shape, lambda *_: (0,) * len(shape), pipeline_mode=pl.Buffered(1))
 
 
 def window(sel, cnt, npair, operands, trows, tcols):
@@ -260,10 +412,6 @@
     return sel.astype(jnp.int32), cnt, npair.astype(jnp.int32)
 
 
-def by_group(weight):
-    return jnp.swapaxes(weight.reshape(weight.shape[0], NGROUP, GW), 0, 1)
-
-
 def body(
     grid_cells,
     remap_weight,
@@ -279,48 +427,32 @@
 ):
     nband = lax.axis_size("band")
     nsect = lax.axis_size("sector")
-    ndev = nband * nsect
     blocks, top, rowcells, tile = remap_weight.shape
     chan = grid_cells.shape[2]
     trows, tcols = (neighbours.shape[0], neighbours.shape[1])
-    cap = max(2, 2 * blocks * top // ndev)
     items = blocks * top
     parts = jnp.einsum(
         "rkct,rcf->rktf", remap_weight, grid_cells, preferred_element_type=jnp.float32
     )
     parts = parts.astype(jnp.bfloat16).reshape(items, tile, chan)
-    dest = remap_dest.reshape(-1)
-    local = remap_tile.reshape(-1)
-    order = jnp.arange(items)
-    earlier = (dest[:, None] == dest[None, :]) & (order[None, :] < order[:, None])
-    rank = jnp.sum(earlier.astype(jnp.int32), axis=1)
-    slot = dest * cap + rank
-    send_parts = jnp.zeros((ndev * cap, tile, chan), jnp.bfloat16).at[slot].set(parts)
-    send_ids = jnp.full((ndev * cap,), -1, jnp.int32).at[slot].set(local)
-    got_parts, got_ids = (
-        lax.all_to_all(send_parts, ("band", "sector"), split_axis=0, concat_axis=0, tiled=True),
-        lax.all_to_all(send_ids, ("band", "sector"), split_axis=0, concat_axis=0, tiled=True),
-    )
     owned = trows * tcols
-    select = (got_ids[None, :] == jnp.arange(owned)[:, None]).astype(jnp.bfloat16)
-    remapped = jnp.einsum(
-        "ls,stc->ltc", select, got_parts, preferred_element_type=jnp.float32
-    ).astype(jnp.bfloat16)
     band_at = lax.axis_index("band")
     sect_at = lax.axis_index("sector")
     nrows = trows * nband
     ncols = tcols * nsect
-    ext = padded(remapped.reshape(trows, tcols, tile, chan), (("band", 0),), 1, False)
-    ext = padded(ext, (("sector", 1),), 1, True)
     ext_rows = band_at * trows - 1 + jnp.arange(trows + 2)
     ext_cols = jnp.mod(sect_at * tcols - 1 + jnp.arange(tcols + 2), ncols)
     tables = rotary_tables(ext_rows, ext_cols, nrows, ncols, tile)
     local_row = neighbours // ncols - band_at * trows + 1
     local_col = jnp.mod(neighbours % ncols - sect_at * tcols + 1, ncols)
     index = (local_row * (tcols + 2) + local_col).reshape(owned, LISTED)
-    sel, cnt, npair = distinct_tiles(index)
+    beside = (tables, distinct_tiles(index), pair_order())
+    dest, local = remap_dest.reshape(-1), remap_tile.reshape(-1)
+    rows, beside = reduced_rows(parts, dest, local, trows, tcols, beside)
+    tables, (sel, cnt, npair), order = beside
+    ext = window_rows(rows)
     operands = (ext, *tables, norm_gain.reshape(1, -1), w_embed)
-    operands += (by_group(w_query), by_group(w_key), by_group(w_value), w_out, pair_order())
+    operands += (w_query, w_key, w_value, w_out, order)
     return window(sel, cnt, npair, operands, trows, tcols)
 
 

time: 362 us -> 189 us (0.52)
  waiting for transfers between devices: 170 us -> 50.4 us
  local copies, waits for them, and re-layouts: 45.8 us -> 1.4 us
  starting transfers between devices: 18.4 us -> 34.9 us
  Pallas kernels: 98.9 us -> 82.5 us
  matrix products: 14 us -> 6.13 us
    all_to_all x2 -> x0, waiting for transfers between devices: 158 us -> none  [the longest x1 158 us: body(): lax.all_to_all(send_parts, ('band', 'sector'), split_axis=0, concat_axis=...]
    ppermute x4 -> x23, waiting for transfers between devices: 12.2 us -> 50.4 us  [the longest x21 42.6 us: exchange(): lax.ppermute(value, axis, [(i, partner(i, count)) for i in range(count)])]
    pallas_call x1, Pallas kernels: 98.9 us -> 70.1 us  [window(): pl.pallas_call(window_kernel, out_shape=jax.ShapeDtypeStruct((trows, tcol...]
    ppermute x4 -> x23, starting transfers between devices: 6.4 us -> 34.9 us  [the longest x21 29 us: exchange(): lax.ppermute(value, axis, [(i, partner(i, count)) for i in range(count)])]
    scatter x2 -> x0, local copies, waits for them, and re-layouts: 20.3 us -> none  [the longest x1 19.4 us: body(): jnp.zeros((ndev * cap, tile, chan), jnp.bfloat16).at[slot].set(parts)]
    pallas_call x0 -> x2, Pallas kernels: none -> 12.4 us  [placed(): pl.pallas_call(place_kernel, out_shape=jax.ShapeDtypeStruct((slots, tile,...]
    all_to_all x2 -> x0, starting transfers between devices: 12 us -> none  [the longest x1 6.1 us: body(): lax.all_to_all(send_ids, ('band', 'sector'), split_axis=0, concat_axis=0,...]
    unnamed x7 -> x8, local copies, waits for them, and re-layouts: 10.1 us -> 0.2 us
  transfers between devices with their start and end apart: 6 -> 23, of which waited for: 5 -> 11; matrix products, arithmetic and copies ran while one was open for 16% -> 6% of each run, Pallas kernels for 0% -> 0%
where the time goes in v2:
time: 189 us; the launch traced here: 188 us
  Pallas kernels  82.5 us (44%)
  waiting for transfers between devices  50.4 us (27%)
  starting transfers between devices  34.9 us (18%)
  other arithmetic  12.2 us (6%)
  matrix products  6.13 us (3%)
    pallas_call x1, Pallas kernels, window(): pl.pallas_call(window_kernel, out_shape=jax.ShapeDtypeStruct((trows, tcol...  70.1 us
    ppermute x21, waiting for transfers between devices, exchange(): lax.ppermute(value, axis, [(i, partner(i, count)) for i in range(count)])  42.6 us
    ppermute x21, starting transfers between devices, exchange(): lax.ppermute(value, axis, [(i, partner(i, count)) for i in range(count)])  29 us
    pallas_call x2, Pallas kernels, placed(): pl.pallas_call(place_kernel, out_shape=jax.ShapeDtypeStruct((slots, tile,...  12.4 us
    dot_general x1, matrix products, body(): jnp.einsum('rkct,rcf->rktf', remap_weight, grid_cells, preferred_element_...  6.13 us
    ppermute x1, waiting for transfers between devices, window_rows(): above = lax.ppermute(wide[-1], 'band', forward)  5.09 us
  transfers between devices with their start and end apart: 23, of which 11 were waited for; matrix products, arithmetic and copies ran while one was open for 6% of the time, Pallas kernels for 0%

profile of v2, /device:TPU:4, one launch (start us, length us, event | category | flops | bytes accessed | tf_op | source)
XLA Modules:
  0.0 187.9 jit_solution(2004047442267592482)
XLA Ops:
  0.0 6.1 %convolution_convert_fusion = bf16[64,2,128,128]{3,2,1,0:T(8,128)(2,1)} fusion(bf16[64,2,128,128]{3,2,1,0:T(8,128)(2,1)} %param.12, bf16[64,128,128]{2,1,0:T(8,128)(2,1)} %param.11), kind=kOutput, calls=%fused_computation | convolution fusion | flops 538968064 | bytes 10485760 | tf_op jit(solution)/shard_map/rkct,rcf->rktf/dot_general | solution.py:434
  6.2 0.1 stack_reshape.6
  6.6 0.6 collective-permute-start
  7.4 0.3 fusion.30
  8.1 0.5 fusion.27
  8.6 0.1 select_reduce_fusion.1
  8.9 0.7 broadcast_select_fusion.sel
  9.6 0.7 fusion.16.order
  10.3 1.8 fusion.13
  12.1 0.9 collective-permute-done
  13.2 0.2 convert_reduce_fusion
  13.6 6.2 %shard_map.109 = bf16[96,128,128]{2,1,0:T(8,128)(2,1)S(1)} custom-call(s32[97]{0:T(128)S(1)} %get-tuple-element.73.start, s32[256]{0:T(256)S(1)} %select_reduce_fusion.listing, bf16[128,128,128]{2,1,0:T(8,128)(2,1)} %bitcast.6.own, bf16[128,128,128]{2,1,0:T(8,128)(2,1)} %collective-permute-done.1.got), custom_call_target="tpu_custom_call" | custom-call | bytes 20971520 | tf_op jit(solution)/shard_map/pallas_call | solution.py:66
  19.9 6.2 %shard_map.110 = bf16[96,128,128]{2,1,0:T(8,128)(2,1)S(1)} custom-call(s32[97]{0:T(128)S(1)} %get-tuple-element.72.start, s32[256]{0:T(256)S(1)} %select_reduce_fusion.listing, bf16[128,128,128]{2,1,0:T(8,128)(2,1)} %bitcast.6.own, bf16[128,128,128]{2,1,0:T(8,128)(2,1)} %collective-permute-done.1.got), custom_call_target="tpu_custom_call" | custom-call | bytes 20971520 | tf_op jit(solution)/shard_map/pallas_call | solution.py:66
  26.1 0.2 fusion.53
  26.4 1.7 collective-permute-start.13
  28.3 1.5 collective-permute-start.2
  29.8 0.5 collective-permute-start.4
  30.3 2.2 %collective-permute-start.15 = (bf16[4,3,128,128]{3,2,1,0:T(8,128)(2,1)S(1)}, bf16[4,3,128,128]{3,2,1,0:T(8,128)(2,1)S(1)}, u32[]{:S(2)}, u32[]{:S(2)}) collective-permute-start(bf16[4,3,128,128]{3,2,1,0:T(8,128)(2,1)S(1)} %get-tuple-element.55), channel_id=1, source_target_pairs={{0,6},{1,7},{2,0},{3,1},{4,2},{5,3},{6,4},{7,5},{8,14},{9,15},{10,... | collective-permute-start | bytes 1179656 | tf_op jit(solution)/shard_map/ppermute | solution.py:27
  32.6 7.7 %collective-permute-done.13 = bf16[4,3,128,128]{3,2,1,0:T(8,128)(2,1)S(1)} collective-permute-done((bf16[4,3,128,128]{3,2,1,0:T(8,128)(2,1)S(1)}, bf16[4,3,128,128]{3,2,1,0:T(8,128)(2,1)S(1)}, u32[]{:S(2)}, u32[]{:S(2)}) %collective-permute-start.13) | collective-permute-done | bytes 393248 | tf_op jit(solution)/shard_map/ppermute | solution.py:27
  40.6 8.1 %collective-permute-done.15 = bf16[4,3,128,128]{3,2,1,0:T(8,128)(2,1)S(1)} collective-permute-done((bf16[4,3,128,128]{3,2,1,0:T(8,128)(2,1)S(1)}, bf16[4,3,128,128]{3,2,1,0:T(8,128)(2,1)S(1)}, u32[]{:S(2)}, u32[]{:S(2)}) %collective-permute-start.15) | collective-permute-done | bytes 393248 | tf_op jit(solution)/shard_map/ppermute | solution.py:27
  48.9 1.8 collective-permute-start.16
  50.6 0.5 fusion.8
  51.1 0.6 collective-permute-start.3
  51.7 1.5 collective-permute-start.5
  53.2 0.6 and_select_fusion.16.npair
  53.8 0.6 convert_element_type.340.cnt
  54.4 3.0 %fusion.4 = (f32[8,128,128]{2,1,0:T(8,128)}, f32[8,128,128]{2,1,0:T(8,128)}) fusion(f32[128]{0:T(128)S(1)} %add_convert_fusion.15, f32[8,128]{1,0:T(8,128)S(1)} %add_multiply_fusion, pred[128]{0:T(512)(128)(4,1)S(1)} %fusion.48), kind=kLoop, calls=%fused_computation.18 | loop fusion | flops 393216 | bytes 1053312 | tf_op jit(solution)/shard_map/jit(_where)/select_n | solution.py:210
  57.4 3.0 %collective-permute-done.3 = bf16[4,3,128,128]{3,2,1,0:T(8,128)(2,1)S(1)} collective-permute-done((bf16[4,3,128,128]{3,2,1,0:T(8,128)(2,1)S(1)}, bf16[4,3,128,128]{3,2,1,0:T(8,128)(2,1)S(1)}, u32[]{:S(2)}, u32[]{:S(2)}) %collective-permute-start.3) | collective-permute-done | bytes 393248 | tf_op jit(solution)/shard_map/ppermute | solution.py:27
  60.6 1.8 collective-permute-start.6
  62.4 2.2 %collective-permute-start.8 = (bf16[3,128,128]{2,1,0:T(8,128)(2,1)S(1)}, bf16[3,128,128]{2,1,0:T(8,128)(2,1)S(1)}, u32[]{:S(2)}, u32[]{:S(2)}) collective-permute-start(bf16[3,128,128]{2,1,0:T(8,128)(2,1)S(1)} %get-tuple-element.49), channel_id=1, source_target_pairs={{0,6},{1,7},{2,0},{3,1},{4,2},{5,3},{6,4},{7,5},{8,14},{9,15},{10,... | collective-permute-start | bytes 294920 | tf_op jit(solution)/shard_map/ppermute | solution.py:27
  64.6 2.9 %collective-permute-done.14 = bf16[4,6,128,128]{3,2,1,0:T(8,128)(2,1)S(1)} collective-permute-done((bf16[4,6,128,128]{3,2,1,0:T(8,128)(2,1)S(1)}, bf16[4,6,128,128]{3,2,1,0:T(8,128)(2,1)S(1)}, u32[]{:S(2)}, u32[]{:S(2)}) %collective-permute-start.14) | collective-permute-done | bytes 786464 | tf_op jit(solution)/shard_map/ppermute | solution.py:27
  67.5 15.3 %collective-permute-done.16 = bf16[4,6,128,128]{3,2,1,0:T(8,128)(2,1)S(1)} collective-permute-done((bf16[4,6,128,128]{3,2,1,0:T(8,128)(2,1)S(1)}, bf16[4,6,128,128]{3,2,1,0:T(8,128)(2,1)S(1)}, u32[]{:S(2)}, u32[]{:S(2)}) %collective-permute-start.16) | collective-permute-done | bytes 786464 | tf_op jit(solution)/shard_map/ppermute | solution.py:27
  82.7 0.4 fusion.2
  83.2 1.6 collective-permute-start.17
  84.8 0.5 collective-permute-start.18
  85.3 1.4 collective-permute-start.19
  86.8 0.6 collective-permute-start.7
  87.5 3.3 %collective-permute-start.9 = (bf16[6,128,128]{2,1,0:T(8,128)(2,1)S(1)}, bf16[6,128,128]{2,1,0:T(8,128)(2,1)S(1)}, u32[]{:S(2)}, u32[]{:S(2)}) collective-permute-start(bf16[6,128,128]{2,1,0:T(8,128)(2,1)S(1)} %pad_maximum_fusion.7), channel_id=1, source_target_pairs={{0,6},{1,7},{2,0},{3,1},{4,2},{5,3},{6,4},{7,5},{8,14},{9,15},{10,... | collective-permute-start | bytes 589832 | tf_op jit(solution)/shard_map/ppermute | solution.py:27
  90.8 0.2 collective-permute-done.17
  91.0 4.4 %collective-permute-done.18 = bf16[6,128,128]{2,1,0:T(8,128)(2,1)S(1)} collective-permute-done((bf16[6,128,128]{2,1,0:T(8,128)(2,1)S(1)}, bf16[6,128,128]{2,1,0:T(8,128)(2,1)S(1)}, u32[]{:S(2)}, u32[]{:S(2)}) %collective-permute-start.18) | collective-permute-done | bytes 196640 | tf_op jit(solution)/shard_map/ppermute | solution.py:27
  95.6 3.5 %collective-permute-start.21 = (bf16[1,128,128]{2,1,0:T(8,128)(2,1)S(1)}, bf16[1,128,128]{2,1,0:T(8,128)(2,1)S(1)}, u32[]{:S(2)}, u32[]{:S(2)}) collective-permute-start(bf16[1,128,128]{2,1,0:T(8,128)(2,1)S(1)} %get-tuple-element.63), channel_id=1, source_target_pairs={{0,7},{1,0},{2,1},{3,2},{4,3},{5,4},{6,5},{7,6},{8,15},{9,8},{10,9... | collective-permute-start | bytes 98312 | tf_op jit(solution)/shard_map/ppermute | solution.py:27
  99.3 3.5 %collective-permute-start.11 = (bf16[1,128,128]{2,1,0:T(8,128)(2,1)S(1)}, bf16[1,128,128]{2,1,0:T(8,128)(2,1)S(1)}, u32[]{:S(2)}, u32[]{:S(2)}) collective-permute-start(bf16[1,128,128]{2,1,0:T(8,128)(2,1)S(1)} %get-tuple-element.61), channel_id=1, source_target_pairs={{0,7},{1,0},{2,1},{3,2},{4,3},{5,4},{6,5},{7,6},{8,15},{9,8},{10,9... | collective-permute-start | bytes 98312 | tf_op jit(solution)/shard_map/ppermute | solution.py:27
  102.9 3.1 %collective-permute-start.22 = (bf16[8,128,128]{2,1,0:T(8,128)(2,1)S(1)}, bf16[8,128,128]{2,1,0:T(8,128)(2,1)S(1)}, u32[]{:S(2)}, u32[]{:S(2)}) collective-permute-start(bf16[8,128,128]{2,1,0:T(8,128)(2,1)S(1)} %get-tuple-element.59), channel_id=1, source_target_pairs={{8,0},{16,8},{24,16},{9,1},{17,9},{25,17},{10,2},{18,10},{26,18},{... | collective-permute-start | bytes 786440 | tf_op jit(solution)/shard_map/ppermute | solution.py:191
  106.1 2.8 %collective-permute-start.12 = (bf16[8,128,128]{2,1,0:T(8,128)(2,1)S(1)}, bf16[8,128,128]{2,1,0:T(8,128)(2,1)S(1)}, u32[]{:S(2)}, u32[]{:S(2)}) collective-permute-start(bf16[8,128,128]{2,1,0:T(8,128)(2,1)S(1)} %get-tuple-element.56), channel_id=1, source_target_pairs={{0,8},{8,16},{16,24},{1,9},{9,17},{17,25},{2,10},{10,18},{18,26},{... | collective-permute-start | bytes 786440 | tf_op jit(solution)/shard_map/ppermute | solution.py:190
  108.9 2.7 %collective-permute-done.22 = bf16[8,128,128]{2,1,0:T(8,128)(2,1)S(1)} collective-permute-done((bf16[8,128,128]{2,1,0:T(8,128)(2,1)S(1)}, bf16[8,128,128]{2,1,0:T(8,128)(2,1)S(1)}, u32[]{:S(2)}, u32[]{:S(2)}) %collective-permute-start.22) | collective-permute-done | bytes 262176 | tf_op jit(solution)/shard_map/ppermute | solution.py:191
  111.6 5.1 %collective-permute-done.12 = bf16[8,128,128]{2,1,0:T(8,128)(2,1)S(1)} collective-permute-done((bf16[8,128,128]{2,1,0:T(8,128)(2,1)S(1)}, bf16[8,128,128]{2,1,0:T(8,128)(2,1)S(1)}, u32[]{:S(2)}, u32[]{:S(2)}) %collective-permute-start.12) | collective-permute-done | bytes 262176 | tf_op jit(solution)/shard_map/ppermute | solution.py:190
  116.6 1.1 pad_maximum_fusion.ext
  117.7 70.1 %shard_map.111 = bf16[2,6,128,1024]{3,2,1,0:T(8,128)(2,1)} custom-call(s32[12,10]{1,0:T(8,128)} %broadcast_select_fusion.sel, f32[12,10]{1,0:T(8,128)} %convert_element_type.340.cnt, s32[12]{0:T(128)} %and_select_fusion.16.npair, bf16[4,8,128,128]{3,2,1,0:T(8,128)(2,1)} %pad_maximum_fusion.ext, f32[4,128,128]{2,1,0:T(8,128)} %get-tuple-element.24.lat_cos, ...), custom_call_target="tpu_custom_call" | custom-call | tf_op jit(solution)/shard_map/pallas_call | solution.py:377
  (76 shorter events, 3.1 us)
Async XLA Ops:
  0.0 6.1 %copy-start.1 = (s32[64,2]{0,1:T(2,128)S(1)}, s32[64,2]{0,1:T(2,128)}, u32[]{:S(2)}) copy-start(s32[64,2]{0,1:T(2,128)} %param.13) | copy-start | bytes 1540
  0.0 6.4 %copy-start.2 = (s32[64,2]{0,1:T(2,128)S(1)}, s32[64,2]{0,1:T(2,128)}, u32[]{:S(2)}) copy-start(s32[64,2]{0,1:T(2,128)} %param.14) | copy-start | bytes 1540
  0.0 7.2 %copy-start = (s32[2,6,9]{2,0,1:T(2,128)S(1)}, s32[2,6,9]{2,0,1:T(2,128)}, u32[]{:S(2)}) copy-start(s32[2,6,9]{2,0,1:T(2,128)} %param.21) | copy-start | bytes 1300
  6.1 7.5 %collective-permute-start.1 = (bf16[128,128,128]{2,1,0:T(8,128)(2,1)}, bf16[128,128,128]{2,1,0:T(8,128)(2,1)}, u32[]{:S(2)}, u32[]{:S(2)}) collective-permute-start(bf16[128,128,128]{2,1,0:T(8,128)(2,1)} %bitcast.6.own), channel_id=1, source_target_pairs={{0,1},{1,0},{2,3},{3,2},{4,5},{5,4},{6,7},{7,6},{8,9},{9,8},{10,11... | collective-permute-start | bytes 12582920 | tf_op jit(solution)/shard_map/ppermute | solution.py:27
  6.6 6.4 %collective-permute-start = (s32[2,128]{1,0:T(2,128)S(1)}, s32[2,128]{1,0:T(2,128)S(1)}, u32[]{:S(2)}, u32[]{:S(2)}) collective-permute-start(s32[2,128]{1,0:T(2,128)S(1)} %pad_add_fusion.1), channel_id=1, source_target_pairs={{0,1},{1,0},{2,3},{3,2},{4,5},{5,4},{6,7},{7,6},{8,9},{9,8},{10,11... | collective-permute-start | bytes 3080 | tf_op jit(solution)/shard_map/ppermute | solution.py:27
  26.4 13.9 %collective-permute-start.13 = (bf16[4,3,128,128]{3,2,1,0:T(8,128)(2,1)S(1)}, bf16[4,3,128,128]{3,2,1,0:T(8,128)(2,1)S(1)}, u32[]{:S(2)}, u32[]{:S(2)}) collective-permute-start(bf16[4,3,128,128]{3,2,1,0:T(8,128)(2,1)S(1)} %get-tuple-element.54), channel_id=1, source_target_pairs={{0,2},{1,3},{2,4},{3,5},{4,6},{5,7},{6,0},{7,1},{8,10},{9,11},{10,... | collective-permute-start | bytes 1179656 | tf_op jit(solution)/shard_map/ppermute | solution.py:27
  28.3 22.4 %collective-permute-start.2 = (bf16[2,4,3,128,128]{4,3,2,1,0:T(8,128)(2,1)S(1)}, bf16[2,4,3,128,128]{4,3,2,1,0:T(8,128)(2,1)S(1)}, u32[]{:S(2)}, u32[]{:S(2)}) collective-permute-start(bf16[2,4,3,128,128]{4,3,2,1,0:T(8,128)(2,1)S(1)} %pad_maximum_fusion.1), channel_id=1, source_target_pairs={{0,8},{8,0},{16,24},{24,16},{1,9},{9,1},{17,25},{25,17},{2,10},{10... | collective-permute-start | bytes 2359304 | tf_op jit(solution)/shard_map/ppermute | solution.py:27
  29.8 20.8 %collective-permute-start.4 = (bf16[2,4,3,128,128]{4,3,2,1,0:T(8,128)(2,1)S(1)}, bf16[2,4,3,128,128]{4,3,2,1,0:T(8,128)(2,1)S(1)}, u32[]{:S(2)}, u32[]{:S(2)}) collective-permute-start(bf16[2,4,3,128,128]{4,3,2,1,0:T(8,128)(2,1)S(1)} %stack.32), channel_id=1, source_target_pairs={{0,16},{8,24},{16,0},{24,8},{1,17},{9,25},{17,1},{25,9},{2,18},{10... | collective-permute-start | bytes 2359304 | tf_op jit(solution)/shard_map/ppermute | solution.py:27
  30.3 18.4 %collective-permute-start.15 = (bf16[4,3,128,128]{3,2,1,0:T(8,128)(2,1)S(1)}, bf16[4,3,128,128]{3,2,1,0:T(8,128)(2,1)S(1)}, u32[]{:S(2)}, u32[]{:S(2)}) collective-permute-start(bf16[4,3,128,128]{3,2,1,0:T(8,128)(2,1)S(1)} %get-tuple-element.55), channel_id=1, source_target_pairs={{0,6},{1,7},{2,0},{3,1},{4,2},{5,3},{6,4},{7,5},{8,14},{9,15},{10,... | collective-permute-start | bytes 1179656 | tf_op jit(solution)/shard_map/ppermute | solution.py:27
  40.5 26.9 %collective-permute-start.14 = (bf16[4,6,128,128]{3,2,1,0:T(8,128)(2,1)S(1)}, bf16[4,6,128,128]{3,2,1,0:T(8,128)(2,1)S(1)}, u32[]{:S(2)}, u32[]{:S(2)}) collective-permute-start(bf16[4,6,128,128]{3,2,1,0:T(8,128)(2,1)S(1)} %pad_maximum_fusion.2), channel_id=1, source_target_pairs={{0,2},{1,3},{2,4},{3,5},{4,6},{5,7},{6,0},{7,1},{8,10},{9,11},{10,... | collective-permute-start | bytes 2359304 | tf_op jit(solution)/shard_map/ppermute | solution.py:27
  48.9 33.9 %collective-permute-start.16 = (bf16[4,6,128,128]{3,2,1,0:T(8,128)(2,1)S(1)}, bf16[4,6,128,128]{3,2,1,0:T(8,128)(2,1)S(1)}, u32[]{:S(2)}, u32[]{:S(2)}) collective-permute-start(bf16[4,6,128,128]{3,2,1,0:T(8,128)(2,1)S(1)} %pad_maximum_fusion.3), channel_id=1, source_target_pairs={{0,6},{1,7},{2,0},{3,1},{4,2},{5,3},{6,4},{7,5},{8,14},{9,15},{10,... | collective-permute-start | bytes 2359304 | tf_op jit(solution)/shard_map/ppermute | solution.py:27
  51.1 9.3 %collective-permute-start.3 = (bf16[4,3,128,128]{3,2,1,0:T(8,128)(2,1)S(1)}, bf16[4,3,128,128]{3,2,1,0:T(8,128)(2,1)S(1)}, u32[]{:S(2)}, u32[]{:S(2)}) collective-permute-start(bf16[4,3,128,128]{3,2,1,0:T(8,128)(2,1)S(1)} %get-tuple-element.42), channel_id=1, source_target_pairs={{0,16},{8,24},{16,0},{24,8},{1,17},{9,25},{17,1},{25,9},{2,18},{10... | collective-permute-start | bytes 1179656 | tf_op jit(solution)/shard_map/ppermute | solution.py:27
  51.7 8.8 %collective-permute-start.5 = (bf16[4,3,128,128]{3,2,1,0:T(8,128)(2,1)S(1)}, bf16[4,3,128,128]{3,2,1,0:T(8,128)(2,1)S(1)}, u32[]{:S(2)}, u32[]{:S(2)}) collective-permute-start(bf16[4,3,128,128]{3,2,1,0:T(8,128)(2,1)S(1)} %get-tuple-element.33), channel_id=1, source_target_pairs={{0,8},{8,0},{16,24},{24,16},{1,9},{9,1},{17,25},{25,17},{2,10},{10... | collective-permute-start | bytes 1179656 | tf_op jit(solution)/shard_map/ppermute | solution.py:27
  60.6 26.2 %collective-permute-start.6 = (bf16[3,128,128]{2,1,0:T(8,128)(2,1)S(1)}, bf16[3,128,128]{2,1,0:T(8,128)(2,1)S(1)}, u32[]{:S(2)}, u32[]{:S(2)}) collective-permute-start(bf16[3,128,128]{2,1,0:T(8,128)(2,1)S(1)} %get-tuple-element.47), channel_id=1, source_target_pairs={{0,2},{1,3},{2,4},{3,5},{4,6},{5,7},{6,0},{7,1},{8,10},{9,11},{10,... | collective-permute-start | bytes 294920 | tf_op jit(solution)/shard_map/ppermute | solution.py:27
  62.4 25.0 %collective-permute-start.8 = (bf16[3,128,128]{2,1,0:T(8,128)(2,1)S(1)}, bf16[3,128,128]{2,1,0:T(8,128)(2,1)S(1)}, u32[]{:S(2)}, u32[]{:S(2)}) collective-permute-start(bf16[3,128,128]{2,1,0:T(8,128)(2,1)S(1)} %get-tuple-element.49), channel_id=1, source_target_pairs={{0,6},{1,7},{2,0},{3,1},{4,2},{5,3},{6,4},{7,5},{8,14},{9,15},{10,... | collective-permute-start | bytes 294920 | tf_op jit(solution)/shard_map/ppermute | solution.py:27
  83.2 7.8 %collective-permute-start.17 = (bf16[6,128,128]{2,1,0:T(8,128)(2,1)S(1)}, bf16[6,128,128]{2,1,0:T(8,128)(2,1)S(1)}, u32[]{:S(2)}, u32[]{:S(2)}) collective-permute-start(bf16[6,128,128]{2,1,0:T(8,128)(2,1)S(1)} %get-tuple-element.51), channel_id=1, source_target_pairs={{0,8},{8,0},{16,24},{24,16},{1,9},{9,1},{17,25},{25,17},{2,10},{10... | collective-permute-start | bytes 589832 | tf_op jit(solution)/shard_map/ppermute | solution.py:27
  84.8 10.6 %collective-permute-start.18 = (bf16[6,128,128]{2,1,0:T(8,128)(2,1)S(1)}, bf16[6,128,128]{2,1,0:T(8,128)(2,1)S(1)}, u32[]{:S(2)}, u32[]{:S(2)}) collective-permute-start(bf16[6,128,128]{2,1,0:T(8,128)(2,1)S(1)} %get-tuple-element.53), channel_id=1, source_target_pairs={{0,16},{8,24},{16,0},{24,8},{1,17},{9,25},{17,1},{25,9},{2,18},{10... | collective-permute-start | bytes 589832 | tf_op jit(solution)/shard_map/ppermute | solution.py:27
  85.3 10.2 %collective-permute-start.19 = (bf16[6,128,128]{2,1,0:T(8,128)(2,1)S(1)}, bf16[6,128,128]{2,1,0:T(8,128)(2,1)S(1)}, u32[]{:S(2)}, u32[]{:S(2)}) collective-permute-start(bf16[6,128,128]{2,1,0:T(8,128)(2,1)S(1)} %get-tuple-element.52), channel_id=1, source_target_pairs={{0,24},{8,16},{16,8},{24,0},{1,25},{9,17},{17,9},{25,1},{2,26},{10... | collective-permute-start | bytes 589832 | tf_op jit(solution)/shard_map/ppermute | solution.py:27
  86.8 12.4 %collective-permute-start.7 = (bf16[6,128,128]{2,1,0:T(8,128)(2,1)S(1)}, bf16[6,128,128]{2,1,0:T(8,128)(2,1)S(1)}, u32[]{:S(2)}, u32[]{:S(2)}) collective-permute-start(bf16[6,128,128]{2,1,0:T(8,128)(2,1)S(1)} %pad_maximum_fusion.6), channel_id=1, source_target_pairs={{0,2},{1,3},{2,4},{3,5},{4,6},{5,7},{6,0},{7,1},{8,10},{9,11},{10,... | collective-permute-start | bytes 589832 | tf_op jit(solution)/shard_map/ppermute | solution.py:27
  87.5 11.7 %collective-permute-start.9 = (bf16[6,128,128]{2,1,0:T(8,128)(2,1)S(1)}, bf16[6,128,128]{2,1,0:T(8,128)(2,1)S(1)}, u32[]{:S(2)}, u32[]{:S(2)}) collective-permute-start(bf16[6,128,128]{2,1,0:T(8,128)(2,1)S(1)} %pad_maximum_fusion.7), channel_id=1, source_target_pairs={{0,6},{1,7},{2,0},{3,1},{4,2},{5,3},{6,4},{7,5},{8,14},{9,15},{10,... | collective-permute-start | bytes 589832 | tf_op jit(solution)/shard_map/ppermute | solution.py:27
  95.6 7.3 %collective-permute-start.20 = (bf16[1,128,128]{2,1,0:T(8,128)(2,1)S(1)}, bf16[1,128,128]{2,1,0:T(8,128)(2,1)S(1)}, u32[]{:S(2)}, u32[]{:S(2)}) collective-permute-start(bf16[1,128,128]{2,1,0:T(8,128)(2,1)S(1)} %get-tuple-element.62), channel_id=1, source_target_pairs={{0,1},{1,2},{2,3},{3,4},{4,5},{5,6},{6,7},{7,0},{8,9},{9,10},{10,1... | collective-permute-start | bytes 98312 | tf_op jit(solution)/shard_map/ppermute | solution.py:27
  95.6 7.2 %collective-permute-start.21 = (bf16[1,128,128]{2,1,0:T(8,128)(2,1)S(1)}, bf16[1,128,128]{2,1,0:T(8,128)(2,1)S(1)}, u32[]{:S(2)}, u32[]{:S(2)}) collective-permute-start(bf16[1,128,128]{2,1,0:T(8,128)(2,1)S(1)} %get-tuple-element.63), channel_id=1, source_target_pairs={{0,7},{1,0},{2,1},{3,2},{4,3},{5,4},{6,5},{7,6},{8,15},{9,8},{10,9... | collective-permute-start | bytes 98312 | tf_op jit(solution)/shard_map/ppermute | solution.py:27
  99.3 6.7 %collective-permute-start.10 = (bf16[1,128,128]{2,1,0:T(8,128)(2,1)S(1)}, bf16[1,128,128]{2,1,0:T(8,128)(2,1)S(1)}, u32[]{:S(2)}, u32[]{:S(2)}) collective-permute-start(bf16[1,128,128]{2,1,0:T(8,128)(2,1)S(1)} %get-tuple-element.60), channel_id=1, source_target_pairs={{0,1},{1,2},{2,3},{3,4},{4,5},{5,6},{6,7},{7,0},{8,9},{9,10},{10,1... | collective-permute-start | bytes 98312 | tf_op jit(solution)/shard_map/ppermute | solution.py:27
  99.3 6.7 %collective-permute-start.11 = (bf16[1,128,128]{2,1,0:T(8,128)(2,1)S(1)}, bf16[1,128,128]{2,1,0:T(8,128)(2,1)S(1)}, u32[]{:S(2)}, u32[]{:S(2)}) collective-permute-start(bf16[1,128,128]{2,1,0:T(8,128)(2,1)S(1)} %get-tuple-element.61), channel_id=1, source_target_pairs={{0,7},{1,0},{2,1},{3,2},{4,3},{5,4},{6,5},{7,6},{8,15},{9,8},{10,9... | collective-permute-start | bytes 98312 | tf_op jit(solution)/shard_map/ppermute | solution.py:27
  102.9 8.6 %collective-permute-start.22 = (bf16[8,128,128]{2,1,0:T(8,128)(2,1)S(1)}, bf16[8,128,128]{2,1,0:T(8,128)(2,1)S(1)}, u32[]{:S(2)}, u32[]{:S(2)}) collective-permute-start(bf16[8,128,128]{2,1,0:T(8,128)(2,1)S(1)} %get-tuple-element.59), channel_id=1, source_target_pairs={{8,0},{16,8},{24,16},{9,1},{17,9},{25,17},{10,2},{18,10},{26,18},{... | collective-permute-start | bytes 786440 | tf_op jit(solution)/shard_map/ppermute | solution.py:191
  106.1 10.6 %collective-permute-start.12 = (bf16[8,128,128]{2,1,0:T(8,128)(2,1)S(1)}, bf16[8,128,128]{2,1,0:T(8,128)(2,1)S(1)}, u32[]{:S(2)}, u32[]{:S(2)}) collective-permute-start(bf16[8,128,128]{2,1,0:T(8,128)(2,1)S(1)} %get-tuple-element.56), channel_id=1, source_target_pairs={{0,8},{8,16},{16,24},{1,9},{9,17},{17,25},{2,10},{10,18},{18,26},{... | collective-permute-start | bytes 786440 | tf_op jit(solution)/shard_map/ppermute | solution.py:190

commit v3 on v2

v3 whole, which is shorter than its diff:
```python
import functools
import math

import jax
import jax.numpy as jnp
from jax import lax
from jax.experimental import pallas as pl
from jax.experimental.pallas import tpu as pltpu
from jax.sharding import PartitionSpec as P

HEADS = 16
HD = 64
GROUP = 4
NGROUP = HEADS // GROUP
GW = GROUP * HD
QUARTER = HD // 4
LISTED = 9
EARLY = 4
PAIRS = (LISTED + 1) // 2


def whole(shape):
    return pl.BlockSpec(shape, lambda *_: (0,) * len(shape), pipeline_mode=pl.Buffered(1))


def exchange(value, axis, partner):
    count = lax.axis_size(axis)
    return lax.ppermute(value, axis, [(i, partner(i, count)) for i in range(count)])


def added(*terms):
    return sum(term.astype(jnp.float32) for term in terms).astype(jnp.bfloat16)


def place_kernel(start, listing, *refs):
    sources, (out, held, arrived) = refs[:-3], refs[-3:]
    step, tile, chan = out.shape
    items = sources[0].shape[0]
    first = pl.program_id(0) * step

    @pl.when(first == 0)
    def _():
        copies = [
            pltpu.make_async_copy(source, held.at[pl.ds(k * items, items)], arrived.at[k])
            for k, source in enumerate(sources)
        ]
        for copy in copies:
            copy.start()
        for copy in copies:
            copy.wait()

    def one_slot(k, _):
        def one_item(i, total):
            return total + held[listing[i]].astype(jnp.float32)

        total = jnp.zeros((tile, chan), jnp.float32)
        total = lax.fori_loop(start[first + k], start[first + k + 1], one_item, total)
        out[k] = total.astype(out.dtype)
        return 0

    lax.fori_loop(0, step, one_slot, 0)


def placed(start, listing, sources):
    slots = start.shape[0] - 1
    items, tile, chan = sources[0].shape
    step = 16
    return pl.pallas_call(
        place_kernel,
        out_shape=jax.ShapeDtypeStruct((slots, tile, chan), sources[0].dtype),
        grid_spec=pltpu.PrefetchScalarGridSpec(
            num_scalar_prefetch=2,
            grid=(slots // step,),
            in_specs=[pl.BlockSpec(memory_space=pl.ANY)] * len(sources),
            out_specs=pl.BlockSpec((step, tile, chan), lambda i, *_: (i, 0, 0)),
            scratch_shapes=[
                pltpu.VMEM((len(sources) * items, tile, chan), sources[0].dtype),
                pltpu.SemaphoreType.DMA((len(sources),)),
            ],
        ),
        compiler_params=pltpu.CompilerParams(vmem_limit_bytes=24 * 1024 * 1024),
        cost_estimate=pl.CostEstimate(
            flops=0, bytes_accessed=20 * 1024 * 1024, transcendentals=0
        ),
    )(start, listing, *sources)


def in_order(slot, slots):
    items = jnp.arange(slot.shape[0])
    before = (slot[None, :] < slot[:, None]) | (
        (slot[None, :] == slot[:, None]) & (items[None, :] < items[:, None])
    )
    rank = jnp.sum(before.astype(jnp.int32), axis=1)
    listing = jnp.sum(jnp.where(rank[None, :] == items[:, None], items[None, :], 0), axis=1)
    start = jnp.sum((slot[None, :] < jnp.arange(slots + 1)[:, None]).astype(jnp.int32), axis=1)
    return listing.astype(jnp.int32), start


def along_ring(blocks, nz):
    def ahead(step):
        return lambda i, count: (i + 2 * step) % count

    if nz != 4:
        return added(blocks[0], *[exchange(blocks[k], "sector", ahead(k)) for k in range(1, nz)])
    half = blocks[2].shape[-3] // 2
    relay_on = exchange(blocks[2][..., :half, :, :], "sector", ahead(1))
    relay_back = exchange(blocks[2][..., half:, :, :], "sector", ahead(-1))
    on = jnp.concatenate(
        [added(blocks[1][..., :half, :, :], relay_on), blocks[1][..., half:, :, :]], axis=-3
    )
    back = jnp.concatenate(
        [blocks[3][..., :half, :, :], added(blocks[3][..., half:, :, :], relay_back)], axis=-3
    )
    return added(
        blocks[0], exchange(on, "sector", ahead(1)), exchange(back, "sector", ahead(-1))
    )


def other_core(i, count):
    return i ^ 1


def other_x(i, count):
    return i ^ 1


def other_y(i, count):
    return i ^ 2


def item_order(dest, local, owned):
    nb = lax.axis_size("band")
    ns = lax.axis_size("sector")
    nz = ns // 2
    band_at = lax.axis_index("band")
    sect_at = lax.axis_index("sector")
    code = jnp.stack([dest, local])
    code = jnp.concatenate([code, exchange(code, "sector", other_core)], axis=1)
    dest, local = code[0], code[1]
    far_band = (dest // ns) ^ band_at
    far_z = jnp.mod(dest % ns // 2 - sect_at // 2, nz)
    rest = owned - EARLY
    cut = nb * nz * EARLY
    z_first = (far_z * nb + far_band) * EARLY + local
    band_first = cut + (far_band * nz + far_z) * rest + local - EARLY
    slot = jnp.where(local < EARLY, z_first, band_first)
    slot = jnp.where(dest % 2 == sect_at % 2, slot, nb * nz * owned).astype(jnp.int32)
    listing, start = in_order(slot, nb * nz * owned)
    return listing, start[: cut + 1], start[cut:]


def z_then_band(dense, nz):
    mine = along_ring([dense[k] for k in range(nz)], nz)
    return added(
        mine[0],
        exchange(mine[1], "band", other_x),
        exchange(mine[2], "band", other_y),
        exchange(mine[3], "band", lambda i, count: i ^ 3),
    )


def band_then_z(dense, nz, beside):
    size = dense.shape[2]
    half = size // 2
    mine = []
    for some, first, second, order in (
        (slice(0, half), other_x, other_y, (1, 3, 0, 2)),
        (slice(half, size), other_y, other_x, (2, 3, 0, 1)),
    ):
        far = jnp.stack([dense[b, :, some] for b in order[:2]])
        come = exchange(far, "band", first)
        sums = [added(dense[b, :, some], come[k]) for k, b in enumerate(order[2:])]
        mine.append((sums[0], exchange(sums[1], "band", second)))
    mine, beside = lax.optimization_barrier((mine, beside))
    blocks = [jnp.concatenate([added(a[k], b[k]) for a, b in mine], axis=0) for k in range(nz)]
    return along_ring(blocks, nz), beside


def from_band(row, step):
    count = lax.axis_size("band")
    pairs = [(i, i + step) for i in range(count) if 0 <= i + step < count]
    return lax.ppermute(row, "band", pairs)


def rotary_tables(ext_rows, ext_cols, nrows, ncols, tile):
    place = jnp.arange(tile)
    across = (place // 16).astype(jnp.float32)
    along = (place % 16).astype(jnp.float32)
    theta = math.pi * (ext_rows[:, None].astype(jnp.float32) + (across + 0.5) * 16.0 / tile) / nrows
    phi = 2.0 * math.pi * (ext_cols[:, None].astype(jnp.float32) + (along + 0.5) / 16.0) / ncols
    lane = jnp.arange(GROUP * 2 * QUARTER)
    freq = (lane % QUARTER + 1).astype(jnp.float32)
    lon = (lane // QUARTER) % 2 == 1
    lat_angle = theta[:, :, None] * freq
    lon_angle = phi[:, :, None] * freq
    return (
        jnp.where(lon, 0.0, jnp.cos(lat_angle)),
        jnp.where(lon, 0.0, jnp.sin(lat_angle)),
        jnp.where(lon, jnp.cos(lon_angle), 0.0),
        jnp.where(lon, jnp.sin(lon_angle), 0.0),
    )


def pair_order():
    new = jnp.arange(GW)
    second = new // (GW // 2)
    rest = new % (GW // 2)
    old = rest // (2 * QUARTER) * HD + (rest // QUARTER) % 2 * 2 * QUARTER + second * QUARTER
    old = old + rest % QUARTER
    return (jnp.arange(GW)[:, None] == old[None, :]).astype(jnp.bfloat16)


def norm_row(tiles, gain, w_embed, normed):
    ecols, tile, chan = tiles.shape
    for c in range(0, ecols, 2):
        x = tiles[c : c + 2].reshape(2 * tile, chan)
        emb = jnp.dot(x, w_embed[...], preferred_element_type=jnp.float32)
        meansq = jnp.mean(emb * emb, axis=-1, keepdims=True)
        scaled = emb * lax.rsqrt(meansq + 1e-05) * gain[...]
        normed[c * tile : (c + 2) * tile, :] = scaled.astype(jnp.bfloat16)


def project_group(normed, places, tables, weights, put_key, put_value, put_query):
    wk_pairs, w_value, wq_pairs = weights
    lat_cos, lat_sin, lon_cos, lon_sin = tables
    tile = lat_cos.shape[1]
    normed = normed[: len(places) * tile, :]
    f32 = jnp.float32
    bf16 = jnp.bfloat16

    def turned(full, k):
        r, c = places[k]
        cosine = lat_cos[r] + lon_cos[c]
        sine = lat_sin[r] + lon_sin[c]
        lower = full[k * tile : (k + 1) * tile, : GW // 2]
        upper = full[k * tile : (k + 1) * tile, GW // 2 :]
        return jnp.concatenate(
            [lower * cosine - upper * sine, lower * sine + upper * cosine], axis=1
        )

    full = jnp.dot(normed, wk_pairs, preferred_element_type=f32)
    for k in range(len(places)):
        put_key(k, turned(full, k).astype(bf16))
    full = jnp.dot(normed, w_value, preferred_element_type=f32)
    for k in range(len(places)):
        put_value(k, full[k * tile : (k + 1) * tile].astype(bf16))
    if put_query is not None:
        full = jnp.dot(normed, wq_pairs, preferred_element_type=f32)
        for k in range(len(places)):
            scaled = turned(full, k) * (math.log2(math.e) / math.sqrt(HD))
            put_query(k, scaled.astype(bf16))


def pair_kernel(w_query, w_key, order, wq_pairs, wk_pairs):
    for source, pairs in ((w_query, wq_pairs), (w_key, wk_pairs)):
        turned = jnp.dot(source[...], order[...], preferred_element_type=jnp.float32)
        pairs[0] = turned.astype(jnp.bfloat16)


def in_pairs(w_query, w_key, order):
    width = w_query.shape[0]
    shape = jax.ShapeDtypeStruct((NGROUP, width, GW), jnp.bfloat16)
    cols = pl.BlockSpec((width, GW), lambda g: (0, g))
    group = pl.BlockSpec((1, width, GW), lambda g: (g, 0, 0))
    return pl.pallas_call(
        pair_kernel,
        out_shape=[shape, shape],
        grid=(NGROUP,),
        in_specs=[cols, cols, whole(order.shape)],
        out_specs=[group, group],
        cost_estimate=pl.CostEstimate(
            flops=4 * width * width * GW, bytes_accessed=16 * width * width, transcendentals=0
        ),
    )(w_query, w_key, order)


def row_kernel(*refs):
    tiles, lat_cos, lat_sin, lon_cos, lon_sin, gain, w_embed, wq_pairs, wk_pairs, w_value = refs[:10]
    keys, values, queries, normed = refs[10:]

    @pl.when(pl.program_id(0) == 0)
    def _():
        norm_row(tiles, gain, w_embed, normed)

    def put_key(k, value):
        keys[k, 0] = value

    def put_value(k, value):
        values[k, 0] = value

    def put_query(k, value):
        queries[k, 0] = value

    places = [(0, c) for c in range(tiles.shape[0])]
    weights = (wk_pairs[0], w_value[...], wq_pairs[0])
    tables = (lat_cos, lat_sin, lon_cos, lon_sin)
    project_group(normed, places, tables, weights, put_key, put_value, put_query)


def projected_row(tiles, tables, gain, w_embed, wq_pairs, wk_pairs, w_value):
    count, tile, chan = tiles.shape
    width = w_embed.shape[1]
    bf16 = jnp.bfloat16
    operands = (tiles, *tables, gain, w_embed, wq_pairs, wk_pairs, w_value)
    pairs_spec = pl.BlockSpec((1, width, GW), lambda g: (g, 0, 0))
    in_specs = [whole(x.shape) for x in operands[:-3]]
    in_specs += [pairs_spec, pairs_spec, pl.BlockSpec((width, GW), lambda g: (0, g))]
    return pl.pallas_call(
        row_kernel,
        out_shape=[jax.ShapeDtypeStruct((count, NGROUP, tile, GW), bf16)] * 3,
        grid=(NGROUP,),
        in_specs=in_specs,
        out_specs=[pl.BlockSpec((count, 1, tile, GW), lambda g: (0, g, 0, 0))] * 3,
        scratch_shapes=[pltpu.VMEM((count * tile, width), bf16)],
        compiler_params=pltpu.CompilerParams(vmem_limit_bytes=60 * 1024 * 1024),
        cost_estimate=pl.CostEstimate(
            flops=6 * count * tile * width * width, bytes_accessed=16000000, transcendentals=0
        ),
    )(*operands)


def window_kernel(sel, cnt, npair, *refs):
    above, below, sides, own, lat_cos, lat_sin, lon_cos, lon_sin, gain, w_embed = refs[:10]
    wq_pairs, wk_pairs, w_value = refs[10:13]
    fetched, refs = refs[13:17], refs[17:]
    out, keys, values, queries, normed, attended, w_out_held, sums, arrived = refs
    row = pl.program_id(0)
    trows, tcols, tile, chan = own.shape
    ecols = tcols + 2
    width = w_embed.shape[1]
    f32 = jnp.float32
    bf16 = jnp.bfloat16

    @pl.when(row == 0)
    def _():
        near = pl.ds(trows * ecols + 1, tcols)
        targets = [keys.at[near], values.at[near], queries.at[pl.ds((trows - 1) * tcols, tcols)]]
        copies = [
            pltpu.make_async_copy(source, target, arrived.at[k])
            for k, (source, target) in enumerate(zip(fetched, targets + [w_out_held]))
        ]
        for copy in copies:
            copy.start()
        beside = [(r, c) for r in range(1, trows + 1) for c in (0, ecols - 1)]
        mine = [[(r, c) for c in range(1, ecols - 1)] for r in range(1, trows)]
        for tiles, places in (
            *[(own.at[r], mine[r]) for r in range(trows - 1)],
            (sides, beside),
            (below, [(trows + 1, c) for c in range(ecols)]),
            (above, [(0, c) for c in range(ecols)]),
        ):
            norm_row(tiles, gain, w_embed, normed)

            def one_group(g, _):
                def put_key(k, value):
                    keys[places[k][0] * ecols + places[k][1], g] = value

                def put_value(k, value):
                    values[places[k][0] * ecols + places[k][1], g] = value

                def put_query(k, value):
                    queries[(places[k][0] - 1) * tcols + places[k][1] - 1, g] = value

                cols = pl.ds(pl.multiple_of(g * GW, GW), GW)
                is_own = places in mine
                weights = (wk_pairs[g], w_value[:, cols], wq_pairs[g] if is_own else None)
                tables = (lat_cos, lat_sin, lon_cos, lon_sin)
                last = put_query if is_own else None
                project_group(normed, places, tables, weights, put_key, put_value, last)
                return 0

            lax.fori_loop(0, NGROUP, one_group, 0)
        for copy in copies:
            copy.wait()

    lane = lax.broadcasted_iota(jnp.int32, (tile, GW), 1)
    pair_head = lane % (GW // 2) // (2 * QUARTER)
    first_head = lax.broadcasted_iota(jnp.int32, (tile, tile), 1) < HD
    heads_per = tile // HD

    def stacked_queries(t, g, heads):
        query = queries[t, g]
        return jnp.concatenate(
            [jnp.where(pair_head == h, query, jnp.zeros_like(query)) for h in heads], axis=0
        )

    def put(g, p, c, result):
        rows = pl.ds(pl.multiple_of(c * tile, tile), tile)
        attended[g, rows, p * tile : (p + 1) * tile] = result.astype(bf16)

    def two_heads(mixed, total):
        mixed = mixed / total
        return jnp.where(first_head, mixed[:tile], mixed[tile:])

    def one_tile(c, _):
        t = row * tcols + c

        def with_pairs(count):
            listed = [sel[t, j] for j in range(2 * count)]
            times = [cnt[t, j].astype(bf16) for j in range(2 * count)]
            spread = jnp.concatenate([jnp.full((tile, tile), n, bf16) for n in times], axis=0)
            low, high = sums[0], sums[1]
            for g in range(NGROUP):
                near = jnp.concatenate([keys[j, g] for j in listed], axis=0)
                for p in range(GROUP // heads_per):
                    heads = range(p * heads_per, (p + 1) * heads_per)
                    scores = lax.dot_general(
                        stacked_queries(t, g, heads),
                        near,
                        (((1,), (1,)), ((), ())),
                        preferred_element_type=f32,
                    )
                    lanes = slice(p * tile, (p + 1) * tile)
                    held = jnp.concatenate(
                        [values[j, g, :, lanes] * n for j, n in zip(listed, times)], axis=0
                    )
                    mixed = jnp.dot(
                        jnp.exp2(scores).astype(bf16),
                        jnp.concatenate([held, spread], axis=1),
                        preferred_element_type=f32,
                    )
                    total = mixed[:, tile:]
                    low = jnp.minimum(low, jnp.minimum(total[:tile], total[tile:]))
                    high = jnp.maximum(high, jnp.maximum(total[:tile], total[tile:]))
                    put(g, p, c, two_heads(mixed[:, :tile], total))
            sums[0], sums[1] = low, high

        for count in range(1, PAIRS + 1):
            pl.when(npair[t] == count)(functools.partial(with_pairs, count))
        return 0

    def one_tile_shifted(c, _):
        t = row * tcols + c

        def one_group(g, _):
            near = jnp.concatenate([keys[sel[t, j], g] for j in range(2 * PAIRS)], axis=0)
            for p in range(GROUP // heads_per):
                heads = range(p * heads_per, (p + 1) * heads_per)
                scores = lax.dot_general(
                    stacked_queries(t, g, heads),
                    near,
                    (((1,), (1,)), ((), ())),
                    preferred_element_type=f32,
                )
                probs = jnp.exp2(scores - jnp.max(scores, axis=1, keepdims=True))
                probs = [
                    probs[:, j * tile : (j + 1) * tile] * cnt[t, j] for j in range(2 * PAIRS)
                ]
                held = jnp.concatenate(
                    [values[sel[t, j], g, :, p * tile : (p + 1) * tile] for j in range(2 * PAIRS)],
                    axis=0,
                )
                mixed = jnp.dot(
                    jnp.concatenate(probs, axis=1).astype(bf16), held, preferred_element_type=f32
                )
                put(g, p, c, two_heads(mixed, jnp.sum(sum(probs), axis=1, keepdims=True)))
            return 0

        lax.fori_loop(0, NGROUP, one_group, 0)
        return 0

    sums[0] = jnp.ones((tile, tile), f32)
    sums[1] = jnp.ones((tile, tile), f32)
    lax.fori_loop(0, tcols, one_tile, 0)
    in_range = (jnp.min(sums[0]) >= 2.0**-80) & (jnp.max(sums[1]) <= 2.0**80)

    @pl.when(jnp.logical_not(in_range))
    def _():
        lax.fori_loop(0, tcols, one_tile_shifted, 0)

    for c in range(0, tcols, 2):
        rows = slice(c * tile, (c + 2) * tile)
        together = jnp.concatenate([attended[g, rows, :] for g in range(NGROUP)], axis=1)
        result = jnp.dot(together, w_out_held[...], preferred_element_type=f32)
        tiles = own[row, c : c + 2].reshape(2 * tile, chan)
        result = result + jnp.dot(tiles, w_embed[...], preferred_element_type=f32)
        out[0, c : c + 2] = result.astype(bf16).reshape(2, tile, width)


def window(lists, tiles, tables, gain, w_embed, pairs, w_value, w_out, last):
    trows, tcols, tile, chan = tiles[-1].shape
    ecols = tcols + 2
    width = w_embed.shape[1]
    owned = trows * tcols
    bf16 = jnp.bfloat16
    held = (*tiles, *tables, gain, w_embed, *pairs, w_value)
    fetched = (*last, w_out)
    return pl.pallas_call(
        window_kernel,
        out_shape=jax.ShapeDtypeStruct((trows, tcols, tile, width), bf16),
        grid_spec=pltpu.PrefetchScalarGridSpec(
            num_scalar_prefetch=3,
            grid=(trows,),
            in_specs=[whole(x.shape) for x in held]
            + [pl.BlockSpec(memory_space=pl.ANY)] * len(fetched),
            out_specs=pl.BlockSpec((1, tcols, tile, width), lambda r, *_: (r, 0, 0, 0)),
            scratch_shapes=[
                pltpu.VMEM(((trows + 2) * ecols, NGROUP, tile, GW), bf16),
                pltpu.VMEM(((trows + 2) * ecols, NGROUP, tile, GW), bf16),
                pltpu.VMEM((owned, NGROUP, tile, GW), bf16),
                pltpu.VMEM((ecols * tile, width), bf16),
                pltpu.VMEM((NGROUP, tcols * tile, GW), bf16),
                pltpu.VMEM(w_out.shape, bf16),
                pltpu.VMEM((2, tile, tile), jnp.float32),
                pltpu.SemaphoreType.DMA((len(fetched),)),
            ],
        ),
        compiler_params=pltpu.CompilerParams(vmem_limit_bytes=62 * 1024 * 1024),
    )(*lists, *held, *fetched)


def distinct_tiles(index):
    same = index[:, :, None] == index[:, None, :]
    times = jnp.sum(same, axis=2)
    order = jnp.arange(LISTED)
    new = ~jnp.any(same & (order[None, None, :] < order[None, :, None]), axis=2)
    place = jnp.sum(new[:, None, :] & (order[None, None, :] < order[None, :, None]), axis=2)
    slots = jnp.arange(2 * PAIRS)
    put = new[:, :, None] & (place[:, :, None] == slots[None, None, :])
    found = jnp.any(put, axis=1)
    sel = jnp.where(found, jnp.sum(jnp.where(put, index[:, :, None], 0), axis=1), index[:, :1])
    cnt = jnp.sum(jnp.where(put, times[:, :, None], 0), axis=1).astype(jnp.float32)
    npair = (jnp.sum(new, axis=1) + 1) // 2
    return sel.astype(jnp.int32), cnt, npair.astype(jnp.int32)


def body(
    grid_cells,
    remap_weight,
    remap_dest,
    remap_tile,
    w_embed,
    norm_gain,
    w_query,
    w_key,
    w_value,
    w_out,
    neighbours,
):
    nband = lax.axis_size("band")
    nsect = lax.axis_size("sector")
    blocks, top, rowcells, tile = remap_weight.shape
    chan = grid_cells.shape[2]
    trows, tcols = (neighbours.shape[0], neighbours.shape[1])
    cut = blocks // 2
    parts = []
    for low in (0, cut):
        piece = jnp.einsum(
            "rkct,rcf->rktf",
            remap_weight[low : low + cut],
            grid_cells[low : low + cut],
            preferred_element_type=jnp.float32,
        )
        parts.append(piece.astype(jnp.bfloat16).reshape(cut * top, tile, chan))
    owned = trows * tcols
    band_at = lax.axis_index("band")
    sect_at = lax.axis_index("sector")
    nrows = trows * nband
    ncols = tcols * nsect
    ext_rows = band_at * trows - 1 + jnp.arange(trows + 2)
    ext_cols = jnp.mod(sect_at * tcols - 1 + jnp.arange(tcols + 2), ncols)
    tables = rotary_tables(ext_rows, ext_cols, nrows, ncols, tile)
    local_row = neighbours // ncols - band_at * trows + 1
    local_col = jnp.mod(neighbours % ncols - sect_at * tcols + 1, ncols)
    index = (local_row * (tcols + 2) + local_col).reshape(owned, LISTED)
    dest, local = remap_dest.reshape(-1), remap_tile.reshape(-1)
    listing, first_start, later_start = item_order(dest, local, owned)
    parts += [exchange(piece, "sector", other_core) for piece in parts]
    nz = nsect // 2
    block = (tile, chan)
    gain = norm_gain.reshape(1, -1)
    beside = (tables, distinct_tiles(index), in_pairs(w_query, w_key, pair_order()))
    z_first = placed(first_start, listing, parts).reshape(nz, nband, EARLY, *block)
    ends = z_then_band(z_first, nz)
    band_first = placed(later_start, listing, parts)
    band_first = band_first.reshape(nband, nz, owned - EARLY, *block)
    later, beside = band_then_z(band_first, nz, beside)
    tables, lists, pairs = beside
    own = jnp.concatenate([ends, later], axis=0)
    own = own.reshape(trows, tcols, *block)

    left = exchange(own[:, -1:], "sector", lambda i, count: (i + 1) % count)
    right = exchange(own[:, :1], "sector", lambda i, count: (i - 1) % count)
    left, right, held_back = lax.optimization_barrier((left, right, own[-1]))
    above = from_band(jnp.concatenate([left[-1], own[-1], right[-1]], axis=0), 1)
    below = from_band(jnp.concatenate([left[0], own[0], right[0]], axis=0), -1)
    lat = (tables[0][trows : trows + 1], tables[1][trows : trows + 1])
    lon = (tables[2][1 : tcols + 1], tables[3][1 : tcols + 1])
    last = projected_row(held_back, (*lat, *lon), gain, w_embed, *pairs, w_value)
    sides = jnp.concatenate([left, right], axis=1)
    tiles = (above, below, sides.reshape(2 * trows, *block), own)
    return window(lists, tiles, tables, gain, w_embed, pairs, w_value, w_out, last)


def solution(mesh):
    return jax.shard_map(
        body,
        mesh=mesh,
        in_specs=(
            P(("band", "sector"), None, None),
            P(("band", "sector"), None, None, None),
            P(("band", "sector"), None),
            P(("band", "sector"), None),
            P(),
            P(),
            P(),
            P(),
            P(),
            P(),
            P("band", "sector", None),
        ),
        out_specs=P("band", "sector", None, None),
        check_vma=False,
    )
```

time: 189 us -> 247 us (1.31)
  Pallas kernels: 82.5 us -> 156 us
  waiting for transfers between devices: 50.4 us -> 33.1 us
  starting transfers between devices: 34.9 us -> 26.2 us
  local copies, waits for them, and re-layouts: 1.4 us -> 8.36 us
  other arithmetic: 12.2 us -> 18.2 us
    pallas_call x1, Pallas kernels: 70.1 us -> 129 us  [window(): pl.pallas_call(window_kernel, out_shape=jax.ShapeDtypeStruct((trows, tcol...]
    pallas_call x0 -> x2, Pallas kernels: none -> 15.5 us  [the longest x1 9.97 us: projected_row(): pl.pallas_call(row_kernel, out_shape=[jax.ShapeDtypeStruct((count, NGROUP...]
    ppermute x21 -> x20, starting transfers between devices: 29 us -> 19.4 us  [exchange(): lax.ppermute(value, axis, [(i, partner(i, count)) for i in range(count)])]
    ppermute x21 -> x20, waiting for transfers between devices: 42.6 us -> 33.1 us  [exchange(): lax.ppermute(value, axis, [(i, partner(i, count)) for i in range(count)])]
    ppermute x2, waiting for transfers between devices: 7.78 us -> 0.01 us  [from_band(): return lax.ppermute(row, 'band', pairs)]
    convert_element_type x10, other arithmetic: 1.53 us -> 7.55 us  [added(): sum((term.astype(jnp.float32) for term in terms)).astype(jnp.bfloat16)]
    slice x5 -> x9, local copies, waits for them, and re-layouts: 0.36 us -> 4.85 us  [the longest x2 2.1 us: body(): lat = (tables[0][trows:trows + 1], tables[1][trows:trows + 1])]
    unnamed x8 -> x24, local copies, waits for them, and re-layouts: 0.2 us -> 2.73 us
  transfers between devices with their start and end apart: 23 -> 22, of which waited for: 11 -> 10; matrix products, arithmetic and copies ran while one was open for 6% -> 11% of each run, Pallas kernels for 0% -> 9%
where the time goes in v3:
time: 247 us
  Pallas kernels  156 us (63%)
  waiting for transfers between devices  33.1 us (13%)
  starting transfers between devices  26.2 us (11%)
  other arithmetic  18.2 us (7%)
  local copies, waits for them, and re-layouts  8.36 us (3%)
  matrix products  4.83 us (2%)
    pallas_call x1, Pallas kernels, window(): pl.pallas_call(window_kernel, out_shape=jax.ShapeDtypeStruct((trows, tcol...  129 us
    ppermute x20, waiting for transfers between devices, exchange(): lax.ppermute(value, axis, [(i, partner(i, count)) for i in range(count)])  33.1 us
    ppermute x20, starting transfers between devices, exchange(): lax.ppermute(value, axis, [(i, partner(i, count)) for i in range(count)])  19.4 us
    pallas_call x2, Pallas kernels, placed(): pl.pallas_call(place_kernel, out_shape=jax.ShapeDtypeStruct((slots, tile,...  11.5 us
    pallas_call x1, Pallas kernels, projected_row(): pl.pallas_call(row_kernel, out_shape=[jax.ShapeDtypeStruct((count, NGROUP...  9.97 us
    convert_element_type x10, other arithmetic, added(): sum((term.astype(jnp.float32) for term in terms)).astype(jnp.bfloat16)  7.55 us
    ppermute x2, starting transfers between devices, from_band(): return lax.ppermute(row, 'band', pairs)  6.74 us
    pallas_call x1, Pallas kernels, in_pairs(): pl.pallas_call(pair_kernel, out_shape=[shape, shape], grid=(NGROUP,), in_...  5.53 us
  transfers between devices with their start and end apart: 22, of which 10 were waited for; matrix products, arithmetic and copies ran while one was open for 11% of the time, Pallas kernels for 9%

profile of v3, /device:TPU:4, one launch (start us, length us, event | category | flops | bytes accessed | tf_op | source)
XLA Modules:
  0.0 246.9 jit_solution(12636864039581720952)
XLA Ops:
  0.0 0.8 copy.22
  0.9 0.8 copy.23
  1.9 2.8 %convolution_convert_fusion.1 = bf16[32,2,128,128]{3,2,1,0:T(8,128)(2,1)S(1)} fusion(bf16[64,2,128,128]{3,2,1,0:T(8,128)(2,1)} %param.12, bf16[64,128,128]{2,1,0:T(8,128)(2,1)} %param.11), kind=kOutput, calls=%fused_computation.1 | convolution fusion | flops 269484032 | bytes 7340032 | tf_op jit(solution)/shard_map/rkct,rcf->rktf/dot_general | solution.py:548
  4.7 0.6 collective-permute-start.1
  5.6 2.1 convolution_convert_fusion
  9.5 0.7 broadcast_select_fusion.sel
  10.2 0.7 fusion.21.order
  10.9 1.8 fusion.13
  12.6 1.9 fusion.7
  15.2 5.0 %shard_map.111 = bf16[64,128,128]{2,1,0:T(8,128)(2,1)S(1)} custom-call(s32[65]{0:T(128)S(1)} %slice.212.start, s32[256]{0:T(256)S(1)} %select_reduce_fusion.listing, bf16[64,128,128]{2,1,0:T(8,128)(2,1)S(1)} %bitcast.76, bf16[64,128,128]{2,1,0:T(8,128)(2,1)} %bitcast.8.refs_1_, bf16[64,128,128]{2,1,0:T(8,128)(2,1)} %collective-permute-done.1.refs_2_, ...), custom_call_target="tpu_custom_call" | custom-call | bytes 20971520 | tf_op jit(solution)/shard_map/pallas_call | solution.py:68
  20.2 1.0 fusion.51
  21.3 3.8 %collective-permute-start.9 = (bf16[4,2,128,128]{3,2,1,0:T(8,128)(2,1)S(1)}, bf16[4,2,128,128]{3,2,1,0:T(8,128)(2,1)S(1)}, u32[]{:S(2)}, u32[]{:S(2)}) collective-permute-start(bf16[4,2,128,128]{3,2,1,0:T(8,128)(2,1)S(1)} %get-tuple-element.71), channel_id=1, source_target_pairs={{0,6},{1,7},{2,0},{3,1},{4,2},{5,3},{6,4},{7,5},{8,14},{9,15},{10,... | collective-permute-start | bytes 786440 | tf_op jit(solution)/shard_map/ppermute | solution.py:28
  25.1 6.5 %shard_map.109 = bf16[128,128,128]{2,1,0:T(8,128)(2,1)S(1)} custom-call(s32[129]{0:T(256)S(1)} %slice.196.start, s32[256]{0:T(256)S(1)} %select_reduce_fusion.listing, bf16[64,128,128]{2,1,0:T(8,128)(2,1)S(1)} %bitcast.77, bf16[64,128,128]{2,1,0:T(8,128)(2,1)} %bitcast.8.refs_1_, bf16[64,128,128]{2,1,0:T(8,128)(2,1)} %collective-permute-done.1.refs_2_, ...), custom_call_target="tpu_custom_call" | custom-call | bytes 20971520 | tf_op jit(solution)/shard_map/pallas_call | solution.py:68
  31.9 1.4 collective-permute-start.3
  34.0 0.8 pad_maximum_fusion.2
  34.8 3.8 %collective-permute-start.10 = (bf16[4,4,128,128]{3,2,1,0:T(8,128)(2,1)}, bf16[4,4,128,128]{3,2,1,0:T(8,128)(2,1)}, u32[]{:S(2)}, u32[]{:S(2)}) collective-permute-start(bf16[4,4,128,128]{3,2,1,0:T(8,128)(2,1)} %pad_maximum_fusion.2), channel_id=1, source_target_pairs={{0,6},{1,7},{2,0},{3,1},{4,2},{5,3},{6,4},{7,5},{8,14},{9,15},{10,... | collective-permute-start | bytes 1572872 | tf_op jit(solution)/shard_map/ppermute | solution.py:28
  38.6 6.3 %collective-permute-done.7 = bf16[4,2,128,128]{3,2,1,0:T(8,128)(2,1)S(1)} collective-permute-done((bf16[4,2,128,128]{3,2,1,0:T(8,128)(2,1)S(1)}, bf16[4,2,128,128]{3,2,1,0:T(8,128)(2,1)S(1)}, u32[]{:S(2)}, u32[]{:S(2)}) %collective-permute-start.7) | collective-permute-done | bytes 262176 | tf_op jit(solution)/shard_map/ppermute | solution.py:28
  45.0 0.9 pad_maximum_fusion.1
  46.4 10.5 %collective-permute-done.3 = bf16[2,4,4,128,128]{4,3,2,1,0:T(8,128)(2,1)S(1)} collective-permute-done((bf16[2,4,4,128,128]{4,3,2,1,0:T(8,128)(2,1)S(1)}, bf16[2,4,4,128,128]{4,3,2,1,0:T(8,128)(2,1)S(1)}, u32[]{:S(2)}, u32[]{:S(2)}) %collective-permute-start.3) | collective-permute-done | bytes 1048608 | tf_op jit(solution)/shard_map/ppermute | solution.py:28
  56.9 1.2 collective-permute-done.5
  58.1 1.6 fusion.11
  60.6 5.5 %shard_map.110 = (bf16[4,1024,256]{2,1,0:T(8,128)(2,1)}, bf16[4,1024,256]{2,1,0:T(8,128)(2,1)}) custom-call(bf16[1024,1024]{1,0:T(8,128)(2,1)} %w_query.1, bf16[1024,1024]{1,0:T(8,128)(2,1)} %w_key.1, bf16[256,256]{1,0:T(8,128)(2,1)} %fusion.21.order), custom_call_target="tpu_custom_call" | custom-call | flops 1073741824 | bytes 16777216 | tf_op jit(solution)/shard_map/pallas_call | solution.py:265
  66.1 0.6 convert_element_type.344.cnt
  66.7 1.4 fusion.1
  68.2 1.6 collective-permute-start.11
  69.8 1.6 collective-permute-start.13
  71.8 3.1 %collective-permute-done.6 = bf16[4,4,128,128]{3,2,1,0:T(8,128)(2,1)} collective-permute-done((bf16[4,4,128,128]{3,2,1,0:T(8,128)(2,1)}, bf16[4,4,128,128]{3,2,1,0:T(8,128)(2,1)}, u32[]{:S(2)}, u32[]{:S(2)}) %collective-permute-start.6) | collective-permute-done | bytes 524320 | tf_op jit(solution)/shard_map/ppermute | solution.py:28
  74.9 1.1 fusion.24
  76.4 1.1 fusion.23
  77.6 1.7 collective-permute-start.14
  79.3 3.1 %collective-permute-done.16 = bf16[4,128,128]{2,1,0:T(8,128)(2,1)S(1)} collective-permute-done((bf16[4,128,128]{2,1,0:T(8,128)(2,1)S(1)}, bf16[4,128,128]{2,1,0:T(8,128)(2,1)S(1)}, u32[]{:S(2)}, u32[]{:S(2)}) %collective-permute-start.16) | collective-permute-done | bytes 131104 | tf_op jit(solution)/shard_map/ppermute | solution.py:28
  82.4 1.0 fusion.14
  83.4 1.0 collective-permute-start.17
  84.8 1.0 fusion.15
  85.8 1.1 collective-permute-start.15
  87.0 1.5 slice.251.refs_1_
  88.5 0.6 slice.252.refs_2_
  89.1 0.8 slice.253.refs_3_
  89.9 0.8 slice.254.refs_4_
  91.2 2.8 %collective-permute-done.15 = bf16[8,128,128]{2,1,0:T(8,128)(2,1)S(1)} collective-permute-done((bf16[8,128,128]{2,1,0:T(8,128)(2,1)S(1)}, bf16[8,128,128]{2,1,0:T(8,128)(2,1)S(1)}, u32[]{:S(2)}, u32[]{:S(2)}) %collective-permute-start.15) | collective-permute-done | bytes 262176 | tf_op jit(solution)/shard_map/ppermute | solution.py:28
  94.9 1.8 collective-permute-done.19
  96.6 3.2 %collective-permute-done.18 = bf16[2,1,128,128]{3,2,1,0:T(8,128)(2,1)S(1)} collective-permute-done((bf16[2,1,128,128]{3,2,1,0:T(8,128)(2,1)S(1)}, bf16[2,1,128,128]{3,2,1,0:T(8,128)(2,1)S(1)}, u32[]{:S(2)}, u32[]{:S(2)}) %collective-permute-start.18) | collective-permute-done | bytes 65568 | tf_op jit(solution)/shard_map/ppermute | solution.py:28
  99.9 3.2 %collective-permute-start.20 = (bf16[8,128,128]{2,1,0:T(8,128)(2,1)S(1)}, bf16[8,128,128]{2,1,0:T(8,128)(2,1)S(1)}, u32[]{:S(2)}, u32[]{:S(2)}) collective-permute-start(bf16[8,128,128]{2,1,0:T(8,128)(2,1)S(1)} %pad_maximum_fusion.6), channel_id=1, source_target_pairs={{0,8},{8,16},{16,24},{1,9},{9,17},{17,25},{2,10},{10,18},{18,26},{... | collective-permute-start | bytes 786440 | tf_op jit(solution)/shard_map/ppermute | solution.py:182
  103.2 3.5 %collective-permute-start.21 = (bf16[8,128,128]{2,1,0:T(8,128)(2,1)S(1)}, bf16[8,128,128]{2,1,0:T(8,128)(2,1)S(1)}, u32[]{:S(2)}, u32[]{:S(2)}) collective-permute-start(bf16[8,128,128]{2,1,0:T(8,128)(2,1)S(1)} %pad_maximum_fusion.7), channel_id=1, source_target_pairs={{8,0},{16,8},{24,16},{9,1},{17,9},{25,17},{10,2},{18,10},{26,18},{... | collective-permute-start | bytes 786440 | tf_op jit(solution)/shard_map/ppermute | solution.py:182
  106.7 10.0 %shard_map.112 = (bf16[6,4,128,256]{3,2,1,0:T(8,128)(2,1)}, bf16[6,4,128,256]{3,2,1,0:T(8,128)(2,1)}, bf16[6,4,128,256]{3,2,1,0:T(8,128)(2,1)}) custom-call(bf16[6,128,128]{2,1,0:T(8,128)(2,1)} %copy-done.7, f32[1,128,128]{2,1,0:T(8,128)} %slice.251.refs_1_, f32[1,128,128]{2,1,0:T(8,128)} %slice.252.refs_2_, f32[6,128,128]{2,1,0:T(8,128)} %slice.253.refs_3_, ...), custom_call_target="tpu_custom_call" | custom-call | flops 4831838208 | bytes 16000000 | tf_op jit(solution)/shard_map/pallas_call | solution.py:308
  116.7 0.7 pad_maximum_fusion.8
  117.4 0.7 copy-done.8
  118.2 128.6 %shard_map.113 = bf16[2,6,128,1024]{3,2,1,0:T(8,128)(2,1)} custom-call(s32[12,10]{1,0:T(8,128)} %broadcast_select_fusion.sel, f32[12,10]{1,0:T(8,128)} %convert_element_type.344.cnt, s32[12]{0:T(128)} %and_select_fusion.14.npair, bf16[8,128,128]{2,1,0:T(8,128)(2,1)} %copy-done.8, bf16[8,128,128]{2,1,0:T(8,128)(2,1)} %copy-done.9, ...), custom_call_target="tpu_custom_call" | custom-call | tf_op jit(solution)/shard_map/pallas_call | solution.py:488
  (100 shorter events, 8.4 us)
Async XLA Ops:
  1.8 3.4 %copy-start.4 = (bf16[64,128,128]{2,1,0:T(8,128)(2,1)S(1)}, bf16[64,128,128]{2,1,0:T(8,128)(2,1)}, u32[]{:S(2)}) copy-start(bf16[64,128,128]{2,1,0:T(8,128)(2,1)} %param.11) | copy-start | bytes 6291460
  1.8 12.7 %collective-permute-start = (s32[2,128]{1,0:T(2,128)S(1)}, s32[2,128]{1,0:T(2,128)S(1)}, u32[]{:S(2)}, u32[]{:S(2)}) collective-permute-start(s32[2,128]{1,0:T(2,128)S(1)} %pad_add_fusion.1), channel_id=1, source_target_pairs={{0,1},{1,0},{2,3},{3,2},{4,5},{5,4},{6,7},{7,6},{8,9},{9,8},{10,11... | collective-permute-start | bytes 3080 | tf_op jit(solution)/shard_map/ppermute | solution.py:28
  1.9 3.7 %copy-start = (bf16[64,2,128,128]{3,2,1,0:T(8,128)(2,1)S(1)}, bf16[64,2,128,128]{3,2,1,0:T(8,128)(2,1)}, u32[]{:S(2)}) copy-start(bf16[64,2,128,128]{3,2,1,0:T(8,128)(2,1)} %param.12) | copy-start | bytes 12582916
  4.7 3.2 %copy-start.10 = (s32[2,6,9]{2,0,1:T(2,128)S(1)}, s32[2,6,9]{2,0,1:T(2,128)}, u32[]{:S(2)}) copy-start(s32[2,6,9]{2,0,1:T(2,128)} %param.21) | copy-start | bytes 1300
  4.7 10.5 %collective-permute-start.1 = (bf16[64,128,128]{2,1,0:T(8,128)(2,1)S(1)}, bf16[64,128,128]{2,1,0:T(8,128)(2,1)}, u32[]{:S(2)}, u32[]{:S(2)}) collective-permute-start(bf16[64,128,128]{2,1,0:T(8,128)(2,1)S(1)} %bitcast.75), channel_id=1, source_target_pairs={{0,1},{1,0},{2,3},{3,2},{4,5},{5,4},{6,7},{7,6},{8,9},{9,8},{10,11... | collective-permute-start | bytes 6291464 | tf_op jit(solution)/shard_map/ppermute | solution.py:28
  7.7 7.5 %collective-permute-start.2 = (bf16[64,128,128]{2,1,0:T(8,128)(2,1)}, bf16[64,128,128]{2,1,0:T(8,128)(2,1)}, u32[]{:S(2)}, u32[]{:S(2)}) collective-permute-start(bf16[64,128,128]{2,1,0:T(8,128)(2,1)} %bitcast.8.refs_1_), channel_id=1, source_target_pairs={{0,1},{1,0},{2,3},{3,2},{4,5},{5,4},{6,7},{7,6},{8,9},{9,8},{10,11... | collective-permute-start | bytes 6291464 | tf_op jit(solution)/shard_map/ppermute | solution.py:28
  12.6 75.8 %copy-start.6 = (f32[4,128,128]{2,1,0:T(8,128)}, f32[4,128,128]{2,1,0:T(8,128)S(1)}, u32[]{:S(2)}) copy-start(f32[4,128,128]{2,1,0:T(8,128)S(1)} %get-tuple-element.38.refs_5_) | copy-start | bytes 786436
  14.5 74.6 %copy-start.2 = (f32[8,128,128]{2,1,0:T(8,128)}, f32[8,128,128]{2,1,0:T(8,128)S(1)}, u32[]{:S(2)}) copy-start(f32[8,128,128]{2,1,0:T(8,128)S(1)} %get-tuple-element.39.refs_6_) | copy-start | bytes 1572868
  14.6 75.3 %copy-start.1 = (f32[8,128,128]{2,1,0:T(8,128)}, f32[8,128,128]{2,1,0:T(8,128)S(1)}, u32[]{:S(2)}) copy-start(f32[8,128,128]{2,1,0:T(8,128)S(1)} %get-tuple-element.40.refs_7_) | copy-start | bytes 1572868
  21.3 12.6 %collective-permute-start.9 = (bf16[4,2,128,128]{3,2,1,0:T(8,128)(2,1)S(1)}, bf16[4,2,128,128]{3,2,1,0:T(8,128)(2,1)S(1)}, u32[]{:S(2)}, u32[]{:S(2)}) collective-permute-start(bf16[4,2,128,128]{3,2,1,0:T(8,128)(2,1)S(1)} %get-tuple-element.71), channel_id=1, source_target_pairs={{0,6},{1,7},{2,0},{3,1},{4,2},{5,3},{6,4},{7,5},{8,14},{9,15},{10,... | collective-permute-start | bytes 786440 | tf_op jit(solution)/shard_map/ppermute | solution.py:28
  31.9 25.0 %collective-permute-start.3 = (bf16[2,4,4,128,128]{4,3,2,1,0:T(8,128)(2,1)S(1)}, bf16[2,4,4,128,128]{4,3,2,1,0:T(8,128)(2,1)S(1)}, u32[]{:S(2)}, u32[]{:S(2)}) collective-permute-start(bf16[2,4,4,128,128]{4,3,2,1,0:T(8,128)(2,1)S(1)} %pad_maximum_fusion), channel_id=1, source_target_pairs={{0,8},{8,0},{16,24},{24,16},{1,9},{9,1},{17,25},{25,17},{2,10},{10... | collective-permute-start | bytes 3145736 | tf_op jit(solution)/shard_map/ppermute | solution.py:28
  33.3 24.8 %collective-permute-start.5 = (bf16[2,4,4,128,128]{4,3,2,1,0:T(8,128)(2,1)S(1)}, bf16[2,4,4,128,128]{4,3,2,1,0:T(8,128)(2,1)S(1)}, u32[]{:S(2)}, u32[]{:S(2)}) collective-permute-start(bf16[2,4,4,128,128]{4,3,2,1,0:T(8,128)(2,1)S(1)} %stack.12), channel_id=1, source_target_pairs={{0,16},{8,24},{16,0},{24,8},{1,17},{9,25},{17,1},{25,9},{2,18},{10... | collective-permute-start | bytes 3145736 | tf_op jit(solution)/shard_map/ppermute | solution.py:28
  33.8 11.1 %collective-permute-start.7 = (bf16[4,2,128,128]{3,2,1,0:T(8,128)(2,1)S(1)}, bf16[4,2,128,128]{3,2,1,0:T(8,128)(2,1)S(1)}, u32[]{:S(2)}, u32[]{:S(2)}) collective-permute-start(bf16[4,2,128,128]{3,2,1,0:T(8,128)(2,1)S(1)} %get-tuple-element.70), channel_id=1, source_target_pairs={{0,2},{1,3},{2,4},{3,5},{4,6},{5,7},{6,0},{7,1},{8,10},{9,11},{10,... | collective-permute-start | bytes 786440 | tf_op jit(solution)/shard_map/ppermute | solution.py:28
  34.8 31.9 %collective-permute-start.10 = (bf16[4,4,128,128]{3,2,1,0:T(8,128)(2,1)}, bf16[4,4,128,128]{3,2,1,0:T(8,128)(2,1)}, u32[]{:S(2)}, u32[]{:S(2)}) collective-permute-start(bf16[4,4,128,128]{3,2,1,0:T(8,128)(2,1)} %pad_maximum_fusion.2), channel_id=1, source_target_pairs={{0,6},{1,7},{2,0},{3,1},{4,2},{5,3},{6,4},{7,5},{8,14},{9,15},{10,... | collective-permute-start | bytes 1572872 | tf_op jit(solution)/shard_map/ppermute | solution.py:28
  45.9 20.9 %collective-permute-start.8 = (bf16[4,4,128,128]{3,2,1,0:T(8,128)(2,1)}, bf16[4,4,128,128]{3,2,1,0:T(8,128)(2,1)}, u32[]{:S(2)}, u32[]{:S(2)}) collective-permute-start(bf16[4,4,128,128]{3,2,1,0:T(8,128)(2,1)} %pad_maximum_fusion.1), channel_id=1, source_target_pairs={{0,2},{1,3},{2,4},{3,5},{4,6},{5,7},{6,0},{7,1},{8,10},{9,11},{10,... | collective-permute-start | bytes 1572872 | tf_op jit(solution)/shard_map/ppermute | solution.py:28
  59.7 15.2 %collective-permute-start.6 = (bf16[4,4,128,128]{3,2,1,0:T(8,128)(2,1)}, bf16[4,4,128,128]{3,2,1,0:T(8,128)(2,1)}, u32[]{:S(2)}, u32[]{:S(2)}) collective-permute-start(bf16[4,4,128,128]{3,2,1,0:T(8,128)(2,1)} %get-tuple-element.49), channel_id=1, source_target_pairs={{0,8},{8,0},{16,24},{24,16},{1,9},{9,1},{17,25},{25,17},{2,10},{10... | collective-permute-start | bytes 1572872 | tf_op jit(solution)/shard_map/ppermute | solution.py:28
  60.3 6.5 %copy-start.5 = (bf16[16,128,128]{2,1,0:T(8,128)(2,1)S(1)}, bf16[16,128,128]{2,1,0:T(8,128)(2,1)}, u32[]{:S(2)}) copy-start(bf16[16,128,128]{2,1,0:T(8,128)(2,1)} %get-tuple-element.60) | copy-start | bytes 1572868
  60.3 14.6 %collective-permute-start.4 = (bf16[4,4,128,128]{3,2,1,0:T(8,128)(2,1)S(1)}, bf16[4,4,128,128]{3,2,1,0:T(8,128)(2,1)}, u32[]{:S(2)}, u32[]{:S(2)}) collective-permute-start(bf16[4,4,128,128]{3,2,1,0:T(8,128)(2,1)S(1)} %get-tuple-element.54), channel_id=1, source_target_pairs={{0,16},{8,24},{16,0},{24,8},{1,17},{9,25},{17,1},{25,9},{2,18},{10... | collective-permute-start | bytes 1572872 | tf_op jit(solution)/shard_map/ppermute | solution.py:28
  68.2 18.7 %collective-permute-start.11 = (bf16[4,128,128]{2,1,0:T(8,128)(2,1)S(1)}, bf16[4,128,128]{2,1,0:T(8,128)(2,1)S(1)}, u32[]{:S(2)}, u32[]{:S(2)}) collective-permute-start(bf16[4,128,128]{2,1,0:T(8,128)(2,1)S(1)} %get-tuple-element.67), channel_id=1, source_target_pairs={{0,8},{8,0},{16,24},{24,16},{1,9},{9,1},{17,25},{25,17},{2,10},{10... | collective-permute-start | bytes 393224 | tf_op jit(solution)/shard_map/ppermute | solution.py:28
  69.8 17.1 %collective-permute-start.13 = (bf16[4,128,128]{2,1,0:T(8,128)(2,1)S(1)}, bf16[4,128,128]{2,1,0:T(8,128)(2,1)S(1)}, u32[]{:S(2)}, u32[]{:S(2)}) collective-permute-start(bf16[4,128,128]{2,1,0:T(8,128)(2,1)S(1)} %get-tuple-element.68), channel_id=1, source_target_pairs={{0,24},{8,16},{16,8},{24,0},{1,25},{9,17},{17,9},{25,1},{2,26},{10... | collective-permute-start | bytes 393224 | tf_op jit(solution)/shard_map/ppermute | solution.py:28
  71.4 15.5 %collective-permute-start.12 = (bf16[4,128,128]{2,1,0:T(8,128)(2,1)S(1)}, bf16[4,128,128]{2,1,0:T(8,128)(2,1)S(1)}, u32[]{:S(2)}, u32[]{:S(2)}) collective-permute-start(bf16[4,128,128]{2,1,0:T(8,128)(2,1)S(1)} %get-tuple-element.69), channel_id=1, source_target_pairs={{0,16},{8,24},{16,0},{24,8},{1,17},{9,25},{17,1},{25,9},{2,18},{10... | collective-permute-start | bytes 393224 | tf_op jit(solution)/shard_map/ppermute | solution.py:28
  76.0 6.3 %collective-permute-start.16 = (bf16[4,128,128]{2,1,0:T(8,128)(2,1)S(1)}, bf16[4,128,128]{2,1,0:T(8,128)(2,1)S(1)}, u32[]{:S(2)}, u32[]{:S(2)}) collective-permute-start(bf16[4,128,128]{2,1,0:T(8,128)(2,1)S(1)} %get-tuple-element.65), channel_id=1, source_target_pairs={{0,6},{1,7},{2,0},{3,1},{4,2},{5,3},{6,4},{7,5},{8,14},{9,15},{10,... | collective-permute-start | bytes 393224 | tf_op jit(solution)/shard_map/ppermute | solution.py:28
  77.6 7.3 %collective-permute-start.14 = (bf16[4,128,128]{2,1,0:T(8,128)(2,1)S(1)}, bf16[4,128,128]{2,1,0:T(8,128)(2,1)S(1)}, u32[]{:S(2)}, u32[]{:S(2)}) collective-permute-start(bf16[4,128,128]{2,1,0:T(8,128)(2,1)S(1)} %get-tuple-element.63), channel_id=1, source_target_pairs={{0,2},{1,3},{2,4},{3,5},{4,6},{5,7},{6,0},{7,1},{8,10},{9,11},{10,... | collective-permute-start | bytes 393224 | tf_op jit(solution)/shard_map/ppermute | solution.py:28
  83.4 7.8 %collective-permute-start.17 = (bf16[8,128,128]{2,1,0:T(8,128)(2,1)S(1)}, bf16[8,128,128]{2,1,0:T(8,128)(2,1)S(1)}, u32[]{:S(2)}, u32[]{:S(2)}) collective-permute-start(bf16[8,128,128]{2,1,0:T(8,128)(2,1)S(1)} %pad_maximum_fusion.5), channel_id=1, source_target_pairs={{0,6},{1,7},{2,0},{3,1},{4,2},{5,3},{6,4},{7,5},{8,14},{9,15},{10,... | collective-permute-start | bytes 786440 | tf_op jit(solution)/shard_map/ppermute | solution.py:28
  85.8 8.2 %collective-permute-start.15 = (bf16[8,128,128]{2,1,0:T(8,128)(2,1)S(1)}, bf16[8,128,128]{2,1,0:T(8,128)(2,1)S(1)}, u32[]{:S(2)}, u32[]{:S(2)}) collective-permute-start(bf16[8,128,128]{2,1,0:T(8,128)(2,1)S(1)} %pad_maximum_fusion.4), channel_id=1, source_target_pairs={{0,2},{1,3},{2,4},{3,5},{4,6},{5,7},{6,0},{7,1},{8,10},{9,11},{10,... | collective-permute-start | bytes 786440 | tf_op jit(solution)/shard_map/ppermute | solution.py:28
  94.2 22.5 %copy-start.3 = (bf16[12,128,128]{2,1,0:T(8,128)(2,1)}, bf16[12,128,128]{2,1,0:T(8,128)(2,1)S(1)}, u32[]{:S(2)}) copy-start(bf16[12,128,128]{2,1,0:T(8,128)(2,1)S(1)} %pad_maximum_fusion.3) | copy-start | bytes 1179652
  94.3 2.4 collective-permute-start.19
  94.3 5.5 %collective-permute-start.18 = (bf16[2,1,128,128]{3,2,1,0:T(8,128)(2,1)S(1)}, bf16[2,1,128,128]{3,2,1,0:T(8,128)(2,1)S(1)}, u32[]{:S(2)}, u32[]{:S(2)}) collective-permute-start(bf16[2,1,128,128]{3,2,1,0:T(8,128)(2,1)S(1)} %get-tuple-element.73), channel_id=1, source_target_pairs={{0,1},{1,2},{2,3},{3,4},{4,5},{5,6},{6,7},{7,0},{8,9},{9,10},{10,1... | collective-permute-start | bytes 196616 | tf_op jit(solution)/shard_map/ppermute | solution.py:28
  94.9 11.9 %copy-start.7 = (bf16[6,128,128]{2,1,0:T(8,128)(2,1)}, bf16[6,128,128]{2,1,0:T(8,128)(2,1)S(1)}, u32[]{:S(2)}) copy-start(bf16[6,128,128]{2,1,0:T(8,128)(2,1)S(1)} %get-tuple-element.43.refs_0_) | copy-start | bytes 589828
  99.9 17.5 %collective-permute-start.20 = (bf16[8,128,128]{2,1,0:T(8,128)(2,1)S(1)}, bf16[8,128,128]{2,1,0:T(8,128)(2,1)S(1)}, u32[]{:S(2)}, u32[]{:S(2)}) collective-permute-start(bf16[8,128,128]{2,1,0:T(8,128)(2,1)S(1)} %pad_maximum_fusion.6), channel_id=1, source_target_pairs={{0,8},{8,16},{16,24},{1,9},{9,17},{17,25},{2,10},{10,18},{18,26},{... | collective-permute-start | bytes 786440 | tf_op jit(solution)/shard_map/ppermute | solution.py:182
  103.2 14.2 %collective-permute-start.21 = (bf16[8,128,128]{2,1,0:T(8,128)(2,1)S(1)}, bf16[8,128,128]{2,1,0:T(8,128)(2,1)S(1)}, u32[]{:S(2)}, u32[]{:S(2)}) collective-permute-start(bf16[8,128,128]{2,1,0:T(8,128)(2,1)S(1)} %pad_maximum_fusion.7), channel_id=1, source_target_pairs={{8,0},{16,8},{24,16},{9,1},{17,9},{25,17},{10,2},{18,10},{26,18},{... | collective-permute-start | bytes 786440 | tf_op jit(solution)/shard_map/ppermute | solution.py:182
  117.4 0.7 copy-start.8
  117.4 0.8 copy-start.9

commit v4 on v3

--- a/solution.py
+++ b/solution.py
@@ -291,7 +291,8 @@
     def put_query(k, value):
         queries[k, 0] = value
 
-    places = [(0, c) for c in range(tiles.shape[0])]
+    tcols = lon_cos.shape[0]
+    places = [(k // tcols, k % tcols) for k in range(tiles.shape[0])]
     weights = (wk_pairs[0], w_value[...], wq_pairs[0])
     tables = (lat_cos, lat_sin, lon_cos, lon_sin)
     project_group(normed, places, tables, weights, put_key, put_value, put_query)
@@ -321,8 +322,8 @@
 
 def window_kernel(sel, cnt, npair, *refs):
     above, below, sides, own, lat_cos, lat_sin, lon_cos, lon_sin, gain, w_embed = refs[:10]
-    wq_pairs, wk_pairs, w_value = refs[10:13]
-    fetched, refs = refs[13:17], refs[17:]
+    wk_pairs, w_value = refs[10:12]
+    fetched, refs = refs[12:16], refs[16:]
     out, keys, values, queries, normed, attended, w_out_held, sums, arrived = refs
     row = pl.program_id(0)
     trows, tcols, tile, chan = own.shape
@@ -333,18 +334,21 @@
 
     @pl.when(row == 0)
     def _():
-        near = pl.ds(trows * ecols + 1, tcols)
-        targets = [keys.at[near], values.at[near], queries.at[pl.ds((trows - 1) * tcols, tcols)]]
+        sources, targets = [], []
+        for r in range(trows):
+            near = pl.ds((r + 1) * ecols + 1, tcols)
+            mine = pl.ds(r * tcols, tcols)
+            sources += [x.at[mine] for x in fetched[:3]]
+            targets += [keys.at[near], values.at[near], queries.at[mine]]
+        sources.append(fetched[3])
         copies = [
             pltpu.make_async_copy(source, target, arrived.at[k])
-            for k, (source, target) in enumerate(zip(fetched, targets + [w_out_held]))
+            for k, (source, target) in enumerate(zip(sources, targets + [w_out_held]))
         ]
         for copy in copies:
             copy.start()
         beside = [(r, c) for r in range(1, trows + 1) for c in (0, ecols - 1)]
-        mine = [[(r, c) for c in range(1, ecols - 1)] for r in range(1, trows)]
         for tiles, places in (
-            *[(own.at[r], mine[r]) for r in range(trows - 1)],
             (sides, beside),
             (below, [(trows + 1, c) for c in range(ecols)]),
             (above, [(0, c) for c in range(ecols)]),
@@ -358,15 +362,10 @@
                 def put_value(k, value):
                     values[places[k][0] * ecols + places[k][1], g] = value
 
-                def put_query(k, value):
-                    queries[(places[k][0] - 1) * tcols + places[k][1] - 1, g] = value
-
                 cols = pl.ds(pl.multiple_of(g * GW, GW), GW)
-                is_own = places in mine
-                weights = (wk_pairs[g], w_value[:, cols], wq_pairs[g] if is_own else None)
+                weights = (wk_pairs[g], w_value[:, cols], None)
                 tables = (lat_cos, lat_sin, lon_cos, lon_sin)
-                last = put_query if is_own else None
-                project_group(normed, places, tables, weights, put_key, put_value, last)
+                project_group(normed, places, tables, weights, put_key, put_value, None)
                 return 0
 
             lax.fori_loop(0, NGROUP, one_group, 0)
@@ -389,8 +388,8 @@
         attended[g, rows, p * tile : (p + 1) * tile] = result.astype(bf16)
 
     def two_heads(mixed, total):
-        mixed = mixed / total
-        return jnp.where(first_head, mixed[:tile], mixed[tile:])
+        mixed = jnp.where(first_head, mixed[:tile], mixed[tile:])
+        return mixed / jnp.where(first_head, total[:tile], total[tile:])
 
     def one_tile(c, _):
         t = row * tcols + c
@@ -483,7 +482,7 @@
     width = w_embed.shape[1]
     owned = trows * tcols
     bf16 = jnp.bfloat16
-    held = (*tiles, *tables, gain, w_embed, *pairs, w_value)
+    held = (*tiles, *tables, gain, w_embed, pairs[1], w_value)
     fetched = (*last, w_out)
     return pl.pallas_call(
         window_kernel,
@@ -502,7 +501,7 @@
                 pltpu.VMEM((NGROUP, tcols * tile, GW), bf16),
                 pltpu.VMEM(w_out.shape, bf16),
                 pltpu.VMEM((2, tile, tile), jnp.float32),
-                pltpu.SemaphoreType.DMA((len(fetched),)),
+                pltpu.SemaphoreType.DMA((3 * trows + 1,)),
             ],
         ),
         compiler_params=pltpu.CompilerParams(vmem_limit_bytes=62 * 1024 * 1024),
@@ -559,7 +558,6 @@
     ncols = tcols * nsect
     ext_rows = band_at * trows - 1 + jnp.arange(trows + 2)
     ext_cols = jnp.mod(sect_at * tcols - 1 + jnp.arange(tcols + 2), ncols)
-    tables = rotary_tables(ext_rows, ext_cols, nrows, ncols, tile)
     local_row = neighbours // ncols - band_at * trows + 1
     local_col = jnp.mod(neighbours % ncols - sect_at * tcols + 1, ncols)
     index = (local_row * (tcols + 2) + local_col).reshape(owned, LISTED)
@@ -569,9 +567,10 @@
     nz = nsect // 2
     block = (tile, chan)
     gain = norm_gain.reshape(1, -1)
+    tables = rotary_tables(ext_rows, ext_cols, nrows, ncols, tile)
     beside = (tables, distinct_tiles(index), in_pairs(w_query, w_key, pair_order()))
-    z_first = placed(first_start, listing, parts).reshape(nz, nband, EARLY, *block)
-    ends = z_then_band(z_first, nz)
+    z_first = placed(first_start, listing, parts)
+    ends = z_then_band(z_first.reshape(nz, nband, EARLY, *block), nz)
     band_first = placed(later_start, listing, parts)
     band_first = band_first.reshape(nband, nz, owned - EARLY, *block)
     later, beside = band_then_z(band_first, nz, beside)
@@ -581,11 +580,12 @@
 
     left = exchange(own[:, -1:], "sector", lambda i, count: (i + 1) % count)
     right = exchange(own[:, :1], "sector", lambda i, count: (i - 1) % count)
-    left, right, held_back = lax.optimization_barrier((left, right, own[-1]))
+    left, right, held_back = lax.optimization_barrier((left, right, own))
     above = from_band(jnp.concatenate([left[-1], own[-1], right[-1]], axis=0), 1)
     below = from_band(jnp.concatenate([left[0], own[0], right[0]], axis=0), -1)
-    lat = (tables[0][trows : trows + 1], tables[1][trows : trows + 1])
+    lat = (tables[0][1 : trows + 1], tables[1][1 : trows + 1])
     lon = (tables[2][1 : tcols + 1], tables[3][1 : tcols + 1])
+    held_back = held_back.reshape(owned, *block)
     last = projected_row(held_back, (*lat, *lon), gain, w_embed, *pairs, w_value)
     sides = jnp.concatenate([left, right], axis=1)
     tiles = (above, below, sides.reshape(2 * trows, *block), own)

time: 247 us -> 247 us (level)
  starting transfers between devices: 26.2 us -> 31.1 us
  waiting for transfers between devices: 33.1 us -> 28.2 us
    pallas_call x1, Pallas kernels: 129 us -> 122 us  [window(): pl.pallas_call(window_kernel, out_shape=jax.ShapeDtypeStruct((trows, tcol...]
    pallas_call x1, Pallas kernels: 9.97 us -> 15.9 us  [projected_row(): pl.pallas_call(row_kernel, out_shape=[jax.ShapeDtypeStruct((count, NGROUP...]
    ppermute x20, starting transfers between devices: 19.4 us -> 25.1 us  [exchange(): lax.ppermute(value, axis, [(i, partner(i, count)) for i in range(count)])]
    ppermute x20, waiting for transfers between devices: 33.1 us -> 28.2 us  [exchange(): lax.ppermute(value, axis, [(i, partner(i, count)) for i in range(count)])]
  transfers between devices with their start and end apart: 22 -> 22, of which waited for: 10 -> 9; matrix products, arithmetic and copies ran while one was open for 11% -> 11% of each run, Pallas kernels for 9% -> 11%
where the time goes in v4:
time: 247 us; the launch traced here: 246 us
  Pallas kernels  155 us (63%)
  starting transfers between devices  31.1 us (13%)
  waiting for transfers between devices  28.2 us (11%)
  other arithmetic  18.3 us (7%)
  local copies, waits for them, and re-layouts  7.61 us (3%)
  matrix products  4.83 us (2%)
    pallas_call x1, Pallas kernels, window(): pl.pallas_call(window_kernel, out_shape=jax.ShapeDtypeStruct((trows, tcol...  122 us
    ppermute x20, waiting for transfers between devices, exchange(): lax.ppermute(value, axis, [(i, partner(i, count)) for i in range(count)])  28.2 us
    ppermute x20, starting transfers between devices, exchange(): lax.ppermute(value, axis, [(i, partner(i, count)) for i in range(count)])  25.1 us
    pallas_call x1, Pallas kernels, projected_row(): pl.pallas_call(row_kernel, out_shape=[jax.ShapeDtypeStruct((count, NGROUP...  15.9 us
    pallas_call x2, Pallas kernels, placed(): pl.pallas_call(place_kernel, out_shape=jax.ShapeDtypeStruct((slots, tile,...  11.4 us
    convert_element_type x10, other arithmetic, added(): sum((term.astype(jnp.float32) for term in terms)).astype(jnp.bfloat16)  7.56 us
    ppermute x2, starting transfers between devices, from_band(): return lax.ppermute(row, 'band', pairs)  6.03 us
    pallas_call x1, Pallas kernels, in_pairs(): pl.pallas_call(pair_kernel, out_shape=[shape, shape], grid=(NGROUP,), in_...  5.51 us
  transfers between devices with their start and end apart: 22, of which 9 were waited for; matrix products, arithmetic and copies ran while one was open for 11% of the time, Pallas kernels for 11%

profile of v4, /device:TPU:4, one launch (start us, length us, event | category | flops | bytes accessed | tf_op | source)
XLA Modules:
  0.0 245.9 jit_solution(17239274529385873182)
XLA Ops:
  0.0 0.8 copy.22
  0.9 0.8 copy.23
  1.9 2.8 %convolution_convert_fusion.1 = bf16[32,2,128,128]{3,2,1,0:T(8,128)(2,1)S(1)} fusion(bf16[64,2,128,128]{3,2,1,0:T(8,128)(2,1)} %param.12, bf16[64,128,128]{2,1,0:T(8,128)(2,1)} %param.11), kind=kOutput, calls=%fused_computation.1 | convolution fusion | flops 269484032 | bytes 7340032 | tf_op jit(solution)/shard_map/rkct,rcf->rktf/dot_general | solution.py:547
  5.6 2.1 convolution_convert_fusion
  10.2 0.7 fusion.21.order
  10.9 1.8 fusion.13
  12.6 1.9 fusion.7
  15.2 5.1 %shard_map.111 = bf16[64,128,128]{2,1,0:T(8,128)(2,1)S(1)} custom-call(s32[65]{0:T(128)S(1)} %slice.211.start, s32[256]{0:T(256)S(1)} %select_reduce_fusion.listing, bf16[64,128,128]{2,1,0:T(8,128)(2,1)S(1)} %bitcast.77, bf16[64,128,128]{2,1,0:T(8,128)(2,1)} %bitcast.8.refs_1_, bf16[64,128,128]{2,1,0:T(8,128)(2,1)} %collective-permute-done.1.refs_2_, ...), custom_call_target="tpu_custom_call" | custom-call | bytes 20971520 | tf_op jit(solution)/shard_map/pallas_call | solution.py:68
  20.4 1.0 fusion.51
  21.4 1.4 collective-permute-start.7
  22.9 6.3 %shard_map.109 = bf16[128,128,128]{2,1,0:T(8,128)(2,1)S(1)} custom-call(s32[129]{0:T(256)S(1)} %slice.195.start, s32[256]{0:T(256)S(1)} %select_reduce_fusion.listing, bf16[64,128,128]{2,1,0:T(8,128)(2,1)S(1)} %bitcast.78, bf16[64,128,128]{2,1,0:T(8,128)(2,1)} %bitcast.8.refs_1_, bf16[64,128,128]{2,1,0:T(8,128)(2,1)} %collective-permute-done.1.refs_2_, ...), custom_call_target="tpu_custom_call" | custom-call | bytes 20971520 | tf_op jit(solution)/shard_map/pallas_call | solution.py:68
  29.4 2.0 collective-permute-start.3
  31.7 2.3 collective-permute-start.9
  34.2 0.9 pad_maximum_fusion.1
  35.0 5.8 %collective-permute-done.9 = bf16[4,2,128,128]{3,2,1,0:T(8,128)(2,1)S(1)} collective-permute-done((bf16[4,2,128,128]{3,2,1,0:T(8,128)(2,1)S(1)}, bf16[4,2,128,128]{3,2,1,0:T(8,128)(2,1)S(1)}, u32[]{:S(2)}, u32[]{:S(2)}) %collective-permute-start.9) | collective-permute-done | bytes 262176 | tf_op jit(solution)/shard_map/ppermute | solution.py:28
  40.9 0.8 pad_maximum_fusion.2
  41.8 4.3 %collective-permute-start.10 = (bf16[4,4,128,128]{3,2,1,0:T(8,128)(2,1)}, bf16[4,4,128,128]{3,2,1,0:T(8,128)(2,1)}, u32[]{:S(2)}, u32[]{:S(2)}) collective-permute-start(bf16[4,4,128,128]{3,2,1,0:T(8,128)(2,1)} %pad_maximum_fusion.2), channel_id=1, source_target_pairs={{0,6},{1,7},{2,0},{3,1},{4,2},{5,3},{6,4},{7,5},{8,14},{9,15},{10,... | collective-permute-start | bytes 1572872 | tf_op jit(solution)/shard_map/ppermute | solution.py:28
  46.6 8.1 %collective-permute-done.3 = bf16[2,4,4,128,128]{4,3,2,1,0:T(8,128)(2,1)S(1)} collective-permute-done((bf16[2,4,4,128,128]{4,3,2,1,0:T(8,128)(2,1)S(1)}, bf16[2,4,4,128,128]{4,3,2,1,0:T(8,128)(2,1)S(1)}, u32[]{:S(2)}, u32[]{:S(2)}) %collective-permute-start.3) | collective-permute-done | bytes 1048608 | tf_op jit(solution)/shard_map/ppermute | solution.py:28
  54.8 1.3 collective-permute-done.5
  56.0 1.6 fusion.11
  58.6 5.5 %shard_map.110 = (bf16[4,1024,256]{2,1,0:T(8,128)(2,1)}, bf16[4,1024,256]{2,1,0:T(8,128)(2,1)}) custom-call(bf16[1024,1024]{1,0:T(8,128)(2,1)} %w_query.1, bf16[1024,1024]{1,0:T(8,128)(2,1)} %w_key.1, bf16[256,256]{1,0:T(8,128)(2,1)} %fusion.21.order), custom_call_target="tpu_custom_call" | custom-call | flops 1073741824 | bytes 16777216 | tf_op jit(solution)/shard_map/pallas_call | solution.py:265
  64.7 1.4 fusion.1
  66.2 1.6 collective-permute-start.11
  67.8 1.5 collective-permute-start.12
  69.7 2.4 collective-permute-done.4
  72.1 1.0 collective-permute-done.6
  73.1 1.1 fusion.23
  74.3 1.7 collective-permute-start.14
  76.0 1.1 fusion.24
  77.1 2.2 collective-permute-start.16
  79.3 2.0 collective-permute-done.14
  81.3 1.0 fusion.15
  82.3 1.1 collective-permute-start.15
  83.4 3.3 %collective-permute-done.16 = bf16[4,128,128]{2,1,0:T(8,128)(2,1)S(1)} collective-permute-done((bf16[4,128,128]{2,1,0:T(8,128)(2,1)S(1)}, bf16[4,128,128]{2,1,0:T(8,128)(2,1)S(1)}, u32[]{:S(2)}, u32[]{:S(2)}) %collective-permute-start.16) | collective-permute-done | bytes 131104 | tf_op jit(solution)/shard_map/ppermute | solution.py:28
  86.7 1.0 fusion.14
  87.7 1.0 collective-permute-start.17
  88.8 0.8 slice.252.refs_3_
  89.6 0.8 slice.253.refs_4_
  91.0 0.7 slice.251.refs_2_
  91.7 2.4 collective-permute-done.17
  94.4 3.5 %collective-permute-start.19 = (bf16[2,1,128,128]{3,2,1,0:T(8,128)(2,1)S(1)}, bf16[2,1,128,128]{3,2,1,0:T(8,128)(2,1)S(1)}, u32[]{:S(2)}, u32[]{:S(2)}) collective-permute-start(bf16[2,1,128,128]{3,2,1,0:T(8,128)(2,1)S(1)} %get-tuple-element.72), channel_id=1, source_target_pairs={{0,7},{1,0},{2,1},{3,2},{4,3},{5,4},{6,5},{7,6},{8,15},{9,8},{10,9... | collective-permute-start | bytes 196616 | tf_op jit(solution)/shard_map/ppermute | solution.py:28
  97.9 1.9 collective-permute-done.18
  99.9 3.4 %collective-permute-start.21 = (bf16[8,128,128]{2,1,0:T(8,128)(2,1)S(1)}, bf16[8,128,128]{2,1,0:T(8,128)(2,1)S(1)}, u32[]{:S(2)}, u32[]{:S(2)}) collective-permute-start(bf16[8,128,128]{2,1,0:T(8,128)(2,1)S(1)} %pad_maximum_fusion.7), channel_id=1, source_target_pairs={{8,0},{16,8},{24,16},{9,1},{17,9},{25,17},{10,2},{18,10},{26,18},{... | collective-permute-start | bytes 786440 | tf_op jit(solution)/shard_map/ppermute | solution.py:182
  103.4 2.6 %collective-permute-start.20 = (bf16[8,128,128]{2,1,0:T(8,128)(2,1)S(1)}, bf16[8,128,128]{2,1,0:T(8,128)(2,1)S(1)}, u32[]{:S(2)}, u32[]{:S(2)}) collective-permute-start(bf16[8,128,128]{2,1,0:T(8,128)(2,1)S(1)} %pad_maximum_fusion.6), channel_id=1, source_target_pairs={{0,8},{8,16},{16,24},{1,9},{9,17},{17,25},{2,10},{10,18},{18,26},{... | collective-permute-start | bytes 786440 | tf_op jit(solution)/shard_map/ppermute | solution.py:182
  106.0 15.9 %shard_map.112 = (bf16[12,4,128,256]{3,2,1,0:T(8,128)(2,1)}, bf16[12,4,128,256]{3,2,1,0:T(8,128)(2,1)}, bf16[12,4,128,256]{3,2,1,0:T(8,128)(2,1)}) custom-call(bf16[12,128,128]{2,1,0:T(8,128)(2,1)} %copy-done.3, f32[2,128,128]{2,1,0:T(8,128)} %slice.250.refs_1_, f32[2,128,128]{2,1,0:T(8,128)} %slice.251.refs_2_, f32[6,128,128]{2,1,0:T(8,128)} %slice.252.refs_3_, ...), custom_call_target="tpu_custom_call" | custom-call | flops 9663676416 | bytes 16000000 | tf_op jit(solution)/shard_map/pallas_call | solution.py:309
  121.9 0.7 pad_maximum_fusion.8
  122.6 0.7 copy-done.8
  123.4 122.4 %shard_map.113 = bf16[2,6,128,1024]{3,2,1,0:T(8,128)(2,1)} custom-call(s32[12,10]{1,0:T(8,128)} %broadcast_select_fusion.sel, f32[12,10]{1,0:T(8,128)} %convert_element_type.344.cnt, s32[12]{0:T(128)} %and_select_fusion.14.npair, bf16[8,128,128]{2,1,0:T(8,128)(2,1)} %copy-done.9, bf16[8,128,128]{2,1,0:T(8,128)(2,1)} %copy-done.8, ...), custom_call_target="tpu_custom_call" | custom-call | tf_op jit(solution)/shard_map/pallas_call | solution.py:487
  (100 shorter events, 8.9 us)
Async XLA Ops:
  1.8 3.4 %copy-start.4 = (bf16[64,128,128]{2,1,0:T(8,128)(2,1)S(1)}, bf16[64,128,128]{2,1,0:T(8,128)(2,1)}, u32[]{:S(2)}) copy-start(bf16[64,128,128]{2,1,0:T(8,128)(2,1)} %param.11) | copy-start | bytes 6291460
  1.8 12.7 %collective-permute-start = (s32[2,128]{1,0:T(2,128)S(1)}, s32[2,128]{1,0:T(2,128)S(1)}, u32[]{:S(2)}, u32[]{:S(2)}) collective-permute-start(s32[2,128]{1,0:T(2,128)S(1)} %pad_add_fusion.1), channel_id=1, source_target_pairs={{0,1},{1,0},{2,3},{3,2},{4,5},{5,4},{6,7},{7,6},{8,9},{9,8},{10,11... | collective-permute-start | bytes 3080 | tf_op jit(solution)/shard_map/ppermute | solution.py:28
  1.9 3.7 %copy-start = (bf16[64,2,128,128]{3,2,1,0:T(8,128)(2,1)S(1)}, bf16[64,2,128,128]{3,2,1,0:T(8,128)(2,1)}, u32[]{:S(2)}) copy-start(bf16[64,2,128,128]{3,2,1,0:T(8,128)(2,1)} %param.12) | copy-start | bytes 12582916
  4.7 3.1 %copy-start.10 = (s32[2,6,9]{2,0,1:T(2,128)S(1)}, s32[2,6,9]{2,0,1:T(2,128)}, u32[]{:S(2)}) copy-start(s32[2,6,9]{2,0,1:T(2,128)} %param.21) | copy-start | bytes 1300
  4.7 10.5 %collective-permute-start.1 = (bf16[64,128,128]{2,1,0:T(8,128)(2,1)S(1)}, bf16[64,128,128]{2,1,0:T(8,128)(2,1)}, u32[]{:S(2)}, u32[]{:S(2)}) collective-permute-start(bf16[64,128,128]{2,1,0:T(8,128)(2,1)S(1)} %bitcast.76), channel_id=1, source_target_pairs={{0,1},{1,0},{2,3},{3,2},{4,5},{5,4},{6,7},{7,6},{8,9},{9,8},{10,11... | collective-permute-start | bytes 6291464 | tf_op jit(solution)/shard_map/ppermute | solution.py:28
  7.7 7.5 %collective-permute-start.2 = (bf16[64,128,128]{2,1,0:T(8,128)(2,1)}, bf16[64,128,128]{2,1,0:T(8,128)(2,1)}, u32[]{:S(2)}, u32[]{:S(2)}) collective-permute-start(bf16[64,128,128]{2,1,0:T(8,128)(2,1)} %bitcast.8.refs_1_), channel_id=1, source_target_pairs={{0,1},{1,0},{2,3},{3,2},{4,5},{5,4},{6,7},{7,6},{8,9},{9,8},{10,11... | collective-permute-start | bytes 6291464 | tf_op jit(solution)/shard_map/ppermute | solution.py:28
  12.6 78.4 %copy-start.6 = (f32[4,128,128]{2,1,0:T(8,128)}, f32[4,128,128]{2,1,0:T(8,128)S(1)}, u32[]{:S(2)}) copy-start(f32[4,128,128]{2,1,0:T(8,128)S(1)} %get-tuple-element.38.refs_5_) | copy-start | bytes 786436
  14.5 74.2 %copy-start.2 = (f32[8,128,128]{2,1,0:T(8,128)}, f32[8,128,128]{2,1,0:T(8,128)S(1)}, u32[]{:S(2)}) copy-start(f32[8,128,128]{2,1,0:T(8,128)S(1)} %get-tuple-element.39.refs_6_) | copy-start | bytes 1572868
  14.6 75.0 %copy-start.1 = (f32[8,128,128]{2,1,0:T(8,128)}, f32[8,128,128]{2,1,0:T(8,128)S(1)}, u32[]{:S(2)}) copy-start(f32[8,128,128]{2,1,0:T(8,128)S(1)} %get-tuple-element.40.refs_7_) | copy-start | bytes 1572868
  21.4 12.6 %collective-permute-start.7 = (bf16[4,2,128,128]{3,2,1,0:T(8,128)(2,1)S(1)}, bf16[4,2,128,128]{3,2,1,0:T(8,128)(2,1)S(1)}, u32[]{:S(2)}, u32[]{:S(2)}) collective-permute-start(bf16[4,2,128,128]{3,2,1,0:T(8,128)(2,1)S(1)} %get-tuple-element.70), channel_id=1, source_target_pairs={{0,2},{1,3},{2,4},{3,5},{4,6},{5,7},{6,0},{7,1},{8,10},{9,11},{10,... | collective-permute-start | bytes 786440 | tf_op jit(solution)/shard_map/ppermute | solution.py:28
  29.4 25.4 %collective-permute-start.3 = (bf16[2,4,4,128,128]{4,3,2,1,0:T(8,128)(2,1)S(1)}, bf16[2,4,4,128,128]{4,3,2,1,0:T(8,128)(2,1)S(1)}, u32[]{:S(2)}, u32[]{:S(2)}) collective-permute-start(bf16[2,4,4,128,128]{4,3,2,1,0:T(8,128)(2,1)S(1)} %pad_maximum_fusion), channel_id=1, source_target_pairs={{0,8},{8,0},{16,24},{24,16},{1,9},{9,1},{17,25},{25,17},{2,10},{10... | collective-permute-start | bytes 3145736 | tf_op jit(solution)/shard_map/ppermute | solution.py:28
  31.4 24.6 %collective-permute-start.5 = (bf16[2,4,4,128,128]{4,3,2,1,0:T(8,128)(2,1)S(1)}, bf16[2,4,4,128,128]{4,3,2,1,0:T(8,128)(2,1)S(1)}, u32[]{:S(2)}, u32[]{:S(2)}) collective-permute-start(bf16[2,4,4,128,128]{4,3,2,1,0:T(8,128)(2,1)S(1)} %stack.12), channel_id=1, source_target_pairs={{0,16},{8,24},{16,0},{24,8},{1,17},{9,25},{17,1},{25,9},{2,18},{10... | collective-permute-start | bytes 3145736 | tf_op jit(solution)/shard_map/ppermute | solution.py:28
  31.7 9.1 %collective-permute-start.9 = (bf16[4,2,128,128]{3,2,1,0:T(8,128)(2,1)S(1)}, bf16[4,2,128,128]{3,2,1,0:T(8,128)(2,1)S(1)}, u32[]{:S(2)}, u32[]{:S(2)}) collective-permute-start(bf16[4,2,128,128]{3,2,1,0:T(8,128)(2,1)S(1)} %get-tuple-element.71), channel_id=1, source_target_pairs={{0,6},{1,7},{2,0},{3,1},{4,2},{5,3},{6,4},{7,5},{8,14},{9,15},{10,... | collective-permute-start | bytes 786440 | tf_op jit(solution)/shard_map/ppermute | solution.py:28
  35.0 29.7 %collective-permute-start.8 = (bf16[4,4,128,128]{3,2,1,0:T(8,128)(2,1)}, bf16[4,4,128,128]{3,2,1,0:T(8,128)(2,1)}, u32[]{:S(2)}, u32[]{:S(2)}) collective-permute-start(bf16[4,4,128,128]{3,2,1,0:T(8,128)(2,1)} %pad_maximum_fusion.1), channel_id=1, source_target_pairs={{0,2},{1,3},{2,4},{3,5},{4,6},{5,7},{6,0},{7,1},{8,10},{9,11},{10,... | collective-permute-start | bytes 1572872 | tf_op jit(solution)/shard_map/ppermute | solution.py:28
  41.8 22.9 %collective-permute-start.10 = (bf16[4,4,128,128]{3,2,1,0:T(8,128)(2,1)}, bf16[4,4,128,128]{3,2,1,0:T(8,128)(2,1)}, u32[]{:S(2)}, u32[]{:S(2)}) collective-permute-start(bf16[4,4,128,128]{3,2,1,0:T(8,128)(2,1)} %pad_maximum_fusion.2), channel_id=1, source_target_pairs={{0,6},{1,7},{2,0},{3,1},{4,2},{5,3},{6,4},{7,5},{8,14},{9,15},{10,... | collective-permute-start | bytes 1572872 | tf_op jit(solution)/shard_map/ppermute | solution.py:28
  57.6 14.5 %collective-permute-start.4 = (bf16[4,4,128,128]{3,2,1,0:T(8,128)(2,1)}, bf16[4,4,128,128]{3,2,1,0:T(8,128)(2,1)}, u32[]{:S(2)}, u32[]{:S(2)}) collective-permute-start(bf16[4,4,128,128]{3,2,1,0:T(8,128)(2,1)} %get-tuple-element.54), channel_id=1, source_target_pairs={{0,16},{8,24},{16,0},{24,8},{1,17},{9,25},{17,1},{25,9},{2,18},{10... | collective-permute-start | bytes 1572872 | tf_op jit(solution)/shard_map/ppermute | solution.py:28
  58.2 6.6 %copy-start.5 = (bf16[16,128,128]{2,1,0:T(8,128)(2,1)S(1)}, bf16[16,128,128]{2,1,0:T(8,128)(2,1)}, u32[]{:S(2)}) copy-start(bf16[16,128,128]{2,1,0:T(8,128)(2,1)} %get-tuple-element.60) | copy-start | bytes 1572868
  58.2 15.0 %collective-permute-start.6 = (bf16[4,4,128,128]{3,2,1,0:T(8,128)(2,1)S(1)}, bf16[4,4,128,128]{3,2,1,0:T(8,128)(2,1)}, u32[]{:S(2)}, u32[]{:S(2)}) collective-permute-start(bf16[4,4,128,128]{3,2,1,0:T(8,128)(2,1)S(1)} %get-tuple-element.49), channel_id=1, source_target_pairs={{0,8},{8,0},{16,24},{24,16},{1,9},{9,1},{17,25},{25,17},{2,10},{10... | collective-permute-start | bytes 1572872 | tf_op jit(solution)/shard_map/ppermute | solution.py:28
  66.2 22.5 %collective-permute-start.11 = (bf16[4,128,128]{2,1,0:T(8,128)(2,1)S(1)}, bf16[4,128,128]{2,1,0:T(8,128)(2,1)S(1)}, u32[]{:S(2)}, u32[]{:S(2)}) collective-permute-start(bf16[4,128,128]{2,1,0:T(8,128)(2,1)S(1)} %get-tuple-element.67), channel_id=1, source_target_pairs={{0,8},{8,0},{16,24},{24,16},{1,9},{9,1},{17,25},{25,17},{2,10},{10... | collective-permute-start | bytes 393224 | tf_op jit(solution)/shard_map/ppermute | solution.py:28
  67.8 20.9 %collective-permute-start.12 = (bf16[4,128,128]{2,1,0:T(8,128)(2,1)S(1)}, bf16[4,128,128]{2,1,0:T(8,128)(2,1)S(1)}, u32[]{:S(2)}, u32[]{:S(2)}) collective-permute-start(bf16[4,128,128]{2,1,0:T(8,128)(2,1)S(1)} %get-tuple-element.69), channel_id=1, source_target_pairs={{0,16},{8,24},{16,0},{24,8},{1,17},{9,25},{17,1},{25,9},{2,18},{10... | collective-permute-start | bytes 393224 | tf_op jit(solution)/shard_map/ppermute | solution.py:28
  69.3 19.4 %collective-permute-start.13 = (bf16[4,128,128]{2,1,0:T(8,128)(2,1)S(1)}, bf16[4,128,128]{2,1,0:T(8,128)(2,1)S(1)}, u32[]{:S(2)}, u32[]{:S(2)}) collective-permute-start(bf16[4,128,128]{2,1,0:T(8,128)(2,1)S(1)} %get-tuple-element.68), channel_id=1, source_target_pairs={{0,24},{8,16},{16,8},{24,0},{1,25},{9,17},{17,9},{25,1},{2,26},{10... | collective-permute-start | bytes 393224 | tf_op jit(solution)/shard_map/ppermute | solution.py:28
  74.3 7.1 %collective-permute-start.14 = (bf16[4,128,128]{2,1,0:T(8,128)(2,1)S(1)}, bf16[4,128,128]{2,1,0:T(8,128)(2,1)S(1)}, u32[]{:S(2)}, u32[]{:S(2)}) collective-permute-start(bf16[4,128,128]{2,1,0:T(8,128)(2,1)S(1)} %get-tuple-element.63), channel_id=1, source_target_pairs={{0,2},{1,3},{2,4},{3,5},{4,6},{5,7},{6,0},{7,1},{8,10},{9,11},{10,... | collective-permute-start | bytes 393224 | tf_op jit(solution)/shard_map/ppermute | solution.py:28
  77.1 13.2 %copy-start.7 = (f32[4,128,128]{2,1,0:T(8,128)S(1)}, f32[4,128,128]{2,1,0:T(8,128)}, u32[]{:S(2)}) copy-start(f32[4,128,128]{2,1,0:T(8,128)} %get-tuple-element.37.refs_4_) | copy-start | bytes 786436
  77.1 9.6 %collective-permute-start.16 = (bf16[4,128,128]{2,1,0:T(8,128)(2,1)S(1)}, bf16[4,128,128]{2,1,0:T(8,128)(2,1)S(1)}, u32[]{:S(2)}, u32[]{:S(2)}) collective-permute-start(bf16[4,128,128]{2,1,0:T(8,128)(2,1)S(1)} %get-tuple-element.65), channel_id=1, source_target_pairs={{0,6},{1,7},{2,0},{3,1},{4,2},{5,3},{6,4},{7,5},{8,14},{9,15},{10,... | collective-permute-start | bytes 393224 | tf_op jit(solution)/shard_map/ppermute | solution.py:28
  82.3 9.3 %collective-permute-start.15 = (bf16[8,128,128]{2,1,0:T(8,128)(2,1)S(1)}, bf16[8,128,128]{2,1,0:T(8,128)(2,1)S(1)}, u32[]{:S(2)}, u32[]{:S(2)}) collective-permute-start(bf16[8,128,128]{2,1,0:T(8,128)(2,1)S(1)} %pad_maximum_fusion.4), channel_id=1, source_target_pairs={{0,2},{1,3},{2,4},{3,5},{4,6},{5,7},{6,0},{7,1},{8,10},{9,11},{10,... | collective-permute-start | bytes 786440 | tf_op jit(solution)/shard_map/ppermute | solution.py:28
  87.7 6.4 %collective-permute-start.17 = (bf16[8,128,128]{2,1,0:T(8,128)(2,1)S(1)}, bf16[8,128,128]{2,1,0:T(8,128)(2,1)S(1)}, u32[]{:S(2)}, u32[]{:S(2)}) collective-permute-start(bf16[8,128,128]{2,1,0:T(8,128)(2,1)S(1)} %pad_maximum_fusion.5), channel_id=1, source_target_pairs={{0,6},{1,7},{2,0},{3,1},{4,2},{5,3},{6,4},{7,5},{8,14},{9,15},{10,... | collective-permute-start | bytes 786440 | tf_op jit(solution)/shard_map/ppermute | solution.py:28
  94.3 11.7 %copy-start.3 = (bf16[12,128,128]{2,1,0:T(8,128)(2,1)}, bf16[12,128,128]{2,1,0:T(8,128)(2,1)S(1)}, u32[]{:S(2)}) copy-start(bf16[12,128,128]{2,1,0:T(8,128)(2,1)S(1)} %pad_maximum_fusion.3) | copy-start | bytes 1179652
  94.3 5.5 %collective-permute-start.18 = (bf16[2,1,128,128]{3,2,1,0:T(8,128)(2,1)S(1)}, bf16[2,1,128,128]{3,2,1,0:T(8,128)(2,1)S(1)}, u32[]{:S(2)}, u32[]{:S(2)}) collective-permute-start(bf16[2,1,128,128]{3,2,1,0:T(8,128)(2,1)S(1)} %get-tuple-element.73), channel_id=1, source_target_pairs={{0,1},{1,2},{2,3},{3,4},{4,5},{5,6},{6,7},{7,0},{8,9},{9,10},{10,1... | collective-permute-start | bytes 196616 | tf_op jit(solution)/shard_map/ppermute | solution.py:28
  94.4 5.5 %collective-permute-start.19 = (bf16[2,1,128,128]{3,2,1,0:T(8,128)(2,1)S(1)}, bf16[2,1,128,128]{3,2,1,0:T(8,128)(2,1)S(1)}, u32[]{:S(2)}, u32[]{:S(2)}) collective-permute-start(bf16[2,1,128,128]{3,2,1,0:T(8,128)(2,1)S(1)} %get-tuple-element.72), channel_id=1, source_target_pairs={{0,7},{1,0},{2,1},{3,2},{4,3},{5,4},{6,5},{7,6},{8,15},{9,8},{10,9... | collective-permute-start | bytes 196616 | tf_op jit(solution)/shard_map/ppermute | solution.py:28
  99.9 22.7 %collective-permute-start.21 = (bf16[8,128,128]{2,1,0:T(8,128)(2,1)S(1)}, bf16[8,128,128]{2,1,0:T(8,128)(2,1)S(1)}, u32[]{:S(2)}, u32[]{:S(2)}) collective-permute-start(bf16[8,128,128]{2,1,0:T(8,128)(2,1)S(1)} %pad_maximum_fusion.7), channel_id=1, source_target_pairs={{8,0},{16,8},{24,16},{9,1},{17,9},{25,17},{10,2},{18,10},{26,18},{... | collective-permute-start | bytes 786440 | tf_op jit(solution)/shard_map/ppermute | solution.py:182
  103.4 19.2 %collective-permute-start.20 = (bf16[8,128,128]{2,1,0:T(8,128)(2,1)S(1)}, bf16[8,128,128]{2,1,0:T(8,128)(2,1)S(1)}, u32[]{:S(2)}, u32[]{:S(2)}) collective-permute-start(bf16[8,128,128]{2,1,0:T(8,128)(2,1)S(1)} %pad_maximum_fusion.6), channel_id=1, source_target_pairs={{0,8},{8,16},{16,24},{1,9},{9,17},{17,25},{2,10},{10,18},{18,26},{... | collective-permute-start | bytes 786440 | tf_op jit(solution)/shard_map/ppermute | solution.py:182
  122.6 0.7 copy-start.8
  122.6 0.8 copy-start.9
